TPU v7x, 32 devices: a whole 2x2x4 slice. The times are simulated.
32 devices in a mesh: groups: 2 (over y), side: 4 (over x, core), tensor: 4 (over z).
Axes of the slice: x: 2, y: 2, z: 4, core: 2. Of those that a mesh axis runs over, the one named last changes fastest.
Arguments:
- query: bfloat16 [128, 6144], P(('groups', 'side'), 'tensor'), parts along dimension 0, may hold values from -160 to 160
- new_key: bfloat16 [128, 1024], P(('groups', 'side'), 'tensor'), parts along dimension 0, may hold values from -6 to 6
- new_value: bfloat16 [128, 1024], P(('groups', 'side'), 'tensor'), parts along dimension 0, may hold values from -6 to 6
- key_cache: bfloat16 [128, 256, 1024], P(('groups', 'side'), None, 'tensor'), parts along dimension 0, may hold values from -6.5 to 6.5
- value_cache: bfloat16 [128, 256, 1024], P(('groups', 'side'), None, 'tensor'), parts along dimension 0, may hold values from -6 to 6
- cache_len: int32 [128], P(('groups', 'side')), parts along dimension 0, may hold values from 2 to 256, as said below
- resid: bfloat16 [128, 6144], P(('groups', 'side')), parts along dimension 0, may hold values from -4 to 4
- w_out: bfloat16 [6144, 6144], P('tensor', 'side'), may hold values from -0.625 to 0.625
- rms_gain: bfloat16 [6144], replicated, may hold values from 0.099609375 to 1.8984375
- w_router: float32 [6144, 8], replicated, may hold values from -0.15625 to 0.15625
- route_ids: int32 [128, 2], P(('groups', 'side')), parts along dimension 0, may hold values from 0 to 7, all different within a row; in each aligned block of 16 rows (0 to 15, 16 to 31, ...) at most 12 rows name the same one
- w_gate: bfloat16 [8, 6144, 8192], P('side', None, 'tensor'), may hold values from -0.078125 to 0.078125
- w_up: bfloat16 [8, 6144, 8192], P('side', None, 'tensor'), may hold values from -0.078125 to 0.078125
- w_down: bfloat16 [8, 8192, 6144], P('side', 'tensor'), may hold values from -0.0625 to 0.0625
Outputs:
- layer_out: bfloat16 [128, 6144], P(('groups', 'side'), 'tensor'), parts along dimension 0
There are 2 independent parts, one for each index of `groups`. A program takes and returns all parts, laid end to end along the dimension named above; an argument that names none is the same for every part. Nothing has to cross between parts.
Inputs may be any that keep to these rules, and one draw needn't show every extreme that they name: `cache_len`: at least one game of each pool has exactly 256 valid positions. `route_ids`: within the games of one index of side (aligned blocks of 16 games), no expert is chosen by more than 12 games, a bound that some block reaches.
All inputs are finite; a program needn't handle non-finite values.
Results may differ from a plain program's by a relative error of at most 0.0095.
Values may be sent and summed in bfloat16 or wider, within the bound.
No kernel may reach another device: no remote copies, remote signals or barrier semaphores. Data moves between devices by JAX's collectives and lax.ppermute only.
A program may use at most 320 MiB of HBM per device.

v0:
```python
import jax
import jax.numpy as jnp
from jax import lax
from jax.sharding import PartitionSpec as P

HEAD_DIM = 128
CAP = 12


def attend_local(query, new_key, new_value, key_cache, value_cache, cache_len):
    count = query.shape[0]
    positions = key_cache.shape[1]
    kv_local = key_cache.shape[2] // HEAD_DIM
    repeat = query.shape[1] // (kv_local * HEAD_DIM)
    queries = query.reshape(count, kv_local, repeat, HEAD_DIM)
    cached_keys = key_cache.reshape(count, positions, kv_local, HEAD_DIM)
    cached_values = value_cache.reshape(count, positions, kv_local, HEAD_DIM)
    scale = 1.0 / HEAD_DIM**0.5
    scores = (
        jnp.einsum("gkrd,gpkd->gkrp", queries, cached_keys, preferred_element_type=jnp.float32)
        * scale
    )
    own_key = new_key.reshape(count, kv_local, HEAD_DIM)
    own_score = (
        jnp.einsum("gkrd,gkd->gkr", queries, own_key, preferred_element_type=jnp.float32) * scale
    )
    valid = jnp.arange(positions, dtype=jnp.int32)[None, :] < cache_len[:, None]
    scores = jnp.where(valid[:, None, None, :], scores, -jnp.inf)
    highest = jnp.maximum(jnp.max(scores, axis=-1), own_score)
    cached_weight = jnp.exp(scores - highest[..., None])
    own_weight = jnp.exp(own_score - highest)
    total = jnp.sum(cached_weight, axis=-1) + own_weight
    cached_weight = (cached_weight / total[..., None]).astype(jnp.bfloat16)
    own_weight = (own_weight / total).astype(jnp.bfloat16)
    mixed = jnp.einsum(
        "gkrp,gpkd->gkrd", cached_weight, cached_values, preferred_element_type=jnp.float32
    )
    own_value = new_value.reshape(count, kv_local, 1, HEAD_DIM).astype(jnp.float32)
    mixed = mixed + own_weight.astype(jnp.float32)[..., None] * own_value
    return mixed.reshape(count, kv_local * repeat * HEAD_DIM).astype(jnp.bfloat16)


def shards(
    query,
    new_key,
    new_value,
    key_cache,
    value_cache,
    cache_len,
    resid,
    w_out,
    rms_gain,
    w_router,
    route_ids,
    w_gate,
    w_up,
    w_down,
):
    attended = attend_local(query, new_key, new_value, key_cache, value_cache, cache_len)
    column_part = jnp.dot(
        lax.all_gather(attended, "side", axis=0, tiled=True),
        w_out,
        preferred_element_type=jnp.float32,
    )
    partial_out = lax.all_to_all(column_part, "side", split_axis=0, concat_axis=1, tiled=True)
    attn_out = lax.psum(partial_out, "tensor")
    stream = (resid.astype(jnp.float32) + attn_out).astype(jnp.bfloat16)
    wide = stream.astype(jnp.float32)
    power = jnp.mean(wide * wide, axis=-1, keepdims=True)
    normed = wide * lax.rsqrt(power + 1e-05) * rms_gain.astype(jnp.float32)
    logits = jnp.dot(normed, w_router, precision=lax.Precision.HIGHEST)
    experts = w_router.shape[1]
    picked = route_ids[:, :, None] == jnp.arange(experts, dtype=jnp.int32)[None, None, :]
    chosen = jnp.sum(jnp.where(picked, logits[:, None, :], 0.0), axis=-1)
    first = 1.0 / (1.0 + jnp.exp(chosen[:, 1] - chosen[:, 0]))
    second = 1.0 / (1.0 + jnp.exp(chosen[:, 0] - chosen[:, 1]))
    pair = jnp.stack([first, second], axis=1)
    weight = jnp.sum(jnp.where(picked, pair[:, :, None], 0.0), axis=1)
    rows = normed.astype(jnp.bfloat16)
    member = jnp.any(picked, axis=1).astype(jnp.int32)
    order_rank = jnp.cumsum(member, axis=0) - member
    capacity = CAP
    placing = (order_rank.T[:, None, :] == jnp.arange(capacity, dtype=jnp.int32)[None, :, None]) & (
        member.T[:, None, :] == 1
    )
    packed = jnp.einsum(
        "ecg,gd->ecd", placing.astype(jnp.bfloat16), rows, preferred_element_type=jnp.float32
    ).astype(jnp.bfloat16)
    side_count = lax.axis_size("side")
    slot_total = max(side_count, experts)
    split_count = slot_total // experts
    slot_local = slot_total // side_count
    width = rows.shape[1]
    packed = jnp.repeat(packed, split_count, axis=0).reshape(
        side_count, slot_local, capacity, width
    )
    arrived = lax.all_to_all(packed, "side", split_axis=0, concat_axis=0, tiled=True)
    gate = jnp.einsum("sjcd,jdf->sjcf", arrived, w_gate, preferred_element_type=jnp.float32)
    upward = jnp.einsum("sjcd,jdf->sjcf", arrived, w_up, preferred_element_type=jnp.float32)
    inner = (jax.nn.silu(gate) * upward).astype(jnp.bfloat16)
    expert_part = jnp.einsum("sjcf,jfd->sjcd", inner, w_down, preferred_element_type=jnp.float32)
    scaled_place = placing.astype(jnp.float32) * weight.T[:, None, :]
    returned = lax.all_to_all(expert_part, "side", split_axis=0, concat_axis=0, tiled=True)
    features = returned.shape[3]
    merged = jnp.sum(returned.reshape(experts, split_count, capacity, features), axis=1)
    moe = lax.psum_scatter(
        jnp.einsum("ecg,ecf->gf", scaled_place, merged, precision=lax.Precision.HIGHEST),
        "tensor",
        scatter_dimension=1,
        tiled=True,
    )
    columns = moe.shape[1]
    local_stream = lax.dynamic_slice_in_dim(wide, lax.axis_index("tensor") * columns, columns, 1)
    return (local_stream + moe).astype(jnp.bfloat16)


def solution(mesh):
    return jax.shard_map(
        shards,
        mesh=mesh,
        in_specs=(
            P(("groups", "side"), "tensor"),
            P(("groups", "side"), "tensor"),
            P(("groups", "side"), "tensor"),
            P(("groups", "side"), None, "tensor"),
            P(("groups", "side"), None, "tensor"),
            P(("groups", "side")),
            P(("groups", "side"), None),
            P("tensor", "side"),
            P(),
            P(),
            P(("groups", "side"), None),
            P("side", None, "tensor"),
            P("side", None, "tensor"),
            P("side", "tensor", None),
        ),
        out_specs=P(("groups", "side"), "tensor"),
        check_vma=False,
    )
```

profile of v0, /device:TPU:0, one launch (start us, length us, event | category | flops | bytes accessed | tf_op | source)
XLA Modules:
  0.0 228.8 jit_solution(17317136523201365541)
XLA Ops:
  6.5 0.0 copy-start
  6.5 0.9 iota_compare_fusion.1
  7.4 0.7 reshape.79
  8.1 0.7 reshape.70
  8.8 0.9 reshape.66
  9.7 0.0 copy-start.6
  9.7 0.1 fusion.69
  9.9 0.0 copy-done
  9.9 0.7 fusion.68
  10.6 0.2 fusion.44
  10.9 0.4 copy-done.6
  11.3 0.4 fusion.38
  11.7 0.1 convert_element_type.65
  11.8 6.8 %all_gather.3 = bf16[64,1536]{1,0:T(8,128)(2,1)S(1)} all-gather(bf16[16,1536]{1,0:T(8,128)(2,1)S(1)} %convert_element_type.65), channel_id=1, replica_groups=mesh['groups'=2,'side'=4,'tensor'=4] {'side'}, dimensions={0}, use_global_device_ids=true | all-gather | bytes 245760 | tf_op jit(solution)/shard_map/all_gather | solution.py:61
  18.7 4.0 %fusion.70 = f32[64,1536]{1,0:T(8,128)} fusion(bf16[64,1536]{1,0:T(8,128)(2,1)S(1)} %all_gather.3, bf16[1536,1536]{1,0:T(8,128)(2,1)} %param.21), kind=kOutput, calls=%fused_computation.71 | convolution fusion | flops 301989888 | bytes 5308416 | tf_op jit(solution)/shard_map/dot_general | solution.py:60
  22.7 3.6 %all-to-all-start = ((f32[4,16,1536]{2,1,0:T(8,128)}), f32[4,16,1536]{2,1,0:T(8,128)S(1)}, u32[]{:S(2)}, u32[]{:S(2)}) async-start(f32[4,16,1536]{2,1,0:T(8,128)} %bitcast.2), calls=%async_computation | async-start | bytes 786432 | tf_op jit(solution)/shard_map/all_to_all | solution.py:65
  26.3 0.0 all-reduce.2.cloned.1.call-start
  26.4 0.0 copy-done.5
  26.4 0.1 copy.53
  26.5 7.2 %all-to-all-done = f32[4,16,1536]{2,1,0:T(8,128)S(1)} async-done(((f32[4,16,1536]{2,1,0:T(8,128)}), f32[4,16,1536]{2,1,0:T(8,128)S(1)}, u32[]{:S(2)}, u32[]{:S(2)}) %all-to-all-start) | async-done | bytes 393248 | tf_op jit(solution)/shard_map/all_to_all | solution.py:65
  33.7 0.8 copy.73
  34.5 0.0 all-reduce.2.cloned.1.call-update
  34.5 0.1 copy.55
  34.7 0.1 copy.54
  34.7 0.0 copy-done.4
  34.7 37.5 %all-reduce.2.cloned.1.call-done = f32[16,6144]{1,0:T(8,128)} async-done(((f32[16,6144]{1,0:T(8,128)}), f32[16,6144]{1,0:T(8,128)}) %all-reduce.2.cloned.1.call-update) | async-done | bytes 393232 | tf_op jit(solution)/shard_map/psum | solution.py:66
  72.3 0.0 copy-done.2
  72.3 1.0 fusion.67
  73.3 0.2 multiply_reduce_fusion
  73.5 0.7 convolution_convert_fusion
  74.2 1.2 copy.57
  75.4 18.3 %all_to_all.29 = bf16[4,2,12,6144]{3,1,2,0:T(2,128)(2,1)S(1)} all-to-all(bf16[4,2,12,6144]{3,1,2,0:T(2,128)(2,1)S(1)} %copy.57), channel_id=1, replica_groups=mesh['groups'=2,'side'=4,'tensor'=4] {'side'}, dimensions={0} | all-to-all | bytes 2359296 | tf_op jit(solution)/shard_map/all_to_all | solution.py:97
  93.7 19.8 %fusion.9 = f32[4,2,12,2048]{3,2,0,1:T(8,128)S(1)} fusion(bf16[2,6144,2048]{2,1,0:T(8,128)(2,1)} %param.25, bf16[4,2,12,6144]{3,1,2,0:T(2,128)(2,1)S(1)} %all_to_all.29), kind=kOutput, calls=%fused_computation.9 | convolution fusion | flops 2415919104 | bytes 52297728 | tf_op jit(solution)/shard_map/sjcd,jdf->sjcf/dot_general | solution.py:98
  113.5 20.2 %fusion.18 = bf16[4,2,12,2048]{3,2,0,1:T(8,128)(2,1)S(1)} fusion(bf16[2,6144,2048]{2,1,0:T(8,128)(2,1)} %param.26, bf16[4,2,12,6144]{3,1,2,0:T(2,128)(2,1)S(1)} %all_to_all.29, f32[4,2,12,2048]{3,2,0,1:T(8,128)S(1)} %fusion.9), kind=kOutput, calls=%fused_computation.12 | convolution fusion | flops 2417098752 | bytes 52690944 | tf_op jit(solution)/shard_map/sjcd,jdf->sjcf/dot_general | solution.py:99
  133.7 21.5 %fusion.6 = f32[4,2,12,6144]{3,2,0,1:T(8,128)} fusion(bf16[4,2,12,2048]{3,2,0,1:T(8,128)(2,1)S(1)} %fusion.18, bf16[2,2048,6144]{2,1,0:T(8,128)(2,1)} %param.27), kind=kOutput, calls=%fused_computation.6 | convolution fusion | flops 2415919104 | bytes 53084160 | tf_op jit(solution)/shard_map/sjcf,jfd->sjcd/dot_general | solution.py:101
  155.2 5.2 %copy.60 = f32[4,2,12,6144]{3,1,2,0:T(2,128)} copy(f32[4,2,12,6144]{3,2,0,1:T(8,128)} %fusion.6) | data formatting | bytes 4718592 | tf_op jit(solution)/shard_map/sjcf,jfd->sjcd/transpose | solution.py:101
  160.3 4.6 %all-to-all-start.2 = ((f32[4,2,12,6144]{3,1,2,0:T(2,128)}), f32[4,2,12,6144]{3,1,2,0:T(2,128)}, u32[]{:S(2)}, u32[]{:S(2)}) async-start(f32[4,2,12,6144]{3,1,2,0:T(2,128)} %copy.60), calls=%async_computation.2 | async-start | bytes 4718592 | tf_op jit(solution)/shard_map/all_to_all | solution.py:103
  164.9 0.0 reduce-scatter.2.cloned.1.call-start
  165.0 0.0 copy-done.3
  165.0 0.6 fusion.42
  165.7 27.8 %all-to-all-done.2 = f32[4,2,12,6144]{3,1,2,0:T(2,128)} async-done(((f32[4,2,12,6144]{3,1,2,0:T(2,128)}), f32[4,2,12,6144]{3,1,2,0:T(2,128)}, u32[]{:S(2)}, u32[]{:S(2)}) %all-to-all-start.2) | async-done | bytes 2359328 | tf_op jit(solution)/shard_map/all_to_all | solution.py:103
  193.5 3.0 %copy.69 = f32[4,2,12,6144]{3,2,1,0:T(8,128)S(1)} copy(f32[4,2,12,6144]{3,1,2,0:T(2,128)} %all-to-all-done.2) | data formatting | bytes 4718592 | tf_op jit(solution)/shard_map/reduce_sum | solution.py:105
  196.6 0.0 copy-start.1
  196.6 4.2 %convolution_bitcast_fusion = f32[16,6144]{1,0:T(8,128)} fusion(f32[8,12,6144]{2,1,0:T(8,128)S(1)} %bitcast.85, f32[8,16]{1,0:T(8,128)S(1)} %bitcast.91, s32[8,16]{1,0:T(8,128)S(1)} %copy.54, pred[8,16]{1,0:T(8,128)(4,1)S(1)} %copy.55), kind=kOutput, calls=%fused_computation.8 | convolution fusion | flops 113250816 | bytes 2753664 | tf_op jit(solution)/shard_map/ecg,ecf->gf/dot_general | solution.py:107
  200.8 0.0 reduce-scatter.2.cloned.1.call-update
  200.8 19.6 %reduce-scatter.2.cloned.1.call-done = f32[16,1536]{1,0:T(8,128)} async-done(((f32[16,6144]{1,0:T(8,128)}), f32[16,1536]{1,0:T(8,128)}) %reduce-scatter.2.cloned.1.call-update) | async-done | bytes 98320 | tf_op jit(solution)/shard_map/reduce_scatter | solution.py:106
  220.4 1.5 add_convert_fusion.1
  221.9 0.0 copy-done.1
  (16 shorter events, 0.2 us)
Async XLA Ops:
  6.5 3.3 %copy-start = (bf16[16,256,256]{2,1,0:T(8,128)(2,1)S(1)}, bf16[16,256,256]{2,1,0:T(8,128)(2,1)}, u32[]{:S(2)}) copy-start(bf16[16,256,256]{2,1,0:T(8,128)(2,1)} %param.17) | copy-start | bytes 6291460
  9.7 1.6 copy-start.6
  18.7 7.7 %copy-start.5 = (s32[16,2]{0,1:T(2,128)S(1)}, s32[16,2]{0,1:T(2,128)}, u32[]{:S(2)}) copy-start(s32[16,2]{0,1:T(2,128)} %param.24) | copy-start | bytes 388
  18.7 16.0 %copy-start.4 = (bf16[6144]{0:T(1024)(128)(2,1)S(1)}, bf16[6144]{0:T(1024)(128)(2,1)}, u32[]{:S(2)}) copy-start(bf16[6144]{0:T(1024)(128)(2,1)} %param.22) | copy-start | bytes 36868
  22.7 49.6 %copy-start.2 = (bf16[16,6144]{1,0:T(8,128)(2,1)S(1)}, bf16[16,6144]{1,0:T(8,128)(2,1)}, u32[]{:S(2)}) copy-start(bf16[16,6144]{1,0:T(8,128)(2,1)} %param.20) | copy-start | bytes 589828
  22.7 11.0 %all-to-all-start = ((f32[4,16,1536]{2,1,0:T(8,128)}), f32[4,16,1536]{2,1,0:T(8,128)S(1)}, u32[]{:S(2)}, u32[]{:S(2)}) async-start(f32[4,16,1536]{2,1,0:T(8,128)} %bitcast.2), calls=%async_computation | async-start | bytes 786432 | tf_op jit(solution)/shard_map/all_to_all | solution.py:65
  26.3 46.0 %all-reduce.2.cloned.1.call-start = ((), (), s32[]{:S(2)}) async-start(), calls=%async_computation.4 | async-start | bytes 786432 | tf_op jit(solution)/shard_map/psum | solution.py:66
  160.3 4.7 %copy-start.3 = (f32[6144,8]{0,1:T(8,128)S(1)}, f32[6144,8]{0,1:T(8,128)}, u32[]{:S(2)}) copy-start(f32[6144,8]{0,1:T(8,128)} %param.23) | copy-start | bytes 589828
  160.3 33.2 %all-to-all-start.2 = ((f32[4,2,12,6144]{3,1,2,0:T(2,128)}), f32[4,2,12,6144]{3,1,2,0:T(2,128)}, u32[]{:S(2)}, u32[]{:S(2)}) async-start(f32[4,2,12,6144]{3,1,2,0:T(2,128)} %copy.60), calls=%async_computation.2 | async-start | bytes 4718592 | tf_op jit(solution)/shard_map/all_to_all | solution.py:103
  164.9 55.5 %reduce-scatter.2.cloned.1.call-start = ((), (), s32[]{:S(2)}) async-start(), calls=%async_computation.5 | async-start | bytes 491520 | tf_op jit(solution)/shard_map/reduce_scatter | solution.py:106
  196.6 25.4 %copy-start.1 = (bf16[16,256,256]{2,1,0:T(8,128)(2,1)S(1)}, bf16[16,256,256]{2,1,0:T(8,128)(2,1)}, u32[]{:S(2)}) copy-start(bf16[16,256,256]{2,1,0:T(8,128)(2,1)} %param.17) | copy-start | bytes 6291460
Sparse Core Ops, SparseCore 0:
  34.6 37.5 all-reduce.1
  201.0 19.3 reduce-scatter.1
where the time goes:
time: 229 us
  waiting for transfers between devices  92.2 us (40%)
  matrix products  72.4 us (32%)
  blocking collectives  25.1 us (11%)
  between operations  13.6 us (6%)
  local copies, waits for them, and re-layouts  13.2 us (6%)
  starting transfers between devices  8.29 us (4%)
  other arithmetic  4.01 us (2%)
    psum x1, waiting for transfers between devices, shards(): attn_out = lax.psum(partial_out, 'tensor')  37.5 us
    all_to_all x1, waiting for transfers between devices, shards(): lax.all_to_all(expert_part, 'side', split_axis=0, concat_axis=0, tiled=True)  27.8 us
    dot_general x1, matrix products, shards(): jnp.einsum('sjcf,jfd->sjcd', inner, w_down, preferred_element_type=jnp.fl...  21.5 us
    dot_general x1, matrix products, shards(): jnp.einsum('sjcd,jdf->sjcf', arrived, w_up, preferred_element_type=jnp.fl...  20.2 us
    dot_general x1, matrix products, shards(): jnp.einsum('sjcd,jdf->sjcf', arrived, w_gate, preferred_element_type=jnp....  19.8 us
    reduce_scatter x1, waiting for transfers between devices, shards(): lax.psum_scatter(jnp.einsum('ecg,ecf->gf', scaled_place, merged, precisio...  19.6 us
    all_to_all x1, blocking collectives, shards(): lax.all_to_all(packed, 'side', split_axis=0, concat_axis=0, tiled=True)  18.3 us
    all_to_all x1, waiting for transfers between devices, shards(): lax.all_to_all(column_part, 'side', split_axis=0, concat_axis=1, tiled=True)  7.25 us
  transfers between devices with their start and end apart: 4, of which 4 were waited for; matrix products, arithmetic and copies ran while one was open for 0% of the time, Pallas kernels for 0%

commit v1 on v0

--- a/solution.py
+++ b/solution.py
@@ -1,10 +1,587 @@
+import functools
+
 import jax
 import jax.numpy as jnp
 from jax import lax
+from jax.experimental import pallas as pl
+from jax.experimental.pallas import tpu as pltpu
 from jax.sharding import PartitionSpec as P
 
 HEAD_DIM = 128
 CAP = 12
+LANES = 128
+FBLOCK = 256
+BF16 = jnp.bfloat16
+F32 = jnp.float32
+MIB = 2**20
+VMEM = pl.BlockSpec(memory_space=pltpu.VMEM)
+SMEM = pl.BlockSpec(memory_space=pltpu.SMEM)
+ANY = pl.BlockSpec(memory_space=pl.ANY)
+
+
+def cost(flops, moved):
+    return pl.CostEstimate(flops=int(flops), bytes_accessed=int(moved), transcendentals=0)
+
+
+def place_of(position, count):
+    bits = count.bit_length() - 1
+    return sum(((position >> b) & 1) << (bits - 1 - b) for b in range(bits))
+
+
+def swap(value, axis, count, mask):
+    return lax.ppermute(value, axis, [(i, i ^ mask) for i in range(count)])
+
+
+def columns(start, size):
+    return pl.ds(pl.multiple_of(start, LANES), size)
+
+
+def attend_body(
+    sides, steps, length, query, new_key, new_value, keys, values, resid, route, *rest
+):
+    outs, (spread, mixed, key32, value32) = rest[:sides], rest[sides:]
+    games, width = query.shape
+    heads = width // HEAD_DIM
+    wide = new_key.shape[1]
+    repeat = heads * HEAD_DIM // wide
+    block = keys.shape[0]
+    positions = keys.shape[1]
+    scale = 1.0 / HEAD_DIM**0.5
+    step = pl.program_id(0)
+
+    @pl.when(step == 0)
+    def _():
+        spread[...] = jnp.zeros_like(spread)
+        for h in range(heads):
+            lane = h // repeat * HEAD_DIM
+            spread[:, h, lane : lane + HEAD_DIM] = query[
+                :, h * HEAD_DIM : (h + 1) * HEAD_DIM
+            ].astype(F32)
+        key32[...] = new_key[...].astype(F32)
+        value32[...] = new_value[...].astype(F32)
+
+    for i in range(block):
+        game = step * block + i
+        q = spread[game]
+        score = (
+            lax.dot_general(
+                q.astype(BF16), keys[i], (((1,), (1,)), ((), ())), preferred_element_type=F32
+            )
+            * scale
+        )
+        own = jnp.sum(q * key32[pl.ds(game, 1), :], axis=-1, keepdims=True) * scale
+        at = lax.broadcasted_iota(jnp.int32, score.shape, 1)
+        score = jnp.where(at < length[game], score, -jnp.inf)
+        top = jnp.maximum(jnp.max(score, axis=-1, keepdims=True), own)
+        e = jnp.exp(score - top)
+        own_e = jnp.exp(own - top)
+        total = jnp.sum(e, axis=-1, keepdims=True) + own_e
+        prob = (e / total).astype(BF16)
+        own_prob = (own_e / total).astype(BF16).astype(F32)
+        mixed[game] = (
+            jnp.dot(prob, values[i], preferred_element_type=F32)
+            + own_prob * value32[pl.ds(game, 1), :]
+        )
+
+    @pl.when(step == steps - 1)
+    def _():
+        side, tensor = lax.axis_index("side"), lax.axis_index("tensor")
+        for h in range(heads):
+            lane = h // repeat * HEAD_DIM
+            part = mixed[:, h, lane : lane + HEAD_DIM].astype(BF16)
+            for out in outs:
+                out[:, h * HEAD_DIM : (h + 1) * HEAD_DIM] = part
+        extra = outs[0].shape[1] - width - LANES
+        row = lax.broadcasted_iota(jnp.int32, (games, games), 0)
+        diagonal = row == lax.broadcasted_iota(jnp.int32, (games, games), 1)
+        lane = lax.broadcasted_iota(jnp.int32, (games, LANES), 1)
+        routes = jnp.zeros((games, LANES), F32)
+        for j in range(route.shape[0]):
+            ids = jnp.broadcast_to(route[j : j + 1, :].astype(F32), (games, games))
+            column = jnp.sum(jnp.where(diagonal, ids, 0.0), axis=-1, keepdims=True)
+            routes = jnp.where(lane == j, column, routes)
+        features = resid.shape[1] // sides
+        for k, out in enumerate(outs):
+            start = jnp.bitwise_xor(side, k) * features + tensor * extra
+            out[:, width : width + extra] = resid[:, columns(start, extra)]
+            out[:, width + extra :] = routes.astype(BF16)
+
+
+def attend(sides, extra, query, new_key, new_value, key_cache, value_cache, cache_len, resid, route_ids):
+    games, width = query.shape
+    positions, wide = key_cache.shape[1:]
+    block = 4
+    steps = games // block
+    heads = -(-(width // HEAD_DIM) // 16) * 16
+    whole = lambda i: (0, 0)
+    out = jax.ShapeDtypeStruct((games, width + extra + LANES), BF16)
+    return pl.pallas_call(
+        functools.partial(attend_body, sides, steps),
+        grid=(steps,),
+        in_specs=[
+            SMEM,
+            pl.BlockSpec(query.shape, whole),
+            pl.BlockSpec(new_key.shape, whole),
+            pl.BlockSpec(new_value.shape, whole),
+            pl.BlockSpec((block, positions, wide), lambda i: (i, 0, 0)),
+            pl.BlockSpec((block, positions, wide), lambda i: (i, 0, 0)),
+            pl.BlockSpec(resid.shape, whole),
+            pl.BlockSpec(route_ids.shape[::-1], whole),
+        ],
+        out_specs=[pl.BlockSpec(out.shape, whole)] * sides,
+        out_shape=[out] * sides,
+        scratch_shapes=[
+            pltpu.VMEM((games, heads, wide), F32),
+            pltpu.VMEM((games, heads, wide), F32),
+            pltpu.VMEM((games, wide), F32),
+            pltpu.VMEM((games, wide), F32),
+        ],
+        compiler_params=pltpu.CompilerParams(vmem_limit_bytes=10 * MIB),
+        cost_estimate=cost(4 * games * heads * positions * wide, 2 * key_cache.size * 2),
+        name="attend",
+    )(cache_len, query, new_key, new_value, key_cache, value_cache, resid, route_ids.T)
+
+
+def project_body(sides, tensors, *refs):
+    blocks, weight = refs[:sides], refs[sides]
+    outs, (rows, total) = refs[sides + 1 : sides + 1 + tensors], refs[sides + 1 + tensors :]
+    games = blocks[0].shape[0]
+    depth, width = weight.shape
+    for p in range(sides):
+        rows[p * games : (p + 1) * games, :] = blocks[place_of(p, sides)][:, :depth]
+    step = 512 if width % 512 == 0 else LANES
+    for c in range(0, width, step):
+        total[:, c : c + step] = jnp.dot(
+            rows[...], weight[:, c : c + step], preferred_element_type=F32
+        )
+    tensor = lax.axis_index("tensor")
+    part = width // tensors
+    for k, out in enumerate(outs):
+        start = jnp.bitwise_xor(tensor, k) * part
+        out[...] = total[:, columns(start, part)].astype(out.dtype)
+
+
+def project(sides, tensors, blocks, w_out):
+    rows = blocks[0].shape[0] * sides
+    depth, width = w_out.shape
+    part = width // tensors
+    shapes = [jax.ShapeDtypeStruct((rows, part), F32 if k == 0 else BF16) for k in range(tensors)]
+    return pl.pallas_call(
+        functools.partial(project_body, sides, tensors),
+        in_specs=[VMEM] * (sides + 1),
+        out_specs=[VMEM] * tensors,
+        out_shape=shapes,
+        scratch_shapes=[pltpu.VMEM((rows, depth), BF16), pltpu.VMEM((rows, width), F32)],
+        compiler_params=pltpu.CompilerParams(vmem_limit_bytes=10 * MIB),
+        cost_estimate=cost(2 * rows * depth * width, 2 * depth * width),
+        name="project",
+    )(*blocks, w_out)
+
+
+def stream_body(sides, tensors, depth, *refs):
+    parts, blocks, out = refs[:tensors], refs[tensors : tensors + sides], refs[-1]
+    games = blocks[0].shape[0]
+    width = out.shape[1]
+    total = parts[0][...]
+    for part in parts[1:]:
+        total = total + part[...].astype(F32)
+    for p in range(sides):
+        resid = blocks[place_of(p, sides)][:, depth : depth + width].astype(F32)
+        out[p * games : (p + 1) * games, :] = (
+            resid + total[p * games : (p + 1) * games, :]
+        ).astype(BF16)
+
+
+def stream_of(sides, tensors, depth, parts, blocks):
+    return pl.pallas_call(
+        functools.partial(stream_body, sides, tensors, depth),
+        in_specs=[VMEM] * (sides + tensors),
+        out_specs=VMEM,
+        out_shape=jax.ShapeDtypeStruct(parts[0].shape, BF16),
+        compiler_params=pltpu.CompilerParams(vmem_limit_bytes=4 * MIB),
+        name="stream",
+    )(*parts, *blocks)
+
+
+def gather_body(tensors, *refs):
+    out = refs[-1]
+    width = refs[0].shape[1]
+    tensor = lax.axis_index("tensor")
+    for k in range(tensors):
+        out[:, columns(jnp.bitwise_xor(tensor, k) * width, width)] = refs[k][...]
+
+
+def gather_columns(tensors, parts):
+    rows, width = parts[0].shape
+    return pl.pallas_call(
+        functools.partial(gather_body, tensors),
+        in_specs=[VMEM] * tensors,
+        out_specs=VMEM,
+        out_shape=jax.ShapeDtypeStruct((rows, width * tensors), BF16),
+        compiler_params=pltpu.CompilerParams(vmem_limit_bytes=4 * MIB),
+        name="columns",
+    )(*parts)
+
+
+def prefetch_body(first, count, per_slot, w_gate, w_up, after, out, sems):
+    del after
+    copies = []
+    for i in range(count):
+        slot, block = divmod(first + i, per_slot)
+        for j, weight in enumerate((w_gate, w_up)):
+            copies.append(
+                pltpu.make_async_copy(
+                    weight.at[slot, :, pl.ds(block * FBLOCK, FBLOCK)],
+                    out.at[i, j],
+                    sems.at[2 * i + j],
+                )
+            )
+    for c in copies:
+        c.start()
+    for c in copies:
+        c.wait()
+
+
+def prefetch(first, count, w_gate, w_up, after):
+    _, depth, hidden = w_gate.shape
+    return pl.pallas_call(
+        functools.partial(prefetch_body, first, count, hidden // FBLOCK),
+        in_specs=[ANY, ANY, ANY],
+        out_specs=VMEM,
+        out_shape=pltpu.VMEM((count, 2, depth, FBLOCK), BF16),
+        scratch_shapes=[pltpu.SemaphoreType.DMA((2 * count,))],
+        compiler_params=pltpu.CompilerParams(vmem_limit_bytes=MIB),
+        cost_estimate=cost(0, count * 2 * depth * FBLOCK * 2),
+        name="prefetch",
+    )(w_gate, w_up, after)
+
+
+def expand_body(sides, held, depth, split, ring, *refs):
+    chunks, refs = refs[:sides], refs[sides:]
+    blocks, refs = refs[:sides], refs[sides:]
+    gain, router, w_gate, w_up = refs[:4]
+    ready, refs = refs[4 : 4 + len(held)], refs[4 + len(held) :]
+    inner, mine, stream, rows, router2, scale, buffer, sems = refs
+    games = blocks[0].shape[0]
+    count = games * sides
+    width = chunks[0].shape[1]
+    features = width * sides
+    slots, _, hidden = w_gate.shape
+    per_slot = hidden // FBLOCK
+    total_steps = slots * per_slot
+    kept = sum(held)
+    streamed = total_steps - kept
+    side, tensor = lax.axis_index("side"), lax.axis_index("tensor")
+
+    def copies(step, half):
+        index = kept + step
+        weight = (w_gate, w_up)[half]
+        slot = (2 * step + half) % ring
+        return pltpu.make_async_copy(
+            weight.at[index // per_slot, :, columns(index % per_slot * FBLOCK, FBLOCK)],
+            buffer.at[slot],
+            sems.at[slot],
+        )
+
+    for u in range(min(ring, 2 * streamed)):
+        copies(u // 2, u % 2).start()
+
+    power = jnp.zeros((count, LANES), F32)
+    for k in range(sides):
+        base = jnp.bitwise_xor(side, k) * width
+        flip = place_of(k, sides)
+        for p in range(sides):
+            q = p ^ flip
+            stream[p * games : (p + 1) * games, columns(base, width)] = chunks[k][
+                q * games : (q + 1) * games, :
+            ]
+    for c in range(0, features, LANES):
+        wide = stream[:, c : c + LANES].astype(F32)
+        power = power + wide * wide
+    norm = lax.rsqrt(jnp.sum(power, axis=-1, keepdims=True) / features + 1e-05)
+    experts = router.shape[0]
+    for c in range(0, features, 512):
+        s = slice(c, c + 512)
+        normed = stream[:, s].astype(F32) * norm * gain[:, s].astype(F32)
+        high = normed.astype(BF16)
+        rows[:count, s] = high
+        rows[count:, s] = (normed - high.astype(F32)).astype(BF16)
+        weight = router[:, s]
+        top = weight.astype(BF16).astype(F32)
+        router2[:, s] = jnp.concatenate([top, weight - top], axis=0).astype(BF16)
+    products = lax.dot_general(
+        rows[...], router2[...], (((1,), (1,)), ((), ())), preferred_element_type=F32
+    )
+    products = products[:count] + products[count:]
+    logits = products[:, :experts] + products[:, experts:]
+    route = jnp.concatenate(
+        [blocks[place_of(p, sides)][:, -LANES:] for p in range(sides)], axis=0
+    ).astype(F32)
+    lane = lax.broadcasted_iota(jnp.int32, route.shape, 1)
+    ids = [jnp.sum(jnp.where(lane == j, route, 0.0), axis=-1, keepdims=True) for j in range(2)]
+    number = lax.broadcasted_iota(jnp.int32, logits.shape, 1).astype(F32)
+    chosen = [
+        jnp.sum(jnp.where(number == ids[j], logits, 0.0), axis=-1, keepdims=True)
+        for j in range(2)
+    ]
+    shares = [
+        1.0 / (1.0 + jnp.exp(chosen[1] - chosen[0])),
+        1.0 / (1.0 + jnp.exp(chosen[0] - chosen[1])),
+    ]
+    for i in range(slots):
+        expert = ((side * slots + i) // split).astype(F32)
+        weight = jnp.where(ids[0] == expert, shares[0], 0.0) + jnp.where(
+            ids[1] == expert, shares[1], 0.0
+        )
+        scale[i] = jnp.broadcast_to(weight, (count, FBLOCK))
+    mine[...] = stream[:games, columns(tensor * mine.shape[1], mine.shape[1])]
+
+    def finish(index, gate, upward):
+        value = gate / (1.0 + jnp.exp(-gate)) * upward * scale[index // per_slot]
+        inner[:, columns(index * FBLOCK, FBLOCK)] = value.astype(BF16)
+
+    def product(weight):
+        return jnp.dot(rows[:count], weight, preferred_element_type=F32)
+
+    def from_ring(step):
+        parts = []
+        for half in range(2):
+            slot = (2 * step + half) % ring
+            copies(step, half).wait()
+            parts.append(product(buffer[slot]))
+
+            @pl.when(2 * step + half + ring < 2 * streamed)
+            def _():
+                copies(step + ring // 2, half).start()
+
+        finish(kept + step, *parts)
+
+    def run(first, last):
+        if last > first:
+            pl.loop(first, last)(from_ring)
+
+    done = 0
+    index = 0
+    for array, n in zip(ready, held, strict=True):
+        for i in range(n):
+            finish(jnp.int32(index), product(array[i, 0]), product(array[i, 1]))
+            index += 1
+            until = streamed * index // kept
+            run(done, until)
+            done = until
+    run(done, streamed)
+
+
+def expand(sides, split, chunks, blocks, gain, router, w_gate, w_up, held, ready, own_width):
+    games = blocks[0].shape[0]
+    count = games * sides
+    features = chunks[0].shape[1] * sides
+    slots, _, hidden = w_gate.shape
+    ring = 4
+    moved = 2 * w_gate.size * 2
+    return pl.pallas_call(
+        functools.partial(expand_body, sides, held, 0, split, ring),
+        in_specs=[VMEM] * (2 * sides + 2) + [ANY, ANY] + [VMEM] * len(ready),
+        out_specs=[VMEM, VMEM],
+        out_shape=[
+            jax.ShapeDtypeStruct((count, slots * hidden), BF16),
+            jax.ShapeDtypeStruct((games, own_width), BF16),
+        ],
+        scratch_shapes=[
+            pltpu.VMEM((count, features), BF16),
+            pltpu.VMEM((2 * count, features), BF16),
+            pltpu.VMEM((2 * router.shape[0], features), BF16),
+            pltpu.VMEM((slots, count, FBLOCK), F32),
+            pltpu.VMEM((ring, features, FBLOCK), BF16),
+            pltpu.SemaphoreType.DMA((ring,)),
+        ],
+        compiler_params=pltpu.CompilerParams(vmem_limit_bytes=20 * MIB),
+        cost_estimate=cost(4 * count * w_gate.size, moved),
+        name="expand",
+    )(*chunks, *blocks, gain, router, w_gate, w_up, *ready)
+
+
+def contract_body(tensors, ring, block, inner, w_down, keep, send, buffer, sems):
+    slots, hidden, features = w_down.shape
+    tensor = lax.axis_index("tensor")
+    part = features // tensors
+    per_part = part // block
+    steps = features // block
+    half = keep.shape[0]
+
+    def copies(step, slot):
+        at = (slots * step + slot) % ring
+        k = step // per_part
+        start = jnp.bitwise_xor(tensor, k) * part + step % per_part * block
+        return pltpu.make_async_copy(
+            w_down.at[slot, :, columns(start, block)], buffer.at[at], sems.at[at]
+        )
+
+    for u in range(min(ring, slots * steps)):
+        copies(u // slots, u % slots).start()
+
+    @pl.loop(0, steps)
+    def _(step):
+        total = None
+        for slot in range(slots):
+            copies(step, slot).wait()
+            at = (slots * step + slot) % ring
+            value = jnp.dot(
+                inner[:, slot * hidden : (slot + 1) * hidden],
+                buffer[at],
+                preferred_element_type=F32,
+            )
+            total = value if total is None else total + value
+
+            @pl.when(slots * step + slot + ring < slots * steps)
+            def _():
+                copies(step + ring // slots, slot).start()
+
+        where = columns(step * block, block)
+        keep[:, where] = total[:half]
+        send[:, where] = total[half:].astype(BF16)
+
+
+def contract(tensors, inner, w_down):
+    count = inner.shape[0]
+    slots, hidden, features = w_down.shape
+    ring = 6
+    block = 512 if features // tensors % 512 == 0 else LANES
+    return pl.pallas_call(
+        functools.partial(contract_body, tensors, ring, block),
+        in_specs=[VMEM, ANY],
+        out_specs=[VMEM, VMEM],
+        out_shape=[
+            jax.ShapeDtypeStruct((count // 2, features), F32),
+            jax.ShapeDtypeStruct((count // 2, features), BF16),
+        ],
+        scratch_shapes=[
+            pltpu.VMEM((ring, hidden, block), BF16),
+            pltpu.SemaphoreType.DMA((ring,)),
+        ],
+        compiler_params=pltpu.CompilerParams(vmem_limit_bytes=18 * MIB),
+        cost_estimate=cost(2 * count * w_down.size, 2 * w_down.size),
+        name="contract",
+    )(inner, w_down)
+
+
+def halve_body(keep, arrived, low, high):
+    total = keep[...] + arrived[...].astype(F32)
+    half = low.shape[0]
+    low[...] = total[:half]
+    high[...] = total[half:].astype(BF16)
+
+
+def halve(keep, arrived):
+    rows, width = keep.shape
+    return pl.pallas_call(
+        halve_body,
+        in_specs=[VMEM, VMEM],
+        out_specs=[VMEM, VMEM],
+        out_shape=[
+            jax.ShapeDtypeStruct((rows // 2, width), F32),
+            jax.ShapeDtypeStruct((rows // 2, width), BF16),
+        ],
+        compiler_params=pltpu.CompilerParams(vmem_limit_bytes=6 * MIB),
+        name="halve",
+    )(keep, arrived)
+
+
+def deal_body(keep, arrived, *outs):
+    width = outs[0].shape[1]
+    for k, out in enumerate(outs):
+        s = slice(k * width, (k + 1) * width)
+        out[...] = (keep[:, s] + arrived[:, s].astype(F32)).astype(out.dtype)
+
+
+def deal(tensors, keep, arrived):
+    rows, width = keep.shape
+    return pl.pallas_call(
+        deal_body,
+        in_specs=[VMEM, VMEM],
+        out_specs=[VMEM] * tensors,
+        out_shape=[
+            jax.ShapeDtypeStruct((rows, width // tensors), F32 if k == 0 else BF16)
+            for k in range(tensors)
+        ],
+        compiler_params=pltpu.CompilerParams(vmem_limit_bytes=4 * MIB),
+        name="deal",
+    )(keep, arrived)
+
+
+def last_body(*refs):
+    stream, parts, out = refs[0], refs[1:-1], refs[-1]
+    total = parts[0][...]
+    for part in parts[1:]:
+        total = total + part[...].astype(F32)
+    out[...] = (stream[...].astype(F32) + total).astype(BF16)
+
+
+def last(stream, parts):
+    return pl.pallas_call(
+        last_body,
+        in_specs=[VMEM] * (1 + len(parts)),
+        out_specs=VMEM,
+        out_shape=jax.ShapeDtypeStruct(stream.shape, BF16),
+        compiler_params=pltpu.CompilerParams(vmem_limit_bytes=4 * MIB),
+        name="last",
+    )(stream, *parts)
+
+
+def shards_kernels(
+    query,
+    new_key,
+    new_value,
+    key_cache,
+    value_cache,
+    cache_len,
+    resid,
+    w_out,
+    rms_gain,
+    w_router,
+    route_ids,
+    w_gate,
+    w_up,
+    w_down,
+):
+    sides, tensors = lax.axis_size("side"), lax.axis_size("tensor")
+    features = resid.shape[1]
+    depth = query.shape[1]
+    extra = features // (sides * tensors)
+    blocks = attend(
+        sides, extra, query, new_key, new_value, key_cache, value_cache, cache_len, resid, route_ids
+    )
+    blocks = [blocks[0]] + [swap(blocks[k], "side", sides, k) for k in range(1, sides)]
+    parts = project(sides, tensors, blocks, w_out)
+    parts = [parts[0]] + [swap(parts[k], "tensor", tensors, k) for k in range(1, tensors)]
+    stream = stream_of(sides, tensors, depth, parts, blocks)
+    pieces = [stream] + [swap(stream, "tensor", tensors, k) for k in range(1, tensors)]
+    own = gather_columns(tensors, pieces)
+    across = swap(own, "side", sides, 2)
+    beside = swap(own, "side", sides, 1)
+    chunks = [own, beside, across, swap(across, "side", sides, 1)]
+    experts = w_router.shape[1]
+    slots = w_gate.shape[0]
+    split = slots * sides // experts
+    held, ready = [], []
+    inner, mine = expand(
+        sides,
+        split,
+        chunks,
+        blocks,
+        rms_gain.reshape(1, features),
+        w_router.T,
+        w_gate,
+        w_up,
+        held,
+        ready,
+        features // tensors,
+    )
+    keep, send = contract(tensors, inner, w_down)
+    low, high = halve(keep, swap(send, "side", sides, 1))
+    dealt = deal(tensors, low, swap(high, "side", sides, 2))
+    dealt = [dealt[0]] + [swap(dealt[k], "tensor", tensors, k) for k in range(1, tensors)]
+    return last(mine, dealt)
 
 
 def attend_local(query, new_key, new_value, key_cache, value_cache, cache_len):
@@ -114,9 +691,14 @@
     return (local_stream + moe).astype(jnp.bfloat16)
 
 
+def tiles(mesh, sides=4):
+    side, tensor = mesh.shape["side"], mesh.shape["tensor"]
+    return side == sides and tensor & (tensor - 1) == 0
+
+
 def solution(mesh):
     return jax.shard_map(
-        shards,
+        shards_kernels if tiles(mesh) else shards,
         mesh=mesh,
         in_specs=(
             P(("groups", "side"), "tensor"),

time: 229 us -> 121 us (0.53)
  matrix products: 72.4 us -> 0 us
  waiting for transfers between devices: 92.2 us -> 28.3 us
  Pallas kernels: 0 us -> 60.7 us
  blocking collectives: 25.1 us -> 0 us
  between operations: 13.6 us -> 0.09 us
  starting transfers between devices: 8.29 us -> 19.6 us
  other arithmetic: 4.01 us -> 0 us
    dot_general x10 -> x0, matrix products: 72.4 us -> none  [the longest x1 21.5 us: shards(): jnp.einsum('sjcf,jfd->sjcd', inner, w_down, preferred_element_type=jnp.fl...]
    pallas_call x0 -> x9, Pallas kernels: none -> 60.7 us  [the longest x1 35.2 us: expand(): pl.pallas_call(functools.partial(expand_body, sides, held, 0, split, ring...]
    psum x1 -> x0, waiting for transfers between devices: 37.5 us -> none  [shards(): attn_out = lax.psum(partial_out, 'tensor')]
    all_to_all x2 -> x0, waiting for transfers between devices: 35 us -> none  [the longest x1 27.8 us: shards(): lax.all_to_all(expert_part, 'side', split_axis=0, concat_axis=0, tiled=True)]
    ppermute x0 -> x17, waiting for transfers between devices: none -> 28.3 us  [swap(): return lax.ppermute(value, axis, [(i, i ^ mask) for i in range(count)])]
    reduce_scatter x1 -> x0, waiting for transfers between devices: 19.6 us -> none  [shards(): lax.psum_scatter(jnp.einsum('ecg,ecf->gf', scaled_place, merged, precisio...]
    ppermute x0 -> x17, starting transfers between devices: none -> 19.6 us  [swap(): return lax.ppermute(value, axis, [(i, i ^ mask) for i in range(count)])]
    all_to_all x1 -> x0, blocking collectives: 18.3 us -> none  [shards(): lax.all_to_all(packed, 'side', split_axis=0, concat_axis=0, tiled=True)]
  transfers between devices with their start and end apart: 4 -> 17, of which waited for: 4 -> 12; matrix products, arithmetic and copies ran while one was open for 0% -> 1% of each run, Pallas kernels for 0% -> 0%
where the time goes in v1:
time: 121 us; the launch traced here: 120 us
  Pallas kernels  60.7 us (50%)
  waiting for transfers between devices  28.3 us (23%)
  starting transfers between devices  19.6 us (16%)
  local copies, waits for them, and re-layouts  11.6 us (10%)
    pallas_call x1, Pallas kernels, expand(): pl.pallas_call(functools.partial(expand_body, sides, held, 0, split, ring...  35.2 us
    ppermute x17, waiting for transfers between devices, swap(): return lax.ppermute(value, axis, [(i, i ^ mask) for i in range(count)])  28.3 us
    ppermute x17, starting transfers between devices, swap(): return lax.ppermute(value, axis, [(i, i ^ mask) for i in range(count)])  19.6 us
    pallas_call x1, Pallas kernels, contract(): pl.pallas_call(functools.partial(contract_body, tensors, ring, block), in...  16.9 us
    unnamed x20, local copies, waits for them, and re-layouts  10.9 us
    pallas_call x1, Pallas kernels, attend(): pl.pallas_call(functools.partial(attend_body, sides, steps), grid=(steps,...  6.9 us
  transfers between devices with their start and end apart: 17, of which 12 were waited for; matrix products, arithmetic and copies ran while one was open for 1% of the time, Pallas kernels for 0%

profile of v1, /device:TPU:0, one launch (start us, length us, event | category | flops | bytes accessed | tf_op | source)
XLA Modules:
  0.0 120.3 jit_solution(603044846536361935)
XLA Ops:
  0.0 1.6 %copy-done.1 = bf16[16,256,256]{2,1,0:T(8,128)(2,1)S(1)} copy-done((bf16[16,256,256]{2,1,0:T(8,128)(2,1)S(1)}, bf16[16,256,256]{2,1,0:T(8,128)(2,1)}, u32[]{:S(2)}) %copy-start.1) | copy-done | bytes 2097176
  1.6 1.6 %copy-done.2 = bf16[16,256,256]{2,1,0:T(8,128)(2,1)S(1)} copy-done((bf16[16,256,256]{2,1,0:T(8,128)(2,1)S(1)}, bf16[16,256,256]{2,1,0:T(8,128)(2,1)}, u32[]{:S(2)}) %copy-start.2) | copy-done | bytes 2097176
  3.2 0.9 copy-done.4
  4.1 0.8 copy-done.5
  4.9 0.7 copy-done.6
  5.6 0.7 copy-done.7
  6.3 0.7 copy-done.8
  7.0 0.7 copy-done.9
  7.6 6.9 %attend.1 = (bf16[16,2048]{1,0:T(8,128)(2,1)S(1)}, bf16[16,2048]{1,0:T(8,128)(2,1)S(1)}, bf16[16,2048]{1,0:T(8,128)(2,1)S(1)}, bf16[16,2048]{1,0:T(8,128)(2,1)S(1)}) custom-call(s32[16]{0:T(128)S(1)} %copy-done.9, bf16[16,1536]{1,0:T(8,128)(2,1)S(1)} %copy-done.5, bf16[16,256]{1,0:T(8,128)(2,1)S(1)} %copy-done.6, bf16[16,256]{1,0:T(8,128)(2,1)S(1)} %copy-done.7, ...), custom_call_target="tpu_custom_call" | custom-call | flops 67108864 | bytes 4194304 | tf_op jit(solution)/shard_map/attend/pallas_call | solution.py:118
  14.6 0.5 collective-permute-start
  15.1 2.6 %collective-permute-start.1 = (bf16[16,2048]{1,0:T(8,128)(2,1)S(1)}, bf16[16,2048]{1,0:T(8,128)(2,1)S(1)}, u32[]{:S(2)}, u32[]{:S(2)}) collective-permute-start(bf16[16,2048]{1,0:T(8,128)(2,1)S(1)} %get-tuple-element.25), channel_id=1, source_target_pairs={{0,8},{4,12},{8,0},{12,4},{1,9},{5,13},{9,1},{13,5},{2,10},{6,14},... | collective-permute-start | bytes 196616 | tf_op jit(solution)/shard_map/ppermute | solution.py:32
  17.6 0.1 collective-permute-start.2
  17.7 0.0 collective-permute-done.refs_1_.refs_5_
  17.7 2.6 %collective-permute-done.1.refs_2_.refs_6_ = bf16[16,2048]{1,0:T(8,128)(2,1)S(1)} collective-permute-done((bf16[16,2048]{1,0:T(8,128)(2,1)S(1)}, bf16[16,2048]{1,0:T(8,128)(2,1)S(1)}, u32[]{:S(2)}, u32[]{:S(2)}) %collective-permute-start.1) | collective-permute-done | bytes 65568 | tf_op jit(solution)/shard_map/ppermute | solution.py:32
  20.3 1.4 %collective-permute-done.2.refs_3_.refs_7_ = bf16[16,2048]{1,0:T(8,128)(2,1)S(1)} collective-permute-done((bf16[16,2048]{1,0:T(8,128)(2,1)S(1)}, bf16[16,2048]{1,0:T(8,128)(2,1)S(1)}, u32[]{:S(2)}, u32[]{:S(2)}) %collective-permute-start.2) | collective-permute-done | bytes 65568 | tf_op jit(solution)/shard_map/ppermute | solution.py:32
  21.7 2.3 %copy-done = bf16[1536,1536]{1,0:T(8,128)(2,1)S(1)} copy-done((bf16[1536,1536]{1,0:T(8,128)(2,1)S(1)}, bf16[1536,1536]{1,0:T(8,128)(2,1)}, u32[]{:S(2)}) %copy-start) | copy-done | bytes 4718616
  24.0 1.0 project.1
  25.0 1.6 %collective-permute-start.3 = (bf16[64,384]{1,0:T(8,128)(2,1)S(1)}, bf16[64,384]{1,0:T(8,128)(2,1)S(1)}, u32[]{:S(2)}, u32[]{:S(2)}) collective-permute-start(bf16[64,384]{1,0:T(8,128)(2,1)S(1)} %get-tuple-element.28), channel_id=1, source_target_pairs={{0,1},{1,0},{2,3},{3,2},{4,5},{5,4},{6,7},{7,6},{8,9},{9,8},{10,11... | collective-permute-start | bytes 147464 | tf_op jit(solution)/shard_map/ppermute | solution.py:32
  26.6 2.6 %collective-permute-start.4 = (bf16[64,384]{1,0:T(8,128)(2,1)S(1)}, bf16[64,384]{1,0:T(8,128)(2,1)S(1)}, u32[]{:S(2)}, u32[]{:S(2)}) collective-permute-start(bf16[64,384]{1,0:T(8,128)(2,1)S(1)} %get-tuple-element.29), channel_id=1, source_target_pairs={{0,2},{1,3},{2,0},{3,1},{4,6},{5,7},{6,4},{7,5},{8,10},{9,11},{10,... | collective-permute-start | bytes 147464 | tf_op jit(solution)/shard_map/ppermute | solution.py:32
  29.2 0.2 collective-permute-start.5
  29.4 0.0 collective-permute-done.3.refs_1_
  29.4 3.1 %collective-permute-done.4.refs_2_ = bf16[64,384]{1,0:T(8,128)(2,1)S(1)} collective-permute-done((bf16[64,384]{1,0:T(8,128)(2,1)S(1)}, bf16[64,384]{1,0:T(8,128)(2,1)S(1)}, u32[]{:S(2)}, u32[]{:S(2)}) %collective-permute-start.4) | collective-permute-done | bytes 49184 | tf_op jit(solution)/shard_map/ppermute | solution.py:32
  32.5 2.6 %collective-permute-done.5.refs_3_ = bf16[64,384]{1,0:T(8,128)(2,1)S(1)} collective-permute-done((bf16[64,384]{1,0:T(8,128)(2,1)S(1)}, bf16[64,384]{1,0:T(8,128)(2,1)S(1)}, u32[]{:S(2)}, u32[]{:S(2)}) %collective-permute-start.5) | collective-permute-done | bytes 49184 | tf_op jit(solution)/shard_map/ppermute | solution.py:32
  35.1 1.1 collective-permute-start.8
  36.3 3.3 %collective-permute-start.6 = (bf16[64,384]{1,0:T(8,128)(2,1)S(1)}, bf16[64,384]{1,0:T(8,128)(2,1)S(1)}, u32[]{:S(2)}, u32[]{:S(2)}) collective-permute-start(bf16[64,384]{1,0:T(8,128)(2,1)S(1)} %stream.1.refs_0_), channel_id=1, source_target_pairs={{0,1},{1,0},{2,3},{3,2},{4,5},{5,4},{6,7},{7,6},{8,9},{9,8},{10,11... | collective-permute-start | bytes 147464 | tf_op jit(solution)/shard_map/ppermute | solution.py:32
  39.6 1.5 %collective-permute-done.8.refs_3_ = bf16[64,384]{1,0:T(8,128)(2,1)S(1)} collective-permute-done((bf16[64,384]{1,0:T(8,128)(2,1)S(1)}, bf16[64,384]{1,0:T(8,128)(2,1)S(1)}, u32[]{:S(2)}, u32[]{:S(2)}) %collective-permute-start.8) | collective-permute-done | bytes 49184 | tf_op jit(solution)/shard_map/ppermute | solution.py:32
  41.1 1.0 collective-permute-done.7.refs_2_
  42.2 0.0 collective-permute-done.6.refs_1_
  42.2 1.4 %collective-permute-start.10 = (bf16[64,1536]{1,0:T(8,128)(2,1)S(1)}, bf16[64,1536]{1,0:T(8,128)(2,1)S(1)}, u32[]{:S(2)}, u32[]{:S(2)}) collective-permute-start(bf16[64,1536]{1,0:T(8,128)(2,1)S(1)} %columns.1.refs_0_), channel_id=1, source_target_pairs={{0,8},{4,12},{8,0},{12,4},{1,9},{5,13},{9,1},{13,5},{2,10},{6,14},... | collective-permute-start | bytes 589832 | tf_op jit(solution)/shard_map/ppermute | solution.py:32
  43.6 0.0 collective-permute-start.9
  43.6 4.3 %collective-permute-done.10.refs_2_ = bf16[64,1536]{1,0:T(8,128)(2,1)S(1)} collective-permute-done((bf16[64,1536]{1,0:T(8,128)(2,1)S(1)}, bf16[64,1536]{1,0:T(8,128)(2,1)S(1)}, u32[]{:S(2)}, u32[]{:S(2)}) %collective-permute-start.10) | collective-permute-done | bytes 196640 | tf_op jit(solution)/shard_map/ppermute | solution.py:32
  47.9 0.0 collective-permute-start.11
  47.9 0.7 reshape.3.refs_8_
  48.7 0.7 collective-permute-done.11.refs_3_
  49.4 0.9 copy-done.3
  50.3 35.2 %expand.1 = (bf16[64,4096]{1,0:T(8,128)(2,1)S(1)}, bf16[16,1536]{1,0:T(8,128)(2,1)S(1)}) custom-call(bf16[64,1536]{1,0:T(8,128)(2,1)S(1)} %columns.1.refs_0_, bf16[64,1536]{1,0:T(8,128)(2,1)S(1)} %collective-permute-done.9.refs_1_, bf16[64,1536]{1,0:T(8,128)(2,1)S(1)} %collective-permute-done.10.refs_2_, ...), custom_call_target="tpu_custom_call" | custom-call | flops 6442450944 | bytes 100663296 | tf_op jit(solution)/shard_map/expand/pallas_call | solution.py:382
  85.5 16.9 %contract.1 = (f32[32,6144]{1,0:T(8,128)S(1)}, bf16[32,6144]{1,0:T(8,128)(2,1)S(1)}) custom-call(bf16[64,4096]{1,0:T(8,128)(2,1)S(1)} %get-tuple-element.32.inner, bf16[2,2048,6144]{2,1,0:T(8,128)(2,1)} %w_down.1), custom_call_target="tpu_custom_call" | custom-call | flops 3221225472 | bytes 50331648 | tf_op jit(solution)/shard_map/contract/pallas_call | solution.py:450
  102.4 0.2 collective-permute-start.12
  102.6 1.6 %collective-permute-done.12.arrived = bf16[32,6144]{1,0:T(8,128)(2,1)S(1)} collective-permute-done((bf16[32,6144]{1,0:T(8,128)(2,1)S(1)}, bf16[32,6144]{1,0:T(8,128)(2,1)S(1)}, u32[]{:S(2)}, u32[]{:S(2)}) %collective-permute-start.12) | collective-permute-done | bytes 393248 | tf_op jit(solution)/shard_map/ppermute | solution.py:32
  104.2 0.1 halve.1
  104.2 1.4 %collective-permute-start.13 = (bf16[16,6144]{1,0:T(8,128)(2,1)S(1)}, bf16[16,6144]{1,0:T(8,128)(2,1)S(1)}, u32[]{:S(2)}, u32[]{:S(2)}) collective-permute-start(bf16[16,6144]{1,0:T(8,128)(2,1)S(1)} %get-tuple-element.36), channel_id=1, source_target_pairs={{0,8},{4,12},{8,0},{12,4},{1,9},{5,13},{9,1},{13,5},{2,10},{6,14},... | collective-permute-start | bytes 589832 | tf_op jit(solution)/shard_map/ppermute | solution.py:32
  105.7 5.6 %collective-permute-done.13.arrived = bf16[16,6144]{1,0:T(8,128)(2,1)S(1)} collective-permute-done((bf16[16,6144]{1,0:T(8,128)(2,1)S(1)}, bf16[16,6144]{1,0:T(8,128)(2,1)S(1)}, u32[]{:S(2)}, u32[]{:S(2)}) %collective-permute-start.13) | collective-permute-done | bytes 196640 | tf_op jit(solution)/shard_map/ppermute | solution.py:32
  111.3 1.6 %collective-permute-start.14 = (bf16[16,1536]{1,0:T(8,128)(2,1)S(1)}, bf16[16,1536]{1,0:T(8,128)(2,1)S(1)}, u32[]{:S(2)}, u32[]{:S(2)}) collective-permute-start(bf16[16,1536]{1,0:T(8,128)(2,1)S(1)} %get-tuple-element.38), channel_id=1, source_target_pairs={{0,1},{1,0},{2,3},{3,2},{4,5},{5,4},{6,7},{7,6},{8,9},{9,8},{10,11... | collective-permute-start | bytes 147464 | tf_op jit(solution)/shard_map/ppermute | solution.py:32
  112.9 0.9 collective-permute-start.15
  113.8 2.0 %collective-permute-start.16 = (bf16[16,1536]{1,0:T(8,128)(2,1)S(1)}, bf16[16,1536]{1,0:T(8,128)(2,1)S(1)}, u32[]{:S(2)}, u32[]{:S(2)}) collective-permute-start(bf16[16,1536]{1,0:T(8,128)(2,1)S(1)} %get-tuple-element.40), channel_id=1, source_target_pairs={{0,3},{1,2},{2,1},{3,0},{4,7},{5,6},{6,5},{7,4},{8,11},{9,10},{10,... | collective-permute-start | bytes 147464 | tf_op jit(solution)/shard_map/ppermute | solution.py:32
  115.7 2.8 %collective-permute-done.15.refs_3_ = bf16[16,1536]{1,0:T(8,128)(2,1)S(1)} collective-permute-done((bf16[16,1536]{1,0:T(8,128)(2,1)S(1)}, bf16[16,1536]{1,0:T(8,128)(2,1)S(1)}, u32[]{:S(2)}, u32[]{:S(2)}) %collective-permute-start.15) | collective-permute-done | bytes 49184 | tf_op jit(solution)/shard_map/ppermute | solution.py:32
  118.5 1.2 collective-permute-done.16.refs_4_
  119.7 0.7 last.1
  (16 shorter events, 0.1 us)
Async XLA Ops:
  0.0 1.6 %copy-start.1 = (bf16[16,256,256]{2,1,0:T(8,128)(2,1)S(1)}, bf16[16,256,256]{2,1,0:T(8,128)(2,1)}, u32[]{:S(2)}) copy-start(bf16[16,256,256]{2,1,0:T(8,128)(2,1)} %keys.1) | copy-start | bytes 6291460
  1.6 1.6 %copy-start.2 = (bf16[16,256,256]{2,1,0:T(8,128)(2,1)S(1)}, bf16[16,256,256]{2,1,0:T(8,128)(2,1)}, u32[]{:S(2)}) copy-start(bf16[16,256,256]{2,1,0:T(8,128)(2,1)} %values.1) | copy-start | bytes 6291460
  3.2 0.9 copy-start.4
  4.1 0.8 copy-start.5
  4.9 0.7 copy-start.6
  5.6 0.7 copy-start.7
  6.3 0.7 copy-start.8
  7.0 0.7 copy-start.9
  14.6 3.2 %collective-permute-start = (bf16[16,2048]{1,0:T(8,128)(2,1)S(1)}, bf16[16,2048]{1,0:T(8,128)(2,1)S(1)}, u32[]{:S(2)}, u32[]{:S(2)}) collective-permute-start(bf16[16,2048]{1,0:T(8,128)(2,1)S(1)} %get-tuple-element.24), channel_id=1, source_target_pairs={{0,4},{4,0},{8,12},{12,8},{1,5},{5,1},{9,13},{13,9},{2,6},{6,2},{1... | collective-permute-start | bytes 196616 | tf_op jit(solution)/shard_map/ppermute | solution.py:32
  15.1 5.2 %collective-permute-start.1 = (bf16[16,2048]{1,0:T(8,128)(2,1)S(1)}, bf16[16,2048]{1,0:T(8,128)(2,1)S(1)}, u32[]{:S(2)}, u32[]{:S(2)}) collective-permute-start(bf16[16,2048]{1,0:T(8,128)(2,1)S(1)} %get-tuple-element.25), channel_id=1, source_target_pairs={{0,8},{4,12},{8,0},{12,4},{1,9},{5,13},{9,1},{13,5},{2,10},{6,14},... | collective-permute-start | bytes 196616 | tf_op jit(solution)/shard_map/ppermute | solution.py:32
  17.6 4.0 %collective-permute-start.2 = (bf16[16,2048]{1,0:T(8,128)(2,1)S(1)}, bf16[16,2048]{1,0:T(8,128)(2,1)S(1)}, u32[]{:S(2)}, u32[]{:S(2)}) collective-permute-start(bf16[16,2048]{1,0:T(8,128)(2,1)S(1)} %get-tuple-element.26), channel_id=1, source_target_pairs={{0,12},{4,8},{8,4},{12,0},{1,13},{5,9},{9,5},{13,1},{2,14},{6,10},... | collective-permute-start | bytes 196616 | tf_op jit(solution)/shard_map/ppermute | solution.py:32
  21.7 2.3 %copy-start = (bf16[1536,1536]{1,0:T(8,128)(2,1)S(1)}, bf16[1536,1536]{1,0:T(8,128)(2,1)}, u32[]{:S(2)}) copy-start(bf16[1536,1536]{1,0:T(8,128)(2,1)} %refs_4_.1) | copy-start | bytes 14155780
  25.0 4.5 %collective-permute-start.3 = (bf16[64,384]{1,0:T(8,128)(2,1)S(1)}, bf16[64,384]{1,0:T(8,128)(2,1)S(1)}, u32[]{:S(2)}, u32[]{:S(2)}) collective-permute-start(bf16[64,384]{1,0:T(8,128)(2,1)S(1)} %get-tuple-element.28), channel_id=1, source_target_pairs={{0,1},{1,0},{2,3},{3,2},{4,5},{5,4},{6,7},{7,6},{8,9},{9,8},{10,11... | collective-permute-start | bytes 147464 | tf_op jit(solution)/shard_map/ppermute | solution.py:32
  26.6 5.9 %collective-permute-start.4 = (bf16[64,384]{1,0:T(8,128)(2,1)S(1)}, bf16[64,384]{1,0:T(8,128)(2,1)S(1)}, u32[]{:S(2)}, u32[]{:S(2)}) collective-permute-start(bf16[64,384]{1,0:T(8,128)(2,1)S(1)} %get-tuple-element.29), channel_id=1, source_target_pairs={{0,2},{1,3},{2,0},{3,1},{4,6},{5,7},{6,4},{7,5},{8,10},{9,11},{10,... | collective-permute-start | bytes 147464 | tf_op jit(solution)/shard_map/ppermute | solution.py:32
  29.2 5.9 %collective-permute-start.5 = (bf16[64,384]{1,0:T(8,128)(2,1)S(1)}, bf16[64,384]{1,0:T(8,128)(2,1)S(1)}, u32[]{:S(2)}, u32[]{:S(2)}) collective-permute-start(bf16[64,384]{1,0:T(8,128)(2,1)S(1)} %get-tuple-element.30), channel_id=1, source_target_pairs={{0,3},{1,2},{2,1},{3,0},{4,7},{5,6},{6,5},{7,4},{8,11},{9,10},{10,... | collective-permute-start | bytes 147464 | tf_op jit(solution)/shard_map/ppermute | solution.py:32
  35.1 6.0 %collective-permute-start.8 = (bf16[64,384]{1,0:T(8,128)(2,1)S(1)}, bf16[64,384]{1,0:T(8,128)(2,1)S(1)}, u32[]{:S(2)}, u32[]{:S(2)}) collective-permute-start(bf16[64,384]{1,0:T(8,128)(2,1)S(1)} %stream.1.refs_0_), channel_id=1, source_target_pairs={{0,3},{1,2},{2,1},{3,0},{4,7},{5,6},{6,5},{7,4},{8,11},{9,10},{10,... | collective-permute-start | bytes 147464 | tf_op jit(solution)/shard_map/ppermute | solution.py:32
  36.3 5.9 %collective-permute-start.7 = (bf16[64,384]{1,0:T(8,128)(2,1)S(1)}, bf16[64,384]{1,0:T(8,128)(2,1)S(1)}, u32[]{:S(2)}, u32[]{:S(2)}) collective-permute-start(bf16[64,384]{1,0:T(8,128)(2,1)S(1)} %stream.1.refs_0_), channel_id=1, source_target_pairs={{0,2},{1,3},{2,0},{3,1},{4,6},{5,7},{6,4},{7,5},{8,10},{9,11},{10,... | collective-permute-start | bytes 147464 | tf_op jit(solution)/shard_map/ppermute | solution.py:32
  36.3 5.9 %collective-permute-start.6 = (bf16[64,384]{1,0:T(8,128)(2,1)S(1)}, bf16[64,384]{1,0:T(8,128)(2,1)S(1)}, u32[]{:S(2)}, u32[]{:S(2)}) collective-permute-start(bf16[64,384]{1,0:T(8,128)(2,1)S(1)} %stream.1.refs_0_), channel_id=1, source_target_pairs={{0,1},{1,0},{2,3},{3,2},{4,5},{5,4},{6,7},{7,6},{8,9},{9,8},{10,11... | collective-permute-start | bytes 147464 | tf_op jit(solution)/shard_map/ppermute | solution.py:32
  42.2 5.7 %collective-permute-start.10 = (bf16[64,1536]{1,0:T(8,128)(2,1)S(1)}, bf16[64,1536]{1,0:T(8,128)(2,1)S(1)}, u32[]{:S(2)}, u32[]{:S(2)}) collective-permute-start(bf16[64,1536]{1,0:T(8,128)(2,1)S(1)} %columns.1.refs_0_), channel_id=1, source_target_pairs={{0,8},{4,12},{8,0},{12,4},{1,9},{5,13},{9,1},{13,5},{2,10},{6,14},... | collective-permute-start | bytes 589832 | tf_op jit(solution)/shard_map/ppermute | solution.py:32
  43.6 5.0 %collective-permute-start.9 = (bf16[64,1536]{1,0:T(8,128)(2,1)S(1)}, bf16[64,1536]{1,0:T(8,128)(2,1)S(1)}, u32[]{:S(2)}, u32[]{:S(2)}) collective-permute-start(bf16[64,1536]{1,0:T(8,128)(2,1)S(1)} %columns.1.refs_0_), channel_id=1, source_target_pairs={{0,4},{4,0},{8,12},{12,8},{1,5},{5,1},{9,13},{13,9},{2,6},{6,2},{1... | collective-permute-start | bytes 589832 | tf_op jit(solution)/shard_map/ppermute | solution.py:32
  47.9 1.4 %collective-permute-start.11 = (bf16[64,1536]{1,0:T(8,128)(2,1)S(1)}, bf16[64,1536]{1,0:T(8,128)(2,1)S(1)}, u32[]{:S(2)}, u32[]{:S(2)}) collective-permute-start(bf16[64,1536]{1,0:T(8,128)(2,1)S(1)} %collective-permute-done.10.refs_2_), channel_id=1, source_target_pairs={{0,4},{4,0},{8,12},{12,8},{1,5},{5,1},{9,13},{13,9},{2,6},{6,2},{1... | collective-permute-start | bytes 589832 | tf_op jit(solution)/shard_map/ppermute | solution.py:32
  49.4 0.9 copy-start.3
  102.4 1.8 %collective-permute-start.12 = (bf16[32,6144]{1,0:T(8,128)(2,1)S(1)}, bf16[32,6144]{1,0:T(8,128)(2,1)S(1)}, u32[]{:S(2)}, u32[]{:S(2)}) collective-permute-start(bf16[32,6144]{1,0:T(8,128)(2,1)S(1)} %get-tuple-element.34), channel_id=1, source_target_pairs={{0,4},{4,0},{8,12},{12,8},{1,5},{5,1},{9,13},{13,9},{2,6},{6,2},{1... | collective-permute-start | bytes 1179656 | tf_op jit(solution)/shard_map/ppermute | solution.py:32
  104.2 7.0 %collective-permute-start.13 = (bf16[16,6144]{1,0:T(8,128)(2,1)S(1)}, bf16[16,6144]{1,0:T(8,128)(2,1)S(1)}, u32[]{:S(2)}, u32[]{:S(2)}) collective-permute-start(bf16[16,6144]{1,0:T(8,128)(2,1)S(1)} %get-tuple-element.36), channel_id=1, source_target_pairs={{0,8},{4,12},{8,0},{12,4},{1,9},{5,13},{9,1},{13,5},{2,10},{6,14},... | collective-permute-start | bytes 589832 | tf_op jit(solution)/shard_map/ppermute | solution.py:32
  111.3 4.5 %collective-permute-start.14 = (bf16[16,1536]{1,0:T(8,128)(2,1)S(1)}, bf16[16,1536]{1,0:T(8,128)(2,1)S(1)}, u32[]{:S(2)}, u32[]{:S(2)}) collective-permute-start(bf16[16,1536]{1,0:T(8,128)(2,1)S(1)} %get-tuple-element.38), channel_id=1, source_target_pairs={{0,1},{1,0},{2,3},{3,2},{4,5},{5,4},{6,7},{7,6},{8,9},{9,8},{10,11... | collective-permute-start | bytes 147464 | tf_op jit(solution)/shard_map/ppermute | solution.py:32
  112.9 5.6 %collective-permute-start.15 = (bf16[16,1536]{1,0:T(8,128)(2,1)S(1)}, bf16[16,1536]{1,0:T(8,128)(2,1)S(1)}, u32[]{:S(2)}, u32[]{:S(2)}) collective-permute-start(bf16[16,1536]{1,0:T(8,128)(2,1)S(1)} %get-tuple-element.39), channel_id=1, source_target_pairs={{0,2},{1,3},{2,0},{3,1},{4,6},{5,7},{6,4},{7,5},{8,10},{9,11},{10,... | collective-permute-start | bytes 147464 | tf_op jit(solution)/shard_map/ppermute | solution.py:32
  113.8 5.9 %collective-permute-start.16 = (bf16[16,1536]{1,0:T(8,128)(2,1)S(1)}, bf16[16,1536]{1,0:T(8,128)(2,1)S(1)}, u32[]{:S(2)}, u32[]{:S(2)}) collective-permute-start(bf16[16,1536]{1,0:T(8,128)(2,1)S(1)} %get-tuple-element.40), channel_id=1, source_target_pairs={{0,3},{1,2},{2,1},{3,0},{4,7},{5,6},{6,5},{7,4},{8,11},{9,10},{10,... | collective-permute-start | bytes 147464 | tf_op jit(solution)/shard_map/ppermute | solution.py:32

commit v2 on v1

v2 whole, which is shorter than its diff:
```python
import functools
import math

import jax
import jax.numpy as jnp
from jax import lax
from jax.experimental import pallas as pl
from jax.experimental.pallas import tpu as pltpu
from jax.sharding import PartitionSpec as P

HEAD_DIM = 128
CAP = 12
LANES = 128
FBLOCK = 256
BF16 = jnp.bfloat16
F32 = jnp.float32
SCOPE = 8 * 2**20
VMEM = pl.BlockSpec(memory_space=pltpu.VMEM)
SMEM = pl.BlockSpec(memory_space=pltpu.SMEM)
ANY = pl.BlockSpec(memory_space=pl.ANY)
HBM = pl.BlockSpec(memory_space=pltpu.HBM)


def cost(flops, moved):
    return pl.CostEstimate(flops=int(flops), bytes_accessed=int(moved), transcendentals=0)


def place_of(position, count):
    bits = count.bit_length() - 1
    return sum(((position >> b) & 1) << (bits - 1 - b) for b in range(bits))


def swap(value, axis, count, mask):
    return lax.ppermute(value, axis, [(i, i ^ mask) for i in range(count)])


def in_hbm(*arrays):
    return [pltpu.with_memory_space_constraint(a, pltpu.HBM) for a in arrays]


def in_vmem(*arrays):
    return [pltpu.with_memory_space_constraint(a, pltpu.VMEM) for a in arrays]


def columns(start, size):
    return pl.ds(pl.multiple_of(start, LANES), size)


def attend_body(
    sides,
    block,
    length,
    query_at,
    new_key_at,
    new_value_at,
    keys_at,
    values_at,
    resid_at,
    route_at,
    w_out_at,
    *rest,
):
    outs, w_out, rest = rest[:sides], rest[sides], rest[sides + 1 :]
    query, new_key, new_value, keys, values, resid, route, sems, rest = *rest[:8], rest[8:]
    spread, mixed, score, own_score, key32, value32 = rest
    games, width = query.shape
    heads = width // HEAD_DIM
    padded = spread.shape[1]
    wide = new_key.shape[1]
    repeat = heads * HEAD_DIM // wide
    scale = 1.0 / HEAD_DIM**0.5
    steps = games // block

    def copy(source, target, sem):
        return pltpu.make_async_copy(source, target, sems.at[sem])

    small = [
        copy(source, target, i)
        for i, (source, target) in enumerate(
            (
                (query_at, query),
                (new_key_at, new_key),
                (new_value_at, new_value),
                (route_at, route),
                (resid_at, resid),
            )
        )
    ]
    caches = [
        [
            copy(source.at[pl.ds(i * block, block)], target.at[pl.ds(i * block, block)], sem + i)
            for i in range(steps)
        ]
        for source, target, sem in ((keys_at, keys, 5), (values_at, values, 5 + steps))
    ]
    after = copy(w_out_at, w_out, 5 + 2 * steps)
    for c in small[:4] + caches[0] + caches[1] + small[4:] + [after]:
        c.start()
    spread[...] = jnp.zeros_like(spread)
    for c in small[:4]:
        c.wait()
    for h in range(heads):
        lane = h // repeat * HEAD_DIM
        spread[:, h, lane : lane + HEAD_DIM] = query[
            :, h * HEAD_DIM : (h + 1) * HEAD_DIM
        ].astype(F32)
    key32[...] = new_key[...].astype(F32)
    value32[...] = new_value[...].astype(F32)
    for game in range(games):
        if game % block == 0:
            caches[0][game // block].wait()
        q = spread[game]
        s = slice(game * padded, (game + 1) * padded)
        value = (
            lax.dot_general(
                q.astype(BF16), keys[game], (((1,), (1,)), ((), ())), preferred_element_type=F32
            )
            * scale
        )
        at = lax.broadcasted_iota(jnp.int32, value.shape, 1)
        score[s] = jnp.where(at < length[game], value, -jnp.inf)
        own = jnp.sum(q * key32[game : game + 1, :], axis=-1, keepdims=True) * scale
        own_score[s] = jnp.broadcast_to(own, (padded, LANES))
    for i in range(steps):
        s = slice(i * block * padded, (i + 1) * block * padded)
        own = own_score[s][:, :1]
        value = score[s]
        top = jnp.maximum(jnp.max(value, axis=-1, keepdims=True), own)
        e = jnp.exp(value - top)
        own_e = jnp.exp(own - top)
        total = jnp.sum(e, axis=-1, keepdims=True) + own_e
        score[s] = e / total
        own_score[s] = jnp.broadcast_to(
            (own_e / total).astype(BF16).astype(F32), (block * padded, LANES)
        )
        caches[1][i].wait()
        for game in range(i * block, (i + 1) * block):
            s = slice(game * padded, (game + 1) * padded)
            mixed[game] = (
                jnp.dot(score[s].astype(BF16), values[game], preferred_element_type=F32)
                + own_score[s][:, :1] * value32[game : game + 1, :]
            )
    small[4].wait()
    side, tensor = lax.axis_index("side"), lax.axis_index("tensor")
    for h in range(heads):
        lane = h // repeat * HEAD_DIM
        part = mixed[:, h, lane : lane + HEAD_DIM].astype(BF16)
        for out in outs:
            out[:, h * HEAD_DIM : (h + 1) * HEAD_DIM] = part
    extra = outs[0].shape[1] - width - LANES
    row = lax.broadcasted_iota(jnp.int32, (games, games), 0)
    diagonal = row == lax.broadcasted_iota(jnp.int32, (games, games), 1)
    lane = lax.broadcasted_iota(jnp.int32, (games, LANES), 1)
    routes = jnp.zeros((games, LANES), F32)
    for j in range(route.shape[0]):
        ids = jnp.broadcast_to(route[j : j + 1, :].astype(F32), (games, games))
        column = jnp.sum(jnp.where(diagonal, ids, 0.0), axis=-1, keepdims=True)
        routes = jnp.where(lane == j, column, routes)
    features = resid.shape[1] // sides
    for k, out in enumerate(outs):
        start = jnp.bitwise_xor(side, k) * features + tensor % 2 * extra
        out[:, width : width + extra] = resid[:, columns(start, extra)]
        out[:, width + extra :] = routes.astype(BF16)
    after.wait()


def attend(
    sides, extra, query, new_key, new_value, key_cache, value_cache, cache_len, resid, route_ids, w_out
):
    games, width = query.shape
    positions, wide = key_cache.shape[1:]
    block = 4
    heads = -(-(width // HEAD_DIM) // 16) * 16
    out = jax.ShapeDtypeStruct((games, width + extra + LANES), BF16)
    routes = route_ids.T
    arrays = [query, new_key, new_value, key_cache, value_cache, resid, routes]
    return pl.pallas_call(
        functools.partial(attend_body, sides, block),
        in_specs=[SMEM] + [HBM] * (len(arrays) + 1),
        out_specs=[VMEM] * (sides + 1),
        out_shape=[out] * sides + [pltpu.VMEM(w_out.shape, BF16)],
        scratch_shapes=[pltpu.VMEM(a.shape, a.dtype) for a in arrays]
        + [
            pltpu.SemaphoreType.DMA((6 + 2 * (games // block),)),
            pltpu.VMEM((games, heads, wide), F32),
            pltpu.VMEM((games, heads, wide), F32),
            pltpu.VMEM((games * heads, positions), F32),
            pltpu.VMEM((games * heads, LANES), F32),
            pltpu.VMEM((games, wide), F32),
            pltpu.VMEM((games, wide), F32),
        ],
        compiler_params=pltpu.CompilerParams(vmem_limit_bytes=SCOPE),
        cost_estimate=cost(4 * games * heads * positions * wide, 2 * key_cache.size * 2),
        name="attend",
    )(cache_len, *in_hbm(*arrays, w_out))


def project_body(sides, *refs):
    blocks, weight = refs[:sides], refs[sides]
    mine, other, rows, total = refs[sides + 2 :]
    games = blocks[0].shape[0]
    depth, width = weight.shape
    for p in range(sides):
        rows[p * games : (p + 1) * games, :] = blocks[place_of(p, sides)][:, :depth]
    step = 512 if width % 512 == 0 else LANES
    for c in range(0, width, step):
        total[:, c : c + step] = jnp.dot(
            rows[...], weight[:, c : c + step], preferred_element_type=F32
        )
    odd = lax.axis_index("tensor") % 2
    half = width // 2
    mine[...] = total[:, columns(odd * half, half)]
    other[...] = total[:, columns((1 - odd) * half, half)].astype(BF16)


def project(sides, blocks, w_out, after):
    rows = blocks[0].shape[0] * sides
    depth, width = w_out.shape
    return pl.pallas_call(
        functools.partial(project_body, sides),
        in_specs=[VMEM] * (sides + 2),
        out_specs=[VMEM] * 2,
        out_shape=[
            jax.ShapeDtypeStruct((rows, width // 2), F32),
            jax.ShapeDtypeStruct((rows, width // 2), BF16),
        ],
        scratch_shapes=[pltpu.VMEM((rows, depth), BF16), pltpu.VMEM((rows, width), F32)],
        compiler_params=pltpu.CompilerParams(vmem_limit_bytes=SCOPE),
        cost_estimate=cost(2 * rows * depth * width, 2 * depth * width),
        name="project",
    )(*blocks, *in_vmem(w_out, after))


def add_body(mine, arrived, after, total, rounded):
    del after
    value = mine[...] + arrived[...].astype(F32)
    total[...] = value
    rounded[...] = value.astype(BF16)


def add(mine, arrived, after):
    return pl.pallas_call(
        add_body,
        in_specs=[VMEM, VMEM, VMEM],
        out_specs=[VMEM] * 2,
        out_shape=[
            jax.ShapeDtypeStruct(mine.shape, F32),
            jax.ShapeDtypeStruct(mine.shape, BF16),
        ],
        compiler_params=pltpu.CompilerParams(vmem_limit_bytes=SCOPE),
        name="add",
    )(mine, arrived, *in_vmem(after))


def stream_body(sides, depth, mine, arrived, *refs):
    blocks, out = refs[:sides], refs[-1]
    games = blocks[0].shape[0]
    width = out.shape[1]
    for p in range(sides):
        s = slice(p * games, (p + 1) * games)
        resid = blocks[place_of(p, sides)][:, depth : depth + width].astype(F32)
        out[s, :] = (resid + (mine[s] + arrived[s].astype(F32))).astype(BF16)


def stream_of(sides, depth, mine, arrived, blocks, after):
    return pl.pallas_call(
        functools.partial(stream_body, sides, depth),
        in_specs=[VMEM] * (sides + 3),
        out_specs=VMEM,
        out_shape=jax.ShapeDtypeStruct(mine.shape, BF16),
        compiler_params=pltpu.CompilerParams(vmem_limit_bytes=SCOPE),
        name="stream",
    )(mine, arrived, *blocks, *in_vmem(after))


def join_body(mine, arrived, out):
    width = mine.shape[1]
    odd = lax.axis_index("tensor") % 2
    out[:, columns(odd * width, width)] = mine[...]
    out[:, columns((1 - odd) * width, width)] = arrived[...]


def join(mine, arrived):
    rows, width = mine.shape
    return pl.pallas_call(
        join_body,
        in_specs=[VMEM] * 2,
        out_specs=VMEM,
        out_shape=jax.ShapeDtypeStruct((rows, 2 * width), BF16),
        compiler_params=pltpu.CompilerParams(vmem_limit_bytes=SCOPE),
        name="join",
    )(mine, arrived)


def prefetch_body(first, per_slot, w_gate, w_up, after, out, sems):
    del after
    copies = []
    for i in range(out.shape[0]):
        slot, block = divmod(first + i, per_slot)
        for half, weight in enumerate((w_gate, w_up)):
            copies.append(
                pltpu.make_async_copy(
                    weight.at[slot, :, pl.ds(block * FBLOCK, FBLOCK)],
                    out.at[i, half],
                    sems.at[i, half],
                )
            )
    for c in copies:
        c.start()
    for c in copies:
        c.wait()


def prefetch(first, count, w_gate, w_up, after):
    _, depth, hidden = w_gate.shape
    return pl.pallas_call(
        functools.partial(prefetch_body, first, hidden // FBLOCK),
        in_specs=[HBM, HBM, VMEM],
        out_specs=VMEM,
        out_shape=pltpu.VMEM((count, 2, depth, FBLOCK), BF16),
        scratch_shapes=[pltpu.SemaphoreType.DMA((count, 2))],
        compiler_params=pltpu.CompilerParams(vmem_limit_bytes=SCOPE),
        cost_estimate=cost(0, count * 2 * depth * FBLOCK * 2),
        name="prefetch",
    )(*in_hbm(w_gate, w_up), after)


def halves(value, gain, rows, where):
    count = value.shape[0]
    scaled = value.astype(F32) * gain.astype(F32)
    high = scaled.astype(BF16)
    rows[:count, where] = high
    rows[count:, where] = (scaled - high.astype(F32)).astype(BF16)


def fold(value):
    count = value.shape[0] // 2
    return value[:count] + value[count:]


def expand_body(sides, held, split, ring, *refs):
    chunks, refs = refs[:sides], refs[sides:]
    blocks, refs = refs[:sides], refs[sides:]
    gain, router, w_gate, w_up = refs[:4]
    ready, refs = refs[4 : 4 + len(held)], refs[4 + len(held) :]
    inner, mine, stream, rows, router2, scale, norms, raw, buffer, sems = refs
    games = blocks[0].shape[0]
    count = games * sides
    width = chunks[0].shape[1]
    features = width * sides
    slots, _, hidden = w_gate.shape
    per_slot = hidden // FBLOCK
    kept = sum(held)
    streamed = slots * per_slot - kept
    side, tensor = lax.axis_index("side"), lax.axis_index("tensor")

    def copies(step):
        index = kept + step
        return [
            pltpu.make_async_copy(
                weight.at[index // per_slot, :, columns(index % per_slot * FBLOCK, FBLOCK)],
                buffer.at[step % ring, half],
                sems.at[step % ring, half],
            )
            for half, weight in enumerate((w_gate, w_up))
        ]

    for step in range(min(ring, streamed)):
        for c in copies(step):
            c.start()

    power = jnp.zeros((count, LANES), F32)
    experts = router.shape[0]
    for k in range(sides):
        base = jnp.bitwise_xor(side, k) * width
        flip = place_of(k, sides)
        for c in range(0, width, 512):
            value = jnp.concatenate(
                [
                    chunks[k][(p ^ flip) * games : (p ^ flip) * games + games, c : c + 512]
                    for p in range(sides)
                ],
                axis=0,
            )
            wide = value.astype(F32)
            for i in range(0, 512, LANES):
                power = power + wide[:, i : i + LANES] * wide[:, i : i + LANES]
            there = columns(base + c, 512)
            stream[:, there] = value[:games]
            halves(value, gain[:, there], rows, there)
            weight = router[:, there]
            top = weight.astype(BF16).astype(F32)
            router2[:, there] = jnp.concatenate([top, weight - top], axis=0).astype(BF16)
    norm = lax.rsqrt(jnp.sum(power, axis=-1, keepdims=True) / features + 1e-05)
    norms[...] = jnp.broadcast_to(norm, norms.shape)
    products = fold(
        lax.dot_general(
            rows[...], router2[...], (((1,), (1,)), ((), ())), preferred_element_type=F32
        )
    )
    logits = (products[:, :experts] + products[:, experts:]) * norm
    route = jnp.concatenate(
        [blocks[place_of(p, sides)][:, -LANES:] for p in range(sides)], axis=0
    ).astype(F32)
    lane = lax.broadcasted_iota(jnp.int32, route.shape, 1)
    ids = [jnp.sum(jnp.where(lane == j, route, 0.0), axis=-1, keepdims=True) for j in range(2)]
    number = lax.broadcasted_iota(jnp.int32, logits.shape, 1).astype(F32)
    chosen = [
        jnp.sum(jnp.where(number == ids[j], logits, 0.0), axis=-1, keepdims=True)
        for j in range(2)
    ]
    shares = [
        1.0 / (1.0 + jnp.exp(chosen[1] - chosen[0])),
        1.0 / (1.0 + jnp.exp(chosen[0] - chosen[1])),
    ]
    for i in range(slots):
        expert = ((side * slots + i) // split).astype(F32)
        weight = jnp.where(ids[0] == expert, shares[0], 0.0) + jnp.where(
            ids[1] == expert, shares[1], 0.0
        )
        scale[i] = jnp.broadcast_to(weight, (count, FBLOCK))
    mine[...] = stream[:, columns(tensor * mine.shape[1], mine.shape[1])]

    def products(weights, turn):
        for half in range(2):
            raw[turn % 2, half] = fold(
                jnp.dot(rows[...], weights[half], preferred_element_type=F32)
            )

    def finish(index, turn):
        gate = raw[turn % 2, 0] * norms[...]
        upward = raw[turn % 2, 1] * norms[...]
        value = gate / (1.0 + jnp.exp(-gate)) * upward * scale[index // per_slot]
        where = columns(index * FBLOCK, FBLOCK)
        high = value.astype(BF16)
        inner[:count, where] = high
        inner[count:, where] = (value - high.astype(F32)).astype(BF16)

    def from_ring(step, turn, before):
        for c in copies(step):
            c.wait()
        products(buffer.at[step % ring], turn)
        if before is not None:
            finish(before, turn + 1)

        @pl.when(step + ring < streamed)
        def _():
            for c in copies(step + ring):
                c.start()

    resident = [(array, i) for array, n in zip(ready, held, strict=True) for i in range(n)]
    done, before = 0, None
    for index in range(kept + 1):
        until = streamed * (index + 1) // (kept + 1)
        if done < until:
            from_ring(jnp.int32(done), done + index, before)

            @pl.loop(done + 1, until)
            def _(step):
                from_ring(step, step + index, kept + step - 1)

            done, before = until, kept + until - 1
        if index < kept:
            array, i = resident[index]
            products(array.at[i], done + index)
            if before is not None:
                finish(before, done + index + 1)
            before = index
    finish(before, streamed + kept - 1)


def expand(sides, split, chunks, blocks, gain, router, w_gate, w_up, held, ready, own_width):
    games = blocks[0].shape[0]
    count = games * sides
    features = chunks[0].shape[1] * sides
    slots, _, hidden = w_gate.shape
    ring = 2
    arguments = [*chunks, *blocks, gain, router]
    return pl.pallas_call(
        functools.partial(expand_body, sides, held, split, ring),
        in_specs=[VMEM] * len(arguments) + [HBM] * 2 + [VMEM] * len(ready),
        out_specs=[VMEM] * 2,
        out_shape=[
            jax.ShapeDtypeStruct((2 * count, slots * hidden), BF16),
            jax.ShapeDtypeStruct((games, own_width), BF16),
        ],
        scratch_shapes=[
            pltpu.VMEM((games, features), BF16),
            pltpu.VMEM((2 * count, features), BF16),
            pltpu.VMEM((2 * router.shape[0], features), BF16),
            pltpu.VMEM((slots, count, FBLOCK), F32),
            pltpu.VMEM((count, FBLOCK), F32),
            pltpu.VMEM((2, 2, count, FBLOCK), F32),
            pltpu.VMEM((ring, 2, features, FBLOCK), BF16),
            pltpu.SemaphoreType.DMA((ring, 2)),
        ],
        compiler_params=pltpu.CompilerParams(vmem_limit_bytes=18 * 2**20),
        cost_estimate=cost(8 * count * w_gate.size, 2 * w_gate.size * 2),
        name="expand",
    )(*arguments, *in_hbm(w_gate, w_up), *in_vmem(*ready))


def contract_body(tensors, ring, block, inner, w_down, keep, send, buffer, sems):
    slots, hidden, features = w_down.shape
    tensor = lax.axis_index("tensor")
    part = features // tensors
    per_part = part // block
    steps = features // block
    half = keep.shape[0]
    deep = ring // slots

    def copies(step):
        start = jnp.bitwise_xor(tensor, step // per_part) * part + step % per_part * block
        return [
            pltpu.make_async_copy(
                w_down.at[slot, :, columns(start, block)],
                buffer.at[step % deep, slot],
                sems.at[step % deep, slot],
            )
            for slot in range(slots)
        ]

    for step in range(min(deep, steps)):
        for c in copies(step):
            c.start()

    def run(step, more):
        for c in copies(step):
            c.wait()
        total = None
        for slot in range(slots):
            value = jnp.dot(
                inner[:, slot * hidden : (slot + 1) * hidden],
                buffer[step % deep, slot],
                preferred_element_type=F32,
            )
            total = value if total is None else total + value
        total = fold(total)
        where = columns(step * block, block)
        keep[:, where] = total[:half]
        send[:, where] = total[half:].astype(BF16)
        if more:
            for c in copies(step + deep):
                c.start()

    edge = max(0, steps - deep)
    pl.loop(0, edge)(lambda step: run(step, True))
    for step in range(edge, steps):
        run(step, False)


def contract(tensors, inner, w_down):
    count = inner.shape[0] // 2
    slots, hidden, features = w_down.shape
    ring = 4 * slots
    block = 512 if features // tensors % 512 == 0 else LANES
    return pl.pallas_call(
        functools.partial(contract_body, tensors, ring, block),
        in_specs=[VMEM, HBM],
        out_specs=[VMEM, VMEM],
        out_shape=[
            jax.ShapeDtypeStruct((count // 2, features), F32),
            jax.ShapeDtypeStruct((count // 2, features), BF16),
        ],
        scratch_shapes=[
            pltpu.VMEM((ring // slots, slots, hidden, block), BF16),
            pltpu.SemaphoreType.DMA((ring // slots, slots)),
        ],
        compiler_params=pltpu.CompilerParams(vmem_limit_bytes=24 * 2**20),
        cost_estimate=cost(4 * count * w_down.size, 2 * w_down.size),
        name="contract",
    )(inner, *in_hbm(w_down))


def halve_body(keep, arrived, low, high):
    total = keep[...] + arrived[...].astype(F32)
    half = low.shape[0]
    low[...] = total[:half]
    high[...] = total[half:].astype(BF16)


def halve(keep, arrived):
    rows, width = keep.shape
    return pl.pallas_call(
        halve_body,
        in_specs=[VMEM, VMEM],
        out_specs=[VMEM, VMEM],
        out_shape=[
            jax.ShapeDtypeStruct((rows // 2, width), F32),
            jax.ShapeDtypeStruct((rows // 2, width), BF16),
        ],
        compiler_params=pltpu.CompilerParams(vmem_limit_bytes=SCOPE),
        name="halve",
    )(keep, arrived)


def deal_body(keep, arrived, *outs):
    width = outs[0].shape[1]
    for k, out in enumerate(outs):
        s = slice(k * width, (k + 1) * width)
        out[...] = (keep[:, s] + arrived[:, s].astype(F32)).astype(out.dtype)


def deal(tensors, keep, arrived):
    rows, width = keep.shape
    return pl.pallas_call(
        deal_body,
        in_specs=[VMEM, VMEM],
        out_specs=[VMEM] * tensors,
        out_shape=[
            jax.ShapeDtypeStruct((rows, width // tensors), F32 if k == 0 else BF16)
            for k in range(tensors)
        ],
        compiler_params=pltpu.CompilerParams(vmem_limit_bytes=SCOPE),
        name="deal",
    )(keep, arrived)


def last_body(*refs):
    stream, parts, out = refs[0], refs[1:-1], refs[-1]
    total = parts[0][...]
    for part in parts[1:]:
        total = total + part[...].astype(F32)
    out[...] = (stream[...].astype(F32) + total).astype(BF16)


def last(stream, parts):
    return pl.pallas_call(
        last_body,
        in_specs=[VMEM] * (1 + len(parts)),
        out_specs=VMEM,
        out_shape=jax.ShapeDtypeStruct(stream.shape, BF16),
        compiler_params=pltpu.CompilerParams(vmem_limit_bytes=SCOPE),
        name="last",
    )(stream, *parts)


def shards_kernels(
    query,
    new_key,
    new_value,
    key_cache,
    value_cache,
    cache_len,
    resid,
    w_out,
    rms_gain,
    w_router,
    route_ids,
    w_gate,
    w_up,
    w_down,
):
    sides, tensors = lax.axis_size("side"), lax.axis_size("tensor")
    features = resid.shape[1]
    depth = query.shape[1]
    extra = features // sides // 2
    slots, _, hidden = w_gate.shape
    held = [2, 1, 2]
    *blocks, w_here = attend(
        sides,
        extra,
        query,
        new_key,
        new_value,
        key_cache,
        value_cache,
        cache_len,
        resid,
        route_ids,
        w_out,
    )
    ready = [prefetch(0, held[0], w_gate, w_up, blocks[0])]
    blocks = [blocks[0]] + [swap(blocks[k], "side", sides, k) for k in range(1, sides)]
    mine, other = project(sides, blocks, w_here, ready[0])
    ready.append(prefetch(held[0], held[1], w_gate, w_up, other))
    mine, other = add(mine, swap(other, "tensor", tensors, 1), ready[1])
    ready.append(prefetch(held[0] + held[1], held[2], w_gate, w_up, other))
    step = 2
    while step < tensors // 2:
        mine, other = add(mine, swap(other, "tensor", tensors, step), ready[2])
        step *= 2
    stream = stream_of(sides, depth, mine, swap(other, "tensor", tensors, step), blocks, ready[2])
    own = join(stream, swap(stream, "tensor", tensors, 1))
    across = swap(own, "side", sides, 2)
    beside = swap(own, "side", sides, 1)
    chunks = [own, beside, across, swap(across, "side", sides, 1)]
    inner, mine = expand(
        sides,
        slots * sides // w_router.shape[1],
        chunks,
        blocks,
        rms_gain.reshape(1, features),
        w_router.T,
        w_gate,
        w_up,
        held,
        ready,
        features // tensors,
    )
    keep, send = contract(tensors, inner, w_down)
    low, high = halve(keep, swap(send, "side", sides, 1))
    dealt = deal(tensors, low, swap(high, "side", sides, 2))
    dealt = [dealt[0]] + [swap(dealt[k], "tensor", tensors, k) for k in range(1, tensors)]
    return last(mine, dealt)


def attend_local(query, new_key, new_value, key_cache, value_cache, cache_len):
    count = query.shape[0]
    positions = key_cache.shape[1]
    kv_local = key_cache.shape[2] // HEAD_DIM
    repeat = query.shape[1] // (kv_local * HEAD_DIM)
    queries = query.reshape(count, kv_local, repeat, HEAD_DIM)
    cached_keys = key_cache.reshape(count, positions, kv_local, HEAD_DIM)
    cached_values = value_cache.reshape(count, positions, kv_local, HEAD_DIM)
    scale = 1.0 / HEAD_DIM**0.5
    scores = (
        jnp.einsum("gkrd,gpkd->gkrp", queries, cached_keys, preferred_element_type=jnp.float32)
        * scale
    )
    own_key = new_key.reshape(count, kv_local, HEAD_DIM)
    own_score = (
        jnp.einsum("gkrd,gkd->gkr", queries, own_key, preferred_element_type=jnp.float32) * scale
    )
    valid = jnp.arange(positions, dtype=jnp.int32)[None, :] < cache_len[:, None]
    scores = jnp.where(valid[:, None, None, :], scores, -jnp.inf)
    highest = jnp.maximum(jnp.max(scores, axis=-1), own_score)
    cached_weight = jnp.exp(scores - highest[..., None])
    own_weight = jnp.exp(own_score - highest)
    total = jnp.sum(cached_weight, axis=-1) + own_weight
    cached_weight = (cached_weight / total[..., None]).astype(jnp.bfloat16)
    own_weight = (own_weight / total).astype(jnp.bfloat16)
    mixed = jnp.einsum(
        "gkrp,gpkd->gkrd", cached_weight, cached_values, preferred_element_type=jnp.float32
    )
    own_value = new_value.reshape(count, kv_local, 1, HEAD_DIM).astype(jnp.float32)
    mixed = mixed + own_weight.astype(jnp.float32)[..., None] * own_value
    return mixed.reshape(count, kv_local * repeat * HEAD_DIM).astype(jnp.bfloat16)


def shards(
    query,
    new_key,
    new_value,
    key_cache,
    value_cache,
    cache_len,
    resid,
    w_out,
    rms_gain,
    w_router,
    route_ids,
    w_gate,
    w_up,
    w_down,
):
    attended = attend_local(query, new_key, new_value, key_cache, value_cache, cache_len)
    column_part = jnp.dot(
        lax.all_gather(attended, "side", axis=0, tiled=True),
        w_out,
        preferred_element_type=jnp.float32,
    )
    partial_out = lax.all_to_all(column_part, "side", split_axis=0, concat_axis=1, tiled=True)
    attn_out = lax.psum(partial_out, "tensor")
    stream = (resid.astype(jnp.float32) + attn_out).astype(jnp.bfloat16)
    wide = stream.astype(jnp.float32)
    power = jnp.mean(wide * wide, axis=-1, keepdims=True)
    normed = wide * lax.rsqrt(power + 1e-05) * rms_gain.astype(jnp.float32)
    logits = jnp.dot(normed, w_router, precision=lax.Precision.HIGHEST)
    experts = w_router.shape[1]
    picked = route_ids[:, :, None] == jnp.arange(experts, dtype=jnp.int32)[None, None, :]
    chosen = jnp.sum(jnp.where(picked, logits[:, None, :], 0.0), axis=-1)
    first = 1.0 / (1.0 + jnp.exp(chosen[:, 1] - chosen[:, 0]))
    second = 1.0 / (1.0 + jnp.exp(chosen[:, 0] - chosen[:, 1]))
    pair = jnp.stack([first, second], axis=1)
    weight = jnp.sum(jnp.where(picked, pair[:, :, None], 0.0), axis=1)
    rows = normed.astype(jnp.bfloat16)
    member = jnp.any(picked, axis=1).astype(jnp.int32)
    order_rank = jnp.cumsum(member, axis=0) - member
    capacity = CAP
    placing = (order_rank.T[:, None, :] == jnp.arange(capacity, dtype=jnp.int32)[None, :, None]) & (
        member.T[:, None, :] == 1
    )
    packed = jnp.einsum(
        "ecg,gd->ecd", placing.astype(jnp.bfloat16), rows, preferred_element_type=jnp.float32
    ).astype(jnp.bfloat16)
    side_count = lax.axis_size("side")
    slot_total = max(side_count, experts)
    split_count = slot_total // experts
    slot_local = slot_total // side_count
    width = rows.shape[1]
    packed = jnp.repeat(packed, split_count, axis=0).reshape(
        side_count, slot_local, capacity, width
    )
    arrived = lax.all_to_all(packed, "side", split_axis=0, concat_axis=0, tiled=True)
    gate = jnp.einsum("sjcd,jdf->sjcf", arrived, w_gate, preferred_element_type=jnp.float32)
    upward = jnp.einsum("sjcd,jdf->sjcf", arrived, w_up, preferred_element_type=jnp.float32)
    inner = (jax.nn.silu(gate) * upward).astype(jnp.bfloat16)
    expert_part = jnp.einsum("sjcf,jfd->sjcd", inner, w_down, preferred_element_type=jnp.float32)
    scaled_place = placing.astype(jnp.float32) * weight.T[:, None, :]
    returned = lax.all_to_all(expert_part, "side", split_axis=0, concat_axis=0, tiled=True)
    features = returned.shape[3]
    merged = jnp.sum(returned.reshape(experts, split_count, capacity, features), axis=1)
    moe = lax.psum_scatter(
        jnp.einsum("ecg,ecf->gf", scaled_place, merged, precision=lax.Precision.HIGHEST),
        "tensor",
        scatter_dimension=1,
        tiled=True,
    )
    columns = moe.shape[1]
    local_stream = lax.dynamic_slice_in_dim(wide, lax.axis_index("tensor") * columns, columns, 1)
    return (local_stream + moe).astype(jnp.bfloat16)


def tiles(mesh, sides=4):
    side, tensor = mesh.shape["side"], mesh.shape["tensor"]
    return side == sides and tensor >= 4 and tensor & (tensor - 1) == 0


def solution(mesh):
    return jax.shard_map(
        shards_kernels if tiles(mesh) else shards,
        mesh=mesh,
        in_specs=(
            P(("groups", "side"), "tensor"),
            P(("groups", "side"), "tensor"),
            P(("groups", "side"), "tensor"),
            P(("groups", "side"), None, "tensor"),
            P(("groups", "side"), None, "tensor"),
            P(("groups", "side")),
            P(("groups", "side"), None),
            P("tensor", "side"),
            P(),
            P(),
            P(("groups", "side"), None),
            P("side", None, "tensor"),
            P("side", None, "tensor"),
            P("side", "tensor", None),
        ),
        out_specs=P(("groups", "side"), "tensor"),
        check_vma=False,
    )
```

time: 121 us -> 98.8 us (0.82)
  local copies, waits for them, and re-layouts: 11.6 us -> 0.68 us
  waiting for transfers between devices: 28.3 us -> 21.5 us
  starting transfers between devices: 19.6 us -> 17.3 us
  Pallas kernels: 60.7 us -> 59 us
    unnamed x20 -> x6, local copies, waits for them, and re-layouts: 10.9 us -> 0.67 us
    ppermute x17 -> x14, waiting for transfers between devices: 28.3 us -> 21.5 us  [swap(): return lax.ppermute(value, axis, [(i, i ^ mask) for i in range(count)])]
    ppermute x17 -> x14, starting transfers between devices: 19.6 us -> 17.3 us  [swap(): return lax.ppermute(value, axis, [(i, i ^ mask) for i in range(count)])]
    pallas_call x5 -> x9, Pallas kernels: 43.1 us -> 41.4 us  [the longest x1 23.6 us: expand(): pl.pallas_call(functools.partial(expand_body, sides, held, split, ring),...]
  transfers between devices with their start and end apart: 17 -> 14, of which waited for: 12 -> 8; matrix products, arithmetic and copies ran while one was open for 1% -> 0% of each run, Pallas kernels for 0% -> 13%
where the time goes in v2:
time: 98.8 us; the launch traced here: 98.6 us
  Pallas kernels  59 us (60%)
  waiting for transfers between devices  21.5 us (22%)
  starting transfers between devices  17.3 us (18%)
    pallas_call x1, Pallas kernels, expand(): pl.pallas_call(functools.partial(expand_body, sides, held, split, ring),...  23.6 us
    ppermute x14, waiting for transfers between devices, swap(): return lax.ppermute(value, axis, [(i, i ^ mask) for i in range(count)])  21.5 us
    ppermute x14, starting transfers between devices, swap(): return lax.ppermute(value, axis, [(i, i ^ mask) for i in range(count)])  17.3 us
    pallas_call x1, Pallas kernels, contract(): pl.pallas_call(functools.partial(contract_body, tensors, ring, block), in...  16.8 us
    pallas_call x3, Pallas kernels, prefetch(): pl.pallas_call(functools.partial(prefetch_body, first, hidden // FBLOCK),...  12.3 us
    pallas_call x1, Pallas kernels, attend(): pl.pallas_call(functools.partial(attend_body, sides, block), in_specs=[SM...  4.41 us
  transfers between devices with their start and end apart: 14, of which 8 were waited for; matrix products, arithmetic and copies ran while one was open for 0% of the time, Pallas kernels for 13%

profile of v2, /device:TPU:0, one launch (start us, length us, event | category | flops | bytes accessed | tf_op | source)
XLA Modules:
  0.0 98.6 jit_solution(14716717558571178490)
XLA Ops:
  0.0 0.0 copy-start.1
  0.0 0.7 copy-done.1
  0.7 4.4 %attend.1 = (bf16[16,2432]{1,0:T(8,128)(2,1)S(1)}, bf16[16,2432]{1,0:T(8,128)(2,1)S(1)}, bf16[16,2432]{1,0:T(8,128)(2,1)S(1)}, bf16[16,2432]{1,0:T(8,128)(2,1)S(1)}, bf16[1536,1536]{1,0:T(8,128)(2,1)S(1)}) custom-call(s32[16]{0:T(128)S(1)} %copy-done.1, bf16[16,1536]{1,0:T(8,128)(2,1)} %query_at.1, bf16[16,256]{1,0:T(8,128)(2,1)} %new_key_at.1, ...), custom_call_target="tpu_custom_call" | custom-call | flops 67108864 | bytes 4194304 | tf_op jit(solution)/shard_map/attend/pallas_call | solution.py:177
  5.1 0.5 collective-permute-start
  5.6 2.6 %collective-permute-start.1 = (bf16[16,2432]{1,0:T(8,128)(2,1)S(1)}, bf16[16,2432]{1,0:T(8,128)(2,1)S(1)}, u32[]{:S(2)}, u32[]{:S(2)}) collective-permute-start(bf16[16,2432]{1,0:T(8,128)(2,1)S(1)} %get-tuple-element.26), channel_id=1, source_target_pairs={{0,8},{4,12},{8,0},{12,4},{1,9},{5,13},{9,1},{13,5},{2,10},{6,14},... | collective-permute-start | bytes 233480 | tf_op jit(solution)/shard_map/ppermute | solution.py:34
  8.2 0.1 collective-permute-start.2
  8.2 4.7 %prefetch.3.refs_5_.refs_12_ = bf16[2,2,6144,256]{3,2,1,0:T(8,128)(2,1)S(1)} custom-call(bf16[2,6144,2048]{2,1,0:T(8,128)(2,1)} %refs_10_.1, bf16[2,6144,2048]{2,1,0:T(8,128)(2,1)} %refs_11_.1, bf16[16,2432]{1,0:T(8,128)(2,1)S(1)} %get-tuple-element.24.after.refs_0_.refs_4_), custom_call_target="tpu_custom_call" | custom-call | bytes 12582912 | tf_op jit(solution)/shard_map/prefetch/pallas_call | solution.py:316
  13.0 0.0 collective-permute-done.refs_1_.refs_5_
  13.0 0.0 collective-permute-done.1.refs_2_.refs_6_
  13.0 0.0 collective-permute-done.2.refs_3_.refs_7_
  13.0 1.0 project.1
  14.0 1.9 %collective-permute-start.3 = (bf16[64,768]{1,0:T(8,128)(2,1)S(1)}, bf16[64,768]{1,0:T(8,128)(2,1)S(1)}, u32[]{:S(2)}, u32[]{:S(2)}) collective-permute-start(bf16[64,768]{1,0:T(8,128)(2,1)S(1)} %get-tuple-element.30.after), channel_id=1, source_target_pairs={{0,1},{1,0},{2,3},{3,2},{4,5},{5,4},{6,7},{7,6},{8,9},{9,8},{10,11... | collective-permute-start | bytes 294920 | tf_op jit(solution)/shard_map/ppermute | solution.py:34
  15.9 2.9 %prefetch.4.after.refs_13_ = bf16[1,2,6144,256]{3,2,1,0:T(8,128)(2,1)S(1)} custom-call(bf16[2,6144,2048]{2,1,0:T(8,128)(2,1)} %refs_10_.1, bf16[2,6144,2048]{2,1,0:T(8,128)(2,1)} %refs_11_.1, bf16[64,768]{1,0:T(8,128)(2,1)S(1)} %get-tuple-element.30.after), custom_call_target="tpu_custom_call" | custom-call | bytes 6291456 | tf_op jit(solution)/shard_map/prefetch/pallas_call | solution.py:316
  18.7 0.4 collective-permute-done.3.arrived
  19.2 2.8 %collective-permute-start.4 = (bf16[64,768]{1,0:T(8,128)(2,1)S(1)}, bf16[64,768]{1,0:T(8,128)(2,1)S(1)}, u32[]{:S(2)}, u32[]{:S(2)}) collective-permute-start(bf16[64,768]{1,0:T(8,128)(2,1)S(1)} %get-tuple-element.32.after), channel_id=1, source_target_pairs={{0,2},{1,3},{2,0},{3,1},{4,6},{5,7},{6,4},{7,5},{8,10},{9,11},{10,... | collective-permute-start | bytes 294920 | tf_op jit(solution)/shard_map/ppermute | solution.py:34
  22.0 4.7 %prefetch.5.refs_4_.refs_14_ = bf16[2,2,6144,256]{3,2,1,0:T(8,128)(2,1)S(1)} custom-call(bf16[2,6144,2048]{2,1,0:T(8,128)(2,1)} %refs_10_.1, bf16[2,6144,2048]{2,1,0:T(8,128)(2,1)} %refs_11_.1, bf16[64,768]{1,0:T(8,128)(2,1)S(1)} %get-tuple-element.32.after), custom_call_target="tpu_custom_call" | custom-call | bytes 12582912 | tf_op jit(solution)/shard_map/prefetch/pallas_call | solution.py:316
  26.7 0.0 copy-start.2
  26.8 0.0 copy-start
  26.8 0.0 collective-permute-done.4.arrived
  26.8 1.6 %collective-permute-start.5 = (bf16[64,768]{1,0:T(8,128)(2,1)S(1)}, bf16[64,768]{1,0:T(8,128)(2,1)S(1)}, u32[]{:S(2)}, u32[]{:S(2)}) collective-permute-start(bf16[64,768]{1,0:T(8,128)(2,1)S(1)} %stream.1.mine), channel_id=1, source_target_pairs={{0,1},{1,0},{2,3},{3,2},{4,5},{5,4},{6,7},{7,6},{8,9},{9,8},{10,11... | collective-permute-start | bytes 294920 | tf_op jit(solution)/shard_map/ppermute | solution.py:34
  28.5 3.0 %collective-permute-done.5.arrived = bf16[64,768]{1,0:T(8,128)(2,1)S(1)} collective-permute-done((bf16[64,768]{1,0:T(8,128)(2,1)S(1)}, bf16[64,768]{1,0:T(8,128)(2,1)S(1)}, u32[]{:S(2)}, u32[]{:S(2)}) %collective-permute-start.5) | collective-permute-done | bytes 98336 | tf_op jit(solution)/shard_map/ppermute | solution.py:34
  31.5 1.6 %collective-permute-start.7 = (bf16[64,1536]{1,0:T(8,128)(2,1)S(1)}, bf16[64,1536]{1,0:T(8,128)(2,1)S(1)}, u32[]{:S(2)}, u32[]{:S(2)}) collective-permute-start(bf16[64,1536]{1,0:T(8,128)(2,1)S(1)} %join.1.refs_0_), channel_id=1, source_target_pairs={{0,8},{4,12},{8,0},{12,4},{1,9},{5,13},{9,1},{13,5},{2,10},{6,14},... | collective-permute-start | bytes 589832 | tf_op jit(solution)/shard_map/ppermute | solution.py:34
  33.1 0.0 collective-permute-start.6
  33.1 4.2 %collective-permute-done.7.refs_2_ = bf16[64,1536]{1,0:T(8,128)(2,1)S(1)} collective-permute-done((bf16[64,1536]{1,0:T(8,128)(2,1)S(1)}, bf16[64,1536]{1,0:T(8,128)(2,1)S(1)}, u32[]{:S(2)}, u32[]{:S(2)}) %collective-permute-start.7) | collective-permute-done | bytes 196640 | tf_op jit(solution)/shard_map/ppermute | solution.py:34
  37.3 0.0 collective-permute-start.8
  37.3 0.0 copy-done.2
  37.3 0.0 collective-permute-done.6.refs_1_
  37.3 1.4 %collective-permute-done.8.refs_3_ = bf16[64,1536]{1,0:T(8,128)(2,1)S(1)} collective-permute-done((bf16[64,1536]{1,0:T(8,128)(2,1)S(1)}, bf16[64,1536]{1,0:T(8,128)(2,1)S(1)}, u32[]{:S(2)}, u32[]{:S(2)}) %collective-permute-start.8) | collective-permute-done | bytes 196640 | tf_op jit(solution)/shard_map/ppermute | solution.py:34
  38.7 0.0 copy-done
  38.7 23.6 %expand.1 = (bf16[128,4096]{1,0:T(8,128)(2,1)S(1)}, bf16[16,1536]{1,0:T(8,128)(2,1)S(1)}) custom-call(bf16[64,1536]{1,0:T(8,128)(2,1)S(1)} %join.1.refs_0_, bf16[64,1536]{1,0:T(8,128)(2,1)S(1)} %collective-permute-done.6.refs_1_, bf16[64,1536]{1,0:T(8,128)(2,1)S(1)} %collective-permute-done.7.refs_2_, bf16[64,1536]{1,0:T(8,128)(2,1)S(1)} %collective-permute-done.8.refs_3_, ...), custom_call_target="tpu_custom_call" | custom-call | flops 12884901888 | bytes 100663296 | tf_op jit(solution)/shard_map/expand/pallas_call | solution.py:479
  62.3 16.8 %contract.1 = (f32[32,6144]{1,0:T(8,128)S(1)}, bf16[32,6144]{1,0:T(8,128)(2,1)S(1)}) custom-call(bf16[128,4096]{1,0:T(8,128)(2,1)S(1)} %get-tuple-element.34.inner, bf16[2,2048,6144]{2,1,0:T(8,128)(2,1)} %w_down.1), custom_call_target="tpu_custom_call" | custom-call | flops 6442450944 | bytes 50331648 | tf_op jit(solution)/shard_map/contract/pallas_call | solution.py:557
  79.1 0.2 collective-permute-start.9
  79.4 1.6 %collective-permute-done.9.arrived = bf16[32,6144]{1,0:T(8,128)(2,1)S(1)} collective-permute-done((bf16[32,6144]{1,0:T(8,128)(2,1)S(1)}, bf16[32,6144]{1,0:T(8,128)(2,1)S(1)}, u32[]{:S(2)}, u32[]{:S(2)}) %collective-permute-start.9) | collective-permute-done | bytes 393248 | tf_op jit(solution)/shard_map/ppermute | solution.py:34
  80.9 0.1 halve.1
  81.0 1.6 %collective-permute-start.10 = (bf16[16,6144]{1,0:T(8,128)(2,1)S(1)}, bf16[16,6144]{1,0:T(8,128)(2,1)S(1)}, u32[]{:S(2)}, u32[]{:S(2)}) collective-permute-start(bf16[16,6144]{1,0:T(8,128)(2,1)S(1)} %get-tuple-element.38), channel_id=1, source_target_pairs={{0,8},{4,12},{8,0},{12,4},{1,9},{5,13},{9,1},{13,5},{2,10},{6,14},... | collective-permute-start | bytes 589832 | tf_op jit(solution)/shard_map/ppermute | solution.py:34
  82.6 5.4 %collective-permute-done.10.arrived = bf16[16,6144]{1,0:T(8,128)(2,1)S(1)} collective-permute-done((bf16[16,6144]{1,0:T(8,128)(2,1)S(1)}, bf16[16,6144]{1,0:T(8,128)(2,1)S(1)}, u32[]{:S(2)}, u32[]{:S(2)}) %collective-permute-start.10) | collective-permute-done | bytes 196640 | tf_op jit(solution)/shard_map/ppermute | solution.py:34
  88.1 1.6 %collective-permute-start.11 = (bf16[16,1536]{1,0:T(8,128)(2,1)S(1)}, bf16[16,1536]{1,0:T(8,128)(2,1)S(1)}, u32[]{:S(2)}, u32[]{:S(2)}) collective-permute-start(bf16[16,1536]{1,0:T(8,128)(2,1)S(1)} %get-tuple-element.40), channel_id=1, source_target_pairs={{0,1},{1,0},{2,3},{3,2},{4,5},{5,4},{6,7},{7,6},{8,9},{9,8},{10,11... | collective-permute-start | bytes 147464 | tf_op jit(solution)/shard_map/ppermute | solution.py:34
  89.7 2.4 %collective-permute-start.12 = (bf16[16,1536]{1,0:T(8,128)(2,1)S(1)}, bf16[16,1536]{1,0:T(8,128)(2,1)S(1)}, u32[]{:S(2)}, u32[]{:S(2)}) collective-permute-start(bf16[16,1536]{1,0:T(8,128)(2,1)S(1)} %get-tuple-element.41), channel_id=1, source_target_pairs={{0,2},{1,3},{2,0},{3,1},{4,6},{5,7},{6,4},{7,5},{8,10},{9,11},{10,... | collective-permute-start | bytes 147464 | tf_op jit(solution)/shard_map/ppermute | solution.py:34
  92.1 0.5 collective-permute-start.13
  92.5 0.0 collective-permute-done.11.refs_2_
  92.5 2.6 %collective-permute-done.12.refs_3_ = bf16[16,1536]{1,0:T(8,128)(2,1)S(1)} collective-permute-done((bf16[16,1536]{1,0:T(8,128)(2,1)S(1)}, bf16[16,1536]{1,0:T(8,128)(2,1)S(1)}, u32[]{:S(2)}, u32[]{:S(2)}) %collective-permute-start.12) | collective-permute-done | bytes 49184 | tf_op jit(solution)/shard_map/ppermute | solution.py:34
  95.1 2.8 %collective-permute-done.13.refs_4_ = bf16[16,1536]{1,0:T(8,128)(2,1)S(1)} collective-permute-done((bf16[16,1536]{1,0:T(8,128)(2,1)S(1)}, bf16[16,1536]{1,0:T(8,128)(2,1)S(1)}, u32[]{:S(2)}, u32[]{:S(2)}) %collective-permute-start.13) | collective-permute-done | bytes 49184 | tf_op jit(solution)/shard_map/ppermute | solution.py:34
  97.9 0.7 last.1
  (5 shorter events, 0.1 us)
Async XLA Ops:
  0.0 0.7 copy-start.1
  5.1 7.9 %collective-permute-start = (bf16[16,2432]{1,0:T(8,128)(2,1)S(1)}, bf16[16,2432]{1,0:T(8,128)(2,1)S(1)}, u32[]{:S(2)}, u32[]{:S(2)}) collective-permute-start(bf16[16,2432]{1,0:T(8,128)(2,1)S(1)} %get-tuple-element.25), channel_id=1, source_target_pairs={{0,4},{4,0},{8,12},{12,8},{1,5},{5,1},{9,13},{13,9},{2,6},{6,2},{1... | collective-permute-start | bytes 233480 | tf_op jit(solution)/shard_map/ppermute | solution.py:34
  5.6 7.4 %collective-permute-start.1 = (bf16[16,2432]{1,0:T(8,128)(2,1)S(1)}, bf16[16,2432]{1,0:T(8,128)(2,1)S(1)}, u32[]{:S(2)}, u32[]{:S(2)}) collective-permute-start(bf16[16,2432]{1,0:T(8,128)(2,1)S(1)} %get-tuple-element.26), channel_id=1, source_target_pairs={{0,8},{4,12},{8,0},{12,4},{1,9},{5,13},{9,1},{13,5},{2,10},{6,14},... | collective-permute-start | bytes 233480 | tf_op jit(solution)/shard_map/ppermute | solution.py:34
  8.2 4.8 %collective-permute-start.2 = (bf16[16,2432]{1,0:T(8,128)(2,1)S(1)}, bf16[16,2432]{1,0:T(8,128)(2,1)S(1)}, u32[]{:S(2)}, u32[]{:S(2)}) collective-permute-start(bf16[16,2432]{1,0:T(8,128)(2,1)S(1)} %get-tuple-element.27), channel_id=1, source_target_pairs={{0,12},{4,8},{8,4},{12,0},{1,13},{5,9},{9,5},{13,1},{2,14},{6,10},... | collective-permute-start | bytes 233480 | tf_op jit(solution)/shard_map/ppermute | solution.py:34
  14.0 5.2 %collective-permute-start.3 = (bf16[64,768]{1,0:T(8,128)(2,1)S(1)}, bf16[64,768]{1,0:T(8,128)(2,1)S(1)}, u32[]{:S(2)}, u32[]{:S(2)}) collective-permute-start(bf16[64,768]{1,0:T(8,128)(2,1)S(1)} %get-tuple-element.30.after), channel_id=1, source_target_pairs={{0,1},{1,0},{2,3},{3,2},{4,5},{5,4},{6,7},{7,6},{8,9},{9,8},{10,11... | collective-permute-start | bytes 294920 | tf_op jit(solution)/shard_map/ppermute | solution.py:34
  19.2 7.6 %collective-permute-start.4 = (bf16[64,768]{1,0:T(8,128)(2,1)S(1)}, bf16[64,768]{1,0:T(8,128)(2,1)S(1)}, u32[]{:S(2)}, u32[]{:S(2)}) collective-permute-start(bf16[64,768]{1,0:T(8,128)(2,1)S(1)} %get-tuple-element.32.after), channel_id=1, source_target_pairs={{0,2},{1,3},{2,0},{3,1},{4,6},{5,7},{6,4},{7,5},{8,10},{9,11},{10,... | collective-permute-start | bytes 294920 | tf_op jit(solution)/shard_map/ppermute | solution.py:34
  26.7 10.5 %copy-start.2 = (bf16[6144]{0:T(1024)(128)(2,1)S(1)}, bf16[6144]{0:T(1024)(128)(2,1)}, u32[]{:S(2)}) copy-start(bf16[6144]{0:T(1024)(128)(2,1)} %param.22) | copy-start | bytes 36868
  26.8 12.0 %copy-start = (f32[6144,8]{0,1:T(8,128)S(1)}, f32[6144,8]{0,1:T(8,128)}, u32[]{:S(2)}) copy-start(f32[6144,8]{0,1:T(8,128)} %param.23) | copy-start | bytes 589828
  26.8 4.7 %collective-permute-start.5 = (bf16[64,768]{1,0:T(8,128)(2,1)S(1)}, bf16[64,768]{1,0:T(8,128)(2,1)S(1)}, u32[]{:S(2)}, u32[]{:S(2)}) collective-permute-start(bf16[64,768]{1,0:T(8,128)(2,1)S(1)} %stream.1.mine), channel_id=1, source_target_pairs={{0,1},{1,0},{2,3},{3,2},{4,5},{5,4},{6,7},{7,6},{8,9},{9,8},{10,11... | collective-permute-start | bytes 294920 | tf_op jit(solution)/shard_map/ppermute | solution.py:34
  31.5 5.7 %collective-permute-start.7 = (bf16[64,1536]{1,0:T(8,128)(2,1)S(1)}, bf16[64,1536]{1,0:T(8,128)(2,1)S(1)}, u32[]{:S(2)}, u32[]{:S(2)}) collective-permute-start(bf16[64,1536]{1,0:T(8,128)(2,1)S(1)} %join.1.refs_0_), channel_id=1, source_target_pairs={{0,8},{4,12},{8,0},{12,4},{1,9},{5,13},{9,1},{13,5},{2,10},{6,14},... | collective-permute-start | bytes 589832 | tf_op jit(solution)/shard_map/ppermute | solution.py:34
  33.1 4.2 %collective-permute-start.6 = (bf16[64,1536]{1,0:T(8,128)(2,1)S(1)}, bf16[64,1536]{1,0:T(8,128)(2,1)S(1)}, u32[]{:S(2)}, u32[]{:S(2)}) collective-permute-start(bf16[64,1536]{1,0:T(8,128)(2,1)S(1)} %join.1.refs_0_), channel_id=1, source_target_pairs={{0,4},{4,0},{8,12},{12,8},{1,5},{5,1},{9,13},{13,9},{2,6},{6,2},{1... | collective-permute-start | bytes 589832 | tf_op jit(solution)/shard_map/ppermute | solution.py:34
  37.3 1.4 %collective-permute-start.8 = (bf16[64,1536]{1,0:T(8,128)(2,1)S(1)}, bf16[64,1536]{1,0:T(8,128)(2,1)S(1)}, u32[]{:S(2)}, u32[]{:S(2)}) collective-permute-start(bf16[64,1536]{1,0:T(8,128)(2,1)S(1)} %collective-permute-done.7.refs_2_), channel_id=1, source_target_pairs={{0,4},{4,0},{8,12},{12,8},{1,5},{5,1},{9,13},{13,9},{2,6},{6,2},{1... | collective-permute-start | bytes 589832 | tf_op jit(solution)/shard_map/ppermute | solution.py:34
  79.1 1.8 %collective-permute-start.9 = (bf16[32,6144]{1,0:T(8,128)(2,1)S(1)}, bf16[32,6144]{1,0:T(8,128)(2,1)S(1)}, u32[]{:S(2)}, u32[]{:S(2)}) collective-permute-start(bf16[32,6144]{1,0:T(8,128)(2,1)S(1)} %get-tuple-element.36), channel_id=1, source_target_pairs={{0,4},{4,0},{8,12},{12,8},{1,5},{5,1},{9,13},{13,9},{2,6},{6,2},{1... | collective-permute-start | bytes 1179656 | tf_op jit(solution)/shard_map/ppermute | solution.py:34
  81.0 7.0 %collective-permute-start.10 = (bf16[16,6144]{1,0:T(8,128)(2,1)S(1)}, bf16[16,6144]{1,0:T(8,128)(2,1)S(1)}, u32[]{:S(2)}, u32[]{:S(2)}) collective-permute-start(bf16[16,6144]{1,0:T(8,128)(2,1)S(1)} %get-tuple-element.38), channel_id=1, source_target_pairs={{0,8},{4,12},{8,0},{12,4},{1,9},{5,13},{9,1},{13,5},{2,10},{6,14},... | collective-permute-start | bytes 589832 | tf_op jit(solution)/shard_map/ppermute | solution.py:34
  88.1 4.5 %collective-permute-start.11 = (bf16[16,1536]{1,0:T(8,128)(2,1)S(1)}, bf16[16,1536]{1,0:T(8,128)(2,1)S(1)}, u32[]{:S(2)}, u32[]{:S(2)}) collective-permute-start(bf16[16,1536]{1,0:T(8,128)(2,1)S(1)} %get-tuple-element.40), channel_id=1, source_target_pairs={{0,1},{1,0},{2,3},{3,2},{4,5},{5,4},{6,7},{7,6},{8,9},{9,8},{10,11... | collective-permute-start | bytes 147464 | tf_op jit(solution)/shard_map/ppermute | solution.py:34
  89.7 5.4 %collective-permute-start.12 = (bf16[16,1536]{1,0:T(8,128)(2,1)S(1)}, bf16[16,1536]{1,0:T(8,128)(2,1)S(1)}, u32[]{:S(2)}, u32[]{:S(2)}) collective-permute-start(bf16[16,1536]{1,0:T(8,128)(2,1)S(1)} %get-tuple-element.41), channel_id=1, source_target_pairs={{0,2},{1,3},{2,0},{3,1},{4,6},{5,7},{6,4},{7,5},{8,10},{9,11},{10,... | collective-permute-start | bytes 147464 | tf_op jit(solution)/shard_map/ppermute | solution.py:34
  92.1 5.9 %collective-permute-start.13 = (bf16[16,1536]{1,0:T(8,128)(2,1)S(1)}, bf16[16,1536]{1,0:T(8,128)(2,1)S(1)}, u32[]{:S(2)}, u32[]{:S(2)}) collective-permute-start(bf16[16,1536]{1,0:T(8,128)(2,1)S(1)} %get-tuple-element.42), channel_id=1, source_target_pairs={{0,3},{1,2},{2,1},{3,0},{4,7},{5,6},{6,5},{7,4},{8,11},{9,10},{10,... | collective-permute-start | bytes 147464 | tf_op jit(solution)/shard_map/ppermute | solution.py:34

commit v3 on v2

--- a/solution.py
+++ b/solution.py
@@ -16,7 +16,6 @@
 F32 = jnp.float32
 SCOPE = 8 * 2**20
 VMEM = pl.BlockSpec(memory_space=pltpu.VMEM)
-SMEM = pl.BlockSpec(memory_space=pltpu.SMEM)
 ANY = pl.BlockSpec(memory_space=pl.ANY)
 HBM = pl.BlockSpec(memory_space=pltpu.HBM)
 
@@ -49,7 +48,7 @@
 def attend_body(
     sides,
     block,
-    length,
+    length_at,
     query_at,
     new_key_at,
     new_value_at,
@@ -62,7 +61,7 @@
 ):
     outs, w_out, rest = rest[:sides], rest[sides], rest[sides + 1 :]
     query, new_key, new_value, keys, values, resid, route, sems, rest = *rest[:8], rest[8:]
-    spread, mixed, score, own_score, key32, value32 = rest
+    length, spread, mixed, score, own_score, key32, value32 = rest
     games, width = query.shape
     heads = width // HEAD_DIM
     padded = spread.shape[1]
@@ -94,10 +93,11 @@
         for source, target, sem in ((keys_at, keys, 5), (values_at, values, 5 + steps))
     ]
     after = copy(w_out_at, w_out, 5 + 2 * steps)
-    for c in small[:4] + caches[0] + caches[1] + small[4:] + [after]:
+    lengths = copy(length_at, length, 6 + 2 * steps)
+    for c in [lengths] + small[:4] + caches[0] + caches[1] + small[4:] + [after]:
         c.start()
     spread[...] = jnp.zeros_like(spread)
-    for c in small[:4]:
+    for c in [lengths] + small[:4]:
         c.wait()
     for h in range(heads):
         lane = h // repeat * HEAD_DIM
@@ -176,12 +176,13 @@
     arrays = [query, new_key, new_value, key_cache, value_cache, resid, routes]
     return pl.pallas_call(
         functools.partial(attend_body, sides, block),
-        in_specs=[SMEM] + [HBM] * (len(arrays) + 1),
+        in_specs=[HBM] * (len(arrays) + 2),
         out_specs=[VMEM] * (sides + 1),
         out_shape=[out] * sides + [pltpu.VMEM(w_out.shape, BF16)],
         scratch_shapes=[pltpu.VMEM(a.shape, a.dtype) for a in arrays]
         + [
-            pltpu.SemaphoreType.DMA((6 + 2 * (games // block),)),
+            pltpu.SemaphoreType.DMA((7 + 2 * (games // block),)),
+            pltpu.SMEM(cache_len.shape, jnp.int32),
             pltpu.VMEM((games, heads, wide), F32),
             pltpu.VMEM((games, heads, wide), F32),
             pltpu.VMEM((games * heads, positions), F32),
@@ -192,7 +193,7 @@
         compiler_params=pltpu.CompilerParams(vmem_limit_bytes=SCOPE),
         cost_estimate=cost(4 * games * heads * positions * wide, 2 * key_cache.size * 2),
         name="attend",
-    )(cache_len, *in_hbm(*arrays, w_out))
+    )(*in_hbm(cache_len, *arrays, w_out))
 
 
 def project_body(sides, *refs):
@@ -273,35 +274,45 @@
     )(mine, arrived, *blocks, *in_vmem(after))
 
 
-def join_body(mine, arrived, out):
+def join_body(mine, arrived, after, out):
+    del after
     width = mine.shape[1]
     odd = lax.axis_index("tensor") % 2
     out[:, columns(odd * width, width)] = mine[...]
     out[:, columns((1 - odd) * width, width)] = arrived[...]
 
 
-def join(mine, arrived):
+def join(mine, arrived, after):
     rows, width = mine.shape
     return pl.pallas_call(
         join_body,
-        in_specs=[VMEM] * 2,
+        in_specs=[VMEM] * 3,
         out_specs=VMEM,
         out_shape=jax.ShapeDtypeStruct((rows, 2 * width), BF16),
         compiler_params=pltpu.CompilerParams(vmem_limit_bytes=SCOPE),
         name="join",
-    )(mine, arrived)
-
-
-def prefetch_body(first, per_slot, w_gate, w_up, after, out, sems):
+    )(mine, arrived, *in_vmem(after))
+
+
+def prefetch_body(first, count, per_slot, block, w_gate, w_up, w_down, after, *refs):
     del after
+    outs, sems = refs[:-1], refs[-1]
     copies = []
-    for i in range(out.shape[0]):
+    if block:
+        start = lax.axis_index("tensor") * (w_down.shape[2] // lax.axis_size("tensor"))
+        for i in range(w_down.shape[0]):
+            copies.append(
+                pltpu.make_async_copy(
+                    w_down.at[i, :, columns(start, block)], outs[count].at[i], sems.at[count, i]
+                )
+            )
+    for i, out in enumerate(outs[:count]):
         slot, block = divmod(first + i, per_slot)
         for half, weight in enumerate((w_gate, w_up)):
             copies.append(
                 pltpu.make_async_copy(
                     weight.at[slot, :, pl.ds(block * FBLOCK, FBLOCK)],
-                    out.at[i, half],
+                    out.at[half],
                     sems.at[i, half],
                 )
             )
@@ -311,18 +322,22 @@
         c.wait()
 
 
-def prefetch(first, count, w_gate, w_up, after):
-    _, depth, hidden = w_gate.shape
-    return pl.pallas_call(
-        functools.partial(prefetch_body, first, hidden // FBLOCK),
-        in_specs=[HBM, HBM, VMEM],
-        out_specs=VMEM,
-        out_shape=pltpu.VMEM((count, 2, depth, FBLOCK), BF16),
-        scratch_shapes=[pltpu.SemaphoreType.DMA((count, 2))],
-        compiler_params=pltpu.CompilerParams(vmem_limit_bytes=SCOPE),
-        cost_estimate=cost(0, count * 2 * depth * FBLOCK * 2),
-        name="prefetch",
-    )(*in_hbm(w_gate, w_up), after)
+def prefetch(first, count, weights, after, block=0):
+    w_gate, _, w_down = weights
+    slots, depth, hidden = w_gate.shape
+    shapes = [(2, depth, FBLOCK)] * count + [(*w_down.shape[:2], block)] * bool(block)
+    return list(
+        pl.pallas_call(
+            functools.partial(prefetch_body, first, count, hidden // FBLOCK, block),
+            in_specs=[HBM] * 3 + [VMEM],
+            out_specs=[VMEM] * len(shapes),
+            out_shape=[pltpu.VMEM(s, BF16) for s in shapes],
+            scratch_shapes=[pltpu.SemaphoreType.DMA((len(shapes), max(2, slots)))],
+            compiler_params=pltpu.CompilerParams(vmem_limit_bytes=SCOPE),
+            cost_estimate=cost(0, sum(2 * math.prod(s) for s in shapes)),
+            name="prefetch",
+        )(*in_hbm(*weights), after)
+    )
 
 
 def halves(value, gain, rows, where):
@@ -338,11 +353,11 @@
     return value[:count] + value[count:]
 
 
-def expand_body(sides, held, split, ring, *refs):
+def expand_body(sides, kept, split, ring, *refs):
     chunks, refs = refs[:sides], refs[sides:]
     blocks, refs = refs[:sides], refs[sides:]
     gain, router, w_gate, w_up = refs[:4]
-    ready, refs = refs[4 : 4 + len(held)], refs[4 + len(held) :]
+    ready, refs = refs[4 : 4 + kept], refs[4 + kept :]
     inner, mine, stream, rows, router2, scale, norms, raw, buffer, sems = refs
     games = blocks[0].shape[0]
     count = games * sides
@@ -350,7 +365,6 @@
     features = width * sides
     slots, _, hidden = w_gate.shape
     per_slot = hidden // FBLOCK
-    kept = sum(held)
     streamed = slots * per_slot - kept
     side, tensor = lax.axis_index("side"), lax.axis_index("tensor")
 
@@ -448,7 +462,6 @@
             for c in copies(step + ring):
                 c.start()
 
-    resident = [(array, i) for array, n in zip(ready, held, strict=True) for i in range(n)]
     done, before = 0, None
     for index in range(kept + 1):
         until = streamed * (index + 1) // (kept + 1)
@@ -461,15 +474,14 @@
 
             done, before = until, kept + until - 1
         if index < kept:
-            array, i = resident[index]
-            products(array.at[i], done + index)
+            products(ready[index], done + index)
             if before is not None:
                 finish(before, done + index + 1)
             before = index
     finish(before, streamed + kept - 1)
 
 
-def expand(sides, split, chunks, blocks, gain, router, w_gate, w_up, held, ready, own_width):
+def expand(sides, split, chunks, blocks, gain, router, w_gate, w_up, ready, own_width):
     games = blocks[0].shape[0]
     count = games * sides
     features = chunks[0].shape[1] * sides
@@ -477,7 +489,7 @@
     ring = 2
     arguments = [*chunks, *blocks, gain, router]
     return pl.pallas_call(
-        functools.partial(expand_body, sides, held, split, ring),
+        functools.partial(expand_body, sides, len(ready), split, ring),
         in_specs=[VMEM] * len(arguments) + [HBM] * 2 + [VMEM] * len(ready),
         out_specs=[VMEM] * 2,
         out_shape=[
@@ -494,13 +506,13 @@
             pltpu.VMEM((ring, 2, features, FBLOCK), BF16),
             pltpu.SemaphoreType.DMA((ring, 2)),
         ],
-        compiler_params=pltpu.CompilerParams(vmem_limit_bytes=18 * 2**20),
+        compiler_params=pltpu.CompilerParams(vmem_limit_bytes=16 * 2**20),
         cost_estimate=cost(8 * count * w_gate.size, 2 * w_gate.size * 2),
         name="expand",
     )(*arguments, *in_hbm(w_gate, w_up), *in_vmem(*ready))
 
 
-def contract_body(tensors, ring, block, inner, w_down, keep, send, buffer, sems):
+def contract_body(tensors, ring, block, inner, first, w_down, keep, send, buffer, sems):
     slots, hidden, features = w_down.shape
     tensor = lax.axis_index("tensor")
     part = features // tensors
@@ -510,7 +522,10 @@
     deep = ring // slots
 
     def copies(step):
-        start = jnp.bitwise_xor(tensor, step // per_part) * part + step % per_part * block
+        number = step // per_part
+        bits = tensors.bit_length() - 1
+        chunk = sum((number >> b) % 2 * 2 ** (bits - 1 - b) for b in range(bits))
+        start = jnp.bitwise_xor(tensor, chunk) * part + step % per_part * block
         return [
             pltpu.make_async_copy(
                 w_down.at[slot, :, columns(start, block)],
@@ -520,18 +535,16 @@
             for slot in range(slots)
         ]
 
-    for step in range(min(deep, steps)):
+    for step in range(1, min(deep + 1, steps)):
         for c in copies(step):
             c.start()
 
-    def run(step, more):
-        for c in copies(step):
-            c.wait()
+    def run(step, more, weights):
         total = None
         for slot in range(slots):
             value = jnp.dot(
                 inner[:, slot * hidden : (slot + 1) * hidden],
-                buffer[step % deep, slot],
+                weights[slot],
                 preferred_element_type=F32,
             )
             total = value if total is None else total + value
@@ -543,20 +556,25 @@
             for c in copies(step + deep):
                 c.start()
 
-    edge = max(0, steps - deep)
-    pl.loop(0, edge)(lambda step: run(step, True))
+    def from_ring(step, more):
+        for c in copies(step):
+            c.wait()
+        run(step, more, buffer.at[step % deep])
+
+    run(0, False, first)
+    edge = max(1, steps - deep)
+    pl.loop(1, edge)(lambda step: from_ring(step, True))
     for step in range(edge, steps):
-        run(step, False)
-
-
-def contract(tensors, inner, w_down):
+        from_ring(step, False)
+
+
+def contract(tensors, block, inner, first, w_down):
     count = inner.shape[0] // 2
     slots, hidden, features = w_down.shape
-    ring = 4 * slots
-    block = 512 if features // tensors % 512 == 0 else LANES
+    ring = 3 * slots
     return pl.pallas_call(
         functools.partial(contract_body, tensors, ring, block),
-        in_specs=[VMEM, HBM],
+        in_specs=[VMEM, VMEM, HBM],
         out_specs=[VMEM, VMEM],
         out_shape=[
             jax.ShapeDtypeStruct((count // 2, features), F32),
@@ -566,54 +584,68 @@
             pltpu.VMEM((ring // slots, slots, hidden, block), BF16),
             pltpu.SemaphoreType.DMA((ring // slots, slots)),
         ],
-        compiler_params=pltpu.CompilerParams(vmem_limit_bytes=24 * 2**20),
+        compiler_params=pltpu.CompilerParams(vmem_limit_bytes=16 * 2**20),
         cost_estimate=cost(4 * count * w_down.size, 2 * w_down.size),
         name="contract",
-    )(inner, *in_hbm(w_down))
-
-
-def halve_body(keep, arrived, low, high):
+    )(inner, *in_vmem(first), *in_hbm(w_down))
+
+
+def halve_body(keep, arrived, low_here, low_there, high_here, high_there):
     total = keep[...] + arrived[...].astype(F32)
-    half = low.shape[0]
-    low[...] = total[:half]
-    high[...] = total[half:].astype(BF16)
+    rows, width = low_here.shape
+    low_here[...] = total[:rows, :width]
+    low_there[...] = total[:rows, width:]
+    high_here[...] = total[rows:, :width].astype(BF16)
+    high_there[...] = total[rows:, width:].astype(BF16)
 
 
 def halve(keep, arrived):
     rows, width = keep.shape
     return pl.pallas_call(
         halve_body,
-        in_specs=[VMEM, VMEM],
-        out_specs=[VMEM, VMEM],
-        out_shape=[
-            jax.ShapeDtypeStruct((rows // 2, width), F32),
-            jax.ShapeDtypeStruct((rows // 2, width), BF16),
-        ],
+        in_specs=[VMEM] * 2,
+        out_specs=[VMEM] * 4,
+        out_shape=[jax.ShapeDtypeStruct((rows // 2, width // 2), t) for t in (F32, F32, BF16, BF16)],
         compiler_params=pltpu.CompilerParams(vmem_limit_bytes=SCOPE),
         name="halve",
     )(keep, arrived)
 
 
-def deal_body(keep, arrived, *outs):
-    width = outs[0].shape[1]
-    for k, out in enumerate(outs):
-        s = slice(k * width, (k + 1) * width)
-        out[...] = (keep[:, s] + arrived[:, s].astype(F32)).astype(out.dtype)
-
-
-def deal(tensors, keep, arrived):
-    rows, width = keep.shape
-    return pl.pallas_call(
-        deal_body,
-        in_specs=[VMEM, VMEM],
-        out_specs=[VMEM] * tensors,
-        out_shape=[
-            jax.ShapeDtypeStruct((rows, width // tensors), F32 if k == 0 else BF16)
-            for k in range(tensors)
-        ],
+def total_body(low, arrived, out):
+    out[...] = (low[...] + arrived[...].astype(F32)).astype(BF16)
+
+
+def total_of(low, arrived):
+    return pl.pallas_call(
+        total_body,
+        in_specs=[VMEM] * 2,
+        out_specs=VMEM,
+        out_shape=jax.ShapeDtypeStruct(low.shape, BF16),
         compiler_params=pltpu.CompilerParams(vmem_limit_bytes=SCOPE),
-        name="deal",
-    )(keep, arrived)
+        name="total",
+    )(low, arrived)
+
+
+def split_body(*refs):
+    parts, (keep, send) = refs[:-2], refs[-2:]
+    value = parts[0][...]
+    for part in parts[1:]:
+        value = value + part[...].astype(F32)
+    width = keep.shape[1]
+    keep[...] = value[:, :width]
+    send[...] = value[:, width:].astype(BF16)
+
+
+def split_columns(*parts):
+    rows, width = parts[0].shape
+    return pl.pallas_call(
+        split_body,
+        in_specs=[VMEM] * len(parts),
+        out_specs=[VMEM] * 2,
+        out_shape=[jax.ShapeDtypeStruct((rows, width // 2), t) for t in (F32, BF16)],
+        compiler_params=pltpu.CompilerParams(vmem_limit_bytes=SCOPE),
+        name="split",
+    )(*parts)
 
 
 def last_body(*refs):
@@ -656,7 +688,8 @@
     depth = query.shape[1]
     extra = features // sides // 2
     slots, _, hidden = w_gate.shape
-    held = [2, 1, 2]
+    held = [1, 1, 1, 1, 1]
+    weights = (w_gate, w_up, w_down)
     *blocks, w_here = attend(
         sides,
         extra,
@@ -670,20 +703,26 @@
         route_ids,
         w_out,
     )
-    ready = [prefetch(0, held[0], w_gate, w_up, blocks[0])]
+    ready = prefetch(0, held[0], weights, blocks[0])
     blocks = [blocks[0]] + [swap(blocks[k], "side", sides, k) for k in range(1, sides)]
-    mine, other = project(sides, blocks, w_here, ready[0])
-    ready.append(prefetch(held[0], held[1], w_gate, w_up, other))
-    mine, other = add(mine, swap(other, "tensor", tensors, 1), ready[1])
-    ready.append(prefetch(held[0] + held[1], held[2], w_gate, w_up, other))
+    mine, other = project(sides, blocks, w_here, ready[-1])
+    ready += prefetch(len(ready), held[1], weights, other)
+    mine, other = add(mine, swap(other, "tensor", tensors, 1), ready[-1])
+    ready += prefetch(len(ready), held[2], weights, other)
     step = 2
     while step < tensors // 2:
-        mine, other = add(mine, swap(other, "tensor", tensors, step), ready[2])
+        mine, other = add(mine, swap(other, "tensor", tensors, step), ready[-1])
         step *= 2
-    stream = stream_of(sides, depth, mine, swap(other, "tensor", tensors, step), blocks, ready[2])
-    own = join(stream, swap(stream, "tensor", tensors, 1))
+    stream = stream_of(sides, depth, mine, swap(other, "tensor", tensors, step), blocks, ready[-1])
+    ready += prefetch(len(ready), held[3], weights, stream)
+    own = join(stream, swap(stream, "tensor", tensors, 1), ready[-1])
+    part = features // tensors
+    block = 512 if part % 512 == 0 else LANES
+    *more, down = prefetch(len(ready), held[4], weights, own, block)
+    ready += more
     across = swap(own, "side", sides, 2)
     beside = swap(own, "side", sides, 1)
+    across, down = lax.optimization_barrier((across, down))
     chunks = [own, beside, across, swap(across, "side", sides, 1)]
     inner, mine = expand(
         sides,
@@ -694,15 +733,19 @@
         w_router.T,
         w_gate,
         w_up,
-        held,
         ready,
-        features // tensors,
-    )
-    keep, send = contract(tensors, inner, w_down)
-    low, high = halve(keep, swap(send, "side", sides, 1))
-    dealt = deal(tensors, low, swap(high, "side", sides, 2))
-    dealt = [dealt[0]] + [swap(dealt[k], "tensor", tensors, k) for k in range(1, tensors)]
-    return last(mine, dealt)
+        part,
+    )
+    keep, send = contract(tensors, block, inner, down, w_down)
+    low_here, low_there, high_here, high_there = halve(keep, swap(send, "side", sides, 1))
+    there = total_of(low_there, swap(high_there, "side", sides, 2))
+    parts = [low_here, swap(high_here, "side", sides, 2), swap(there, "tensor", tensors, 1)]
+    mask = 2
+    while mask < tensors:
+        keep, send = split_columns(*parts)
+        parts = [keep, swap(send, "tensor", tensors, mask)]
+        mask *= 2
+    return last(mine, parts)
 
 
 def attend_local(query, new_key, new_value, key_cache, value_cache, cache_len):

time: 98.8 us -> 95 us (0.962)
  waiting for transfers between devices: 21.5 us -> 17.4 us
  Pallas kernels: 59 us -> 61.4 us
  starting transfers between devices: 17.3 us -> 15.8 us
    ppermute x14, waiting for transfers between devices: 21.5 us -> 17.4 us  [swap(): return lax.ppermute(value, axis, [(i, i ^ mask) for i in range(count)])]
    pallas_call x8 -> x11, Pallas kernels: 40.5 us -> 43.6 us  [the longest x1 23.6 us: expand(): pl.pallas_call(functools.partial(expand_body, sides, len(ready), split, r...]
    ppermute x14, starting transfers between devices: 17.3 us -> 15.8 us  [swap(): return lax.ppermute(value, axis, [(i, i ^ mask) for i in range(count)])]
  transfers between devices with their start and end apart: 14 -> 14, of which waited for: 8 -> 10; matrix products, arithmetic and copies ran while one was open for 0% -> 0% of each run, Pallas kernels for 13% -> 17%
where the time goes in v3:
time: 95 us; the launch traced here: 94.8 us
  Pallas kernels  61.4 us (65%)
  waiting for transfers between devices  17.4 us (18%)
  starting transfers between devices  15.8 us (17%)
    pallas_call x1, Pallas kernels, expand(): pl.pallas_call(functools.partial(expand_body, sides, len(ready), split, r...  23.6 us
    ppermute x14, waiting for transfers between devices, swap(): return lax.ppermute(value, axis, [(i, i ^ mask) for i in range(count)])  17.4 us
    pallas_call x1, Pallas kernels, contract(): pl.pallas_call(functools.partial(contract_body, tensors, ring, block), in...  16.1 us
    pallas_call x5, Pallas kernels, prefetch(): pl.pallas_call(functools.partial(prefetch_body, first, count, hidden // F...  16 us
    ppermute x14, starting transfers between devices, swap(): return lax.ppermute(value, axis, [(i, i ^ mask) for i in range(count)])  15.8 us
    pallas_call x1, Pallas kernels, attend(): pl.pallas_call(functools.partial(attend_body, sides, block), in_specs=[HB...  3.88 us
  transfers between devices with their start and end apart: 14, of which 10 were waited for; matrix products, arithmetic and copies ran while one was open for 0% of the time, Pallas kernels for 17%

profile of v3, /device:TPU:0, one launch (start us, length us, event | category | flops | bytes accessed | tf_op | source)
XLA Modules:
  0.0 94.8 jit_solution(2375003915836443726)
XLA Ops:
  0.0 3.9 %attend.1 = (bf16[16,2432]{1,0:T(8,128)(2,1)S(1)}, bf16[16,2432]{1,0:T(8,128)(2,1)S(1)}, bf16[16,2432]{1,0:T(8,128)(2,1)S(1)}, bf16[16,2432]{1,0:T(8,128)(2,1)S(1)}, bf16[1536,1536]{1,0:T(8,128)(2,1)S(1)}) custom-call(s32[16]{0:T(128)} %length_at.1, bf16[16,1536]{1,0:T(8,128)(2,1)} %query_at.1, bf16[16,256]{1,0:T(8,128)(2,1)} %new_key_at.1, ...), custom_call_target="tpu_custom_call" | custom-call | flops 67108864 | bytes 4194304 | tf_op jit(solution)/shard_map/attend/pallas_call | solution.py:177
  3.9 0.5 collective-permute-start
  4.4 2.6 %collective-permute-start.1 = (bf16[16,2432]{1,0:T(8,128)(2,1)S(1)}, bf16[16,2432]{1,0:T(8,128)(2,1)S(1)}, u32[]{:S(2)}, u32[]{:S(2)}) collective-permute-start(bf16[16,2432]{1,0:T(8,128)(2,1)S(1)} %get-tuple-element.30), channel_id=1, source_target_pairs={{0,8},{4,12},{8,0},{12,4},{1,9},{5,13},{9,1},{13,5},{2,10},{6,14},... | collective-permute-start | bytes 233480 | tf_op jit(solution)/shard_map/ppermute | solution.py:33
  7.0 0.1 collective-permute-start.2
  7.0 2.9 %prefetch.5.refs_5_.refs_12_ = bf16[2,6144,256]{2,1,0:T(8,128)(2,1)S(1)} custom-call(bf16[2,6144,2048]{2,1,0:T(8,128)(2,1)} %refs_10_.1, bf16[2,6144,2048]{2,1,0:T(8,128)(2,1)} %refs_11_.1, bf16[2,2048,6144]{2,1,0:T(8,128)(2,1)} %w_down.11, bf16[16,2432]{1,0:T(8,128)(2,1)S(1)} %get-tuple-element.28.after.refs_0_.refs_4_), custom_call_target="tpu_custom_call" | custom-call | bytes 6291456 | tf_op jit(solution)/shard_map/prefetch/pallas_call | solution.py:330
  9.9 0.0 copy-start
  9.9 0.0 collective-permute-done.refs_1_.refs_5_
  9.9 0.0 collective-permute-done.1.refs_2_.refs_6_
  10.0 1.3 %collective-permute-done.2.refs_3_.refs_7_ = bf16[16,2432]{1,0:T(8,128)(2,1)S(1)} collective-permute-done((bf16[16,2432]{1,0:T(8,128)(2,1)S(1)}, bf16[16,2432]{1,0:T(8,128)(2,1)S(1)}, u32[]{:S(2)}, u32[]{:S(2)}) %collective-permute-start.2) | collective-permute-done | bytes 77856 | tf_op jit(solution)/shard_map/ppermute | solution.py:33
  11.3 1.0 %project.1 = (f32[64,768]{1,0:T(8,128)S(1)}, bf16[64,768]{1,0:T(8,128)(2,1)S(1)}) custom-call(bf16[16,2432]{1,0:T(8,128)(2,1)S(1)} %get-tuple-element.28.after.refs_0_.refs_4_, bf16[16,2432]{1,0:T(8,128)(2,1)S(1)} %collective-permute-done.refs_1_.refs_5_, bf16[16,2432]{1,0:T(8,128)(2,1)S(1)} %collective-permute-done.1.refs_2_.refs_6_, ...), custom_call_target="tpu_custom_call" | custom-call | flops 301989888 | bytes 4718592 | tf_op jit(solution)/shard_map/project/pallas_call | solution.py:220
  12.3 2.0 %collective-permute-start.3 = (bf16[64,768]{1,0:T(8,128)(2,1)S(1)}, bf16[64,768]{1,0:T(8,128)(2,1)S(1)}, u32[]{:S(2)}, u32[]{:S(2)}) collective-permute-start(bf16[64,768]{1,0:T(8,128)(2,1)S(1)} %get-tuple-element.34.after), channel_id=1, source_target_pairs={{0,1},{1,0},{2,3},{3,2},{4,5},{5,4},{6,7},{7,6},{8,9},{9,8},{10,11... | collective-permute-start | bytes 294920 | tf_op jit(solution)/shard_map/ppermute | solution.py:33
  14.2 2.9 %prefetch.6.after.refs_13_ = bf16[2,6144,256]{2,1,0:T(8,128)(2,1)S(1)} custom-call(bf16[2,6144,2048]{2,1,0:T(8,128)(2,1)} %refs_10_.1, bf16[2,6144,2048]{2,1,0:T(8,128)(2,1)} %refs_11_.1, bf16[2,2048,6144]{2,1,0:T(8,128)(2,1)} %w_down.11, bf16[64,768]{1,0:T(8,128)(2,1)S(1)} %get-tuple-element.34.after), custom_call_target="tpu_custom_call" | custom-call | bytes 6291456 | tf_op jit(solution)/shard_map/prefetch/pallas_call | solution.py:330
  17.1 0.0 copy-done
  17.1 0.2 collective-permute-done.3.arrived
  17.3 2.8 %collective-permute-start.4 = (bf16[64,768]{1,0:T(8,128)(2,1)S(1)}, bf16[64,768]{1,0:T(8,128)(2,1)S(1)}, u32[]{:S(2)}, u32[]{:S(2)}) collective-permute-start(bf16[64,768]{1,0:T(8,128)(2,1)S(1)} %get-tuple-element.36.after), channel_id=1, source_target_pairs={{0,2},{1,3},{2,0},{3,1},{4,6},{5,7},{6,4},{7,5},{8,10},{9,11},{10,... | collective-permute-start | bytes 294920 | tf_op jit(solution)/shard_map/ppermute | solution.py:33
  20.2 2.9 %prefetch.7.refs_4_.refs_14_ = bf16[2,6144,256]{2,1,0:T(8,128)(2,1)S(1)} custom-call(bf16[2,6144,2048]{2,1,0:T(8,128)(2,1)} %refs_10_.1, bf16[2,6144,2048]{2,1,0:T(8,128)(2,1)} %refs_11_.1, bf16[2,2048,6144]{2,1,0:T(8,128)(2,1)} %w_down.11, bf16[64,768]{1,0:T(8,128)(2,1)S(1)} %get-tuple-element.36.after), custom_call_target="tpu_custom_call" | custom-call | bytes 6291456 | tf_op jit(solution)/shard_map/prefetch/pallas_call | solution.py:330
  23.0 1.7 %collective-permute-done.4.arrived = bf16[64,768]{1,0:T(8,128)(2,1)S(1)} collective-permute-done((bf16[64,768]{1,0:T(8,128)(2,1)S(1)}, bf16[64,768]{1,0:T(8,128)(2,1)S(1)}, u32[]{:S(2)}, u32[]{:S(2)}) %collective-permute-start.4) | collective-permute-done | bytes 98336 | tf_op jit(solution)/shard_map/ppermute | solution.py:33
  24.8 0.6 collective-permute-start.5
  25.5 2.9 %prefetch.8.after.refs_15_ = bf16[2,6144,256]{2,1,0:T(8,128)(2,1)S(1)} custom-call(bf16[2,6144,2048]{2,1,0:T(8,128)(2,1)} %refs_10_.1, bf16[2,6144,2048]{2,1,0:T(8,128)(2,1)} %refs_11_.1, bf16[2,2048,6144]{2,1,0:T(8,128)(2,1)} %w_down.11, bf16[64,768]{1,0:T(8,128)(2,1)S(1)} %stream.1.after.mine), custom_call_target="tpu_custom_call" | custom-call | bytes 6291456 | tf_op jit(solution)/shard_map/prefetch/pallas_call | solution.py:330
  28.3 1.2 %collective-permute-done.5.arrived = bf16[64,768]{1,0:T(8,128)(2,1)S(1)} collective-permute-done((bf16[64,768]{1,0:T(8,128)(2,1)S(1)}, bf16[64,768]{1,0:T(8,128)(2,1)S(1)}, u32[]{:S(2)}, u32[]{:S(2)}) %collective-permute-start.5) | collective-permute-done | bytes 98336 | tf_op jit(solution)/shard_map/ppermute | solution.py:33
  29.5 0.0 copy-start.2
  29.5 0.0 slice-start.1
  29.6 0.0 copy-start.1
  29.6 1.5 %collective-permute-start.7 = (bf16[64,1536]{1,0:T(8,128)(2,1)S(1)}, bf16[64,1536]{1,0:T(8,128)(2,1)S(1)}, u32[]{:S(2)}, u32[]{:S(2)}) collective-permute-start(bf16[64,1536]{1,0:T(8,128)(2,1)S(1)} %join.1.after.refs_0_), channel_id=1, source_target_pairs={{0,8},{4,12},{8,0},{12,4},{1,9},{5,13},{9,1},{13,5},{2,10},{6,14},... | collective-permute-start | bytes 589832 | tf_op jit(solution)/shard_map/ppermute | solution.py:33
  31.1 0.0 collective-permute-start.6
  31.1 4.5 %prefetch.9 = (bf16[2,6144,256]{2,1,0:T(8,128)(2,1)S(1)}, bf16[2,2048,512]{2,1,0:T(8,128)(2,1)S(1)}) custom-call(bf16[2,6144,2048]{2,1,0:T(8,128)(2,1)} %refs_10_.1, bf16[2,6144,2048]{2,1,0:T(8,128)(2,1)} %refs_11_.1, bf16[2,2048,6144]{2,1,0:T(8,128)(2,1)} %w_down.11, bf16[64,1536]{1,0:T(8,128)(2,1)S(1)} %join.1.after.refs_0_), custom_call_target="tpu_custom_call" | custom-call | bytes 10485760 | tf_op jit(solution)/shard_map/prefetch/pallas_call | solution.py:330
  35.6 0.0 collective-permute-done.7.refs_2_
  35.6 0.3 collective-permute-start.8
  35.9 0.0 copy-done.2
  35.9 0.0 collective-permute-done.6.refs_1_
  36.0 1.1 %collective-permute-done.8.refs_3_ = bf16[64,1536]{1,0:T(8,128)(2,1)S(1)} collective-permute-done((bf16[64,1536]{1,0:T(8,128)(2,1)S(1)}, bf16[64,1536]{1,0:T(8,128)(2,1)S(1)}, u32[]{:S(2)}, u32[]{:S(2)}) %collective-permute-start.8) | collective-permute-done | bytes 196640 | tf_op jit(solution)/shard_map/ppermute | solution.py:33
  37.1 0.0 slice-done
  37.1 0.0 slice-done.1
  37.1 0.0 copy-done.1
  37.1 23.6 %expand.1 = (bf16[128,4096]{1,0:T(8,128)(2,1)S(1)}, bf16[16,1536]{1,0:T(8,128)(2,1)S(1)}) custom-call(bf16[64,1536]{1,0:T(8,128)(2,1)S(1)} %join.1.after.refs_0_, bf16[64,1536]{1,0:T(8,128)(2,1)S(1)} %collective-permute-done.6.refs_1_, bf16[64,1536]{1,0:T(8,128)(2,1)S(1)} %collective-permute-done.7.refs_2_, ...), custom_call_target="tpu_custom_call" | custom-call | flops 12884901888 | bytes 100663296 | tf_op jit(solution)/shard_map/expand/pallas_call | solution.py:491
  60.7 16.1 %contract.1 = (f32[32,6144]{1,0:T(8,128)S(1)}, bf16[32,6144]{1,0:T(8,128)(2,1)S(1)}) custom-call(bf16[128,4096]{1,0:T(8,128)(2,1)S(1)} %get-tuple-element.41.inner, bf16[2,2048,512]{2,1,0:T(8,128)(2,1)S(1)} %get-tuple-element.42.first, bf16[2,2048,6144]{2,1,0:T(8,128)(2,1)} %w_down.11), custom_call_target="tpu_custom_call" | custom-call | flops 6442450944 | bytes 50331648 | tf_op jit(solution)/shard_map/contract/pallas_call | solution.py:575
  76.8 0.3 collective-permute-start.9
  77.2 1.4 %collective-permute-done.9.arrived = bf16[32,6144]{1,0:T(8,128)(2,1)S(1)} collective-permute-done((bf16[32,6144]{1,0:T(8,128)(2,1)S(1)}, bf16[32,6144]{1,0:T(8,128)(2,1)S(1)}, u32[]{:S(2)}, u32[]{:S(2)}) %collective-permute-start.9) | collective-permute-done | bytes 393248 | tf_op jit(solution)/shard_map/ppermute | solution.py:33
  78.6 0.1 halve.1
  78.7 1.2 %collective-permute-start.11 = (bf16[16,3072]{1,0:T(8,128)(2,1)S(1)}, bf16[16,3072]{1,0:T(8,128)(2,1)S(1)}, u32[]{:S(2)}, u32[]{:S(2)}) collective-permute-start(bf16[16,3072]{1,0:T(8,128)(2,1)S(1)} %get-tuple-element.48), channel_id=1, source_target_pairs={{0,8},{4,12},{8,0},{12,4},{1,9},{5,13},{9,1},{13,5},{2,10},{6,14},... | collective-permute-start | bytes 294920 | tf_op jit(solution)/shard_map/ppermute | solution.py:33
  79.8 0.9 collective-permute-start.10
  80.8 3.6 %collective-permute-done.11.arrived = bf16[16,3072]{1,0:T(8,128)(2,1)S(1)} collective-permute-done((bf16[16,3072]{1,0:T(8,128)(2,1)S(1)}, bf16[16,3072]{1,0:T(8,128)(2,1)S(1)}, u32[]{:S(2)}, u32[]{:S(2)}) %collective-permute-start.11) | collective-permute-done | bytes 98336 | tf_op jit(solution)/shard_map/ppermute | solution.py:33
  84.4 0.6 collective-permute-start.12
  85.0 0.8 collective-permute-done.10.refs_1_
  85.8 3.2 %collective-permute-done.12.refs_2_ = bf16[16,3072]{1,0:T(8,128)(2,1)S(1)} collective-permute-done((bf16[16,3072]{1,0:T(8,128)(2,1)S(1)}, bf16[16,3072]{1,0:T(8,128)(2,1)S(1)}, u32[]{:S(2)}, u32[]{:S(2)}) %collective-permute-start.12) | collective-permute-done | bytes 98336 | tf_op jit(solution)/shard_map/ppermute | solution.py:33
  89.1 2.4 %collective-permute-start.13 = (bf16[16,1536]{1,0:T(8,128)(2,1)S(1)}, bf16[16,1536]{1,0:T(8,128)(2,1)S(1)}, u32[]{:S(2)}, u32[]{:S(2)}) collective-permute-start(bf16[16,1536]{1,0:T(8,128)(2,1)S(1)} %get-tuple-element.50), channel_id=1, source_target_pairs={{0,2},{1,3},{2,0},{3,1},{4,6},{5,7},{6,4},{7,5},{8,10},{9,11},{10,... | collective-permute-start | bytes 147464 | tf_op jit(solution)/shard_map/ppermute | solution.py:33
  91.5 2.7 %collective-permute-done.13.refs_2_ = bf16[16,1536]{1,0:T(8,128)(2,1)S(1)} collective-permute-done((bf16[16,1536]{1,0:T(8,128)(2,1)S(1)}, bf16[16,1536]{1,0:T(8,128)(2,1)S(1)}, u32[]{:S(2)}, u32[]{:S(2)}) %collective-permute-start.13) | collective-permute-done | bytes 49184 | tf_op jit(solution)/shard_map/ppermute | solution.py:33
  94.2 0.6 last.1
  (8 shorter events, 0.2 us)
Async XLA Ops:
  3.9 6.0 %collective-permute-start = (bf16[16,2432]{1,0:T(8,128)(2,1)S(1)}, bf16[16,2432]{1,0:T(8,128)(2,1)S(1)}, u32[]{:S(2)}, u32[]{:S(2)}) collective-permute-start(bf16[16,2432]{1,0:T(8,128)(2,1)S(1)} %get-tuple-element.29), channel_id=1, source_target_pairs={{0,4},{4,0},{8,12},{12,8},{1,5},{5,1},{9,13},{13,9},{2,6},{6,2},{1... | collective-permute-start | bytes 233480 | tf_op jit(solution)/shard_map/ppermute | solution.py:33
  4.4 5.5 %collective-permute-start.1 = (bf16[16,2432]{1,0:T(8,128)(2,1)S(1)}, bf16[16,2432]{1,0:T(8,128)(2,1)S(1)}, u32[]{:S(2)}, u32[]{:S(2)}) collective-permute-start(bf16[16,2432]{1,0:T(8,128)(2,1)S(1)} %get-tuple-element.30), channel_id=1, source_target_pairs={{0,8},{4,12},{8,0},{12,4},{1,9},{5,13},{9,1},{13,5},{2,10},{6,14},... | collective-permute-start | bytes 233480 | tf_op jit(solution)/shard_map/ppermute | solution.py:33
  7.0 4.3 %collective-permute-start.2 = (bf16[16,2432]{1,0:T(8,128)(2,1)S(1)}, bf16[16,2432]{1,0:T(8,128)(2,1)S(1)}, u32[]{:S(2)}, u32[]{:S(2)}) collective-permute-start(bf16[16,2432]{1,0:T(8,128)(2,1)S(1)} %get-tuple-element.31), channel_id=1, source_target_pairs={{0,12},{4,8},{8,4},{12,0},{1,13},{5,9},{9,5},{13,1},{2,14},{6,10},... | collective-permute-start | bytes 233480 | tf_op jit(solution)/shard_map/ppermute | solution.py:33
  9.9 7.2 %copy-start = (bf16[2,6144,256]{2,1,0:T(8,128)(2,1)}, bf16[2,6144,256]{2,1,0:T(8,128)(2,1)S(1)}, u32[]{:S(2)}) copy-start(bf16[2,6144,256]{2,1,0:T(8,128)(2,1)S(1)} %prefetch.5.refs_5_.refs_12_) | copy-start | bytes 18874372
  12.3 5.0 %collective-permute-start.3 = (bf16[64,768]{1,0:T(8,128)(2,1)S(1)}, bf16[64,768]{1,0:T(8,128)(2,1)S(1)}, u32[]{:S(2)}, u32[]{:S(2)}) collective-permute-start(bf16[64,768]{1,0:T(8,128)(2,1)S(1)} %get-tuple-element.34.after), channel_id=1, source_target_pairs={{0,1},{1,0},{2,3},{3,2},{4,5},{5,4},{6,7},{7,6},{8,9},{9,8},{10,11... | collective-permute-start | bytes 294920 | tf_op jit(solution)/shard_map/ppermute | solution.py:33
  17.3 7.4 %collective-permute-start.4 = (bf16[64,768]{1,0:T(8,128)(2,1)S(1)}, bf16[64,768]{1,0:T(8,128)(2,1)S(1)}, u32[]{:S(2)}, u32[]{:S(2)}) collective-permute-start(bf16[64,768]{1,0:T(8,128)(2,1)S(1)} %get-tuple-element.36.after), channel_id=1, source_target_pairs={{0,2},{1,3},{2,0},{3,1},{4,6},{5,7},{6,4},{7,5},{8,10},{9,11},{10,... | collective-permute-start | bytes 294920 | tf_op jit(solution)/shard_map/ppermute | solution.py:33
  24.8 4.7 %collective-permute-start.5 = (bf16[64,768]{1,0:T(8,128)(2,1)S(1)}, bf16[64,768]{1,0:T(8,128)(2,1)S(1)}, u32[]{:S(2)}, u32[]{:S(2)}) collective-permute-start(bf16[64,768]{1,0:T(8,128)(2,1)S(1)} %stream.1.after.mine), channel_id=1, source_target_pairs={{0,1},{1,0},{2,3},{3,2},{4,5},{5,4},{6,7},{7,6},{8,9},{9,8},{10,11... | collective-permute-start | bytes 294920 | tf_op jit(solution)/shard_map/ppermute | solution.py:33
  29.5 7.6 %slice-start = ((s8[6291456]{0:T(1024)(128)(4,1)}), s8[4194304]{0:T(1024)(128)(4,1)S(1)}, s32[]{:S(2)}) async-start(s8[6291456]{0:T(1024)(128)(4,1)} %bitcast.2), calls=%async_computation | async-start | bytes 8388608
  29.5 6.4 %copy-start.2 = (bf16[6144]{0:T(1024)(128)(2,1)S(1)}, bf16[6144]{0:T(1024)(128)(2,1)}, u32[]{:S(2)}) copy-start(bf16[6144]{0:T(1024)(128)(2,1)} %param.22) | copy-start | bytes 36868
  29.5 7.6 %slice-start.1 = ((s8[6291456]{0:T(1024)(128)(4,1)}), s8[2097152]{0:T(1024)(128)(4,1)S(1)}, s32[]{:S(2)}) async-start(s8[6291456]{0:T(1024)(128)(4,1)} %bitcast.2), calls=%async_computation.1 | async-start | bytes 4194304
  29.6 7.5 %copy-start.1 = (f32[6144,8]{0,1:T(8,128)S(1)}, f32[6144,8]{0,1:T(8,128)}, u32[]{:S(2)}) copy-start(f32[6144,8]{0,1:T(8,128)} %param.23) | copy-start | bytes 589828
  29.6 6.0 %collective-permute-start.7 = (bf16[64,1536]{1,0:T(8,128)(2,1)S(1)}, bf16[64,1536]{1,0:T(8,128)(2,1)S(1)}, u32[]{:S(2)}, u32[]{:S(2)}) collective-permute-start(bf16[64,1536]{1,0:T(8,128)(2,1)S(1)} %join.1.after.refs_0_), channel_id=1, source_target_pairs={{0,8},{4,12},{8,0},{12,4},{1,9},{5,13},{9,1},{13,5},{2,10},{6,14},... | collective-permute-start | bytes 589832 | tf_op jit(solution)/shard_map/ppermute | solution.py:33
  31.1 4.9 %collective-permute-start.6 = (bf16[64,1536]{1,0:T(8,128)(2,1)S(1)}, bf16[64,1536]{1,0:T(8,128)(2,1)S(1)}, u32[]{:S(2)}, u32[]{:S(2)}) collective-permute-start(bf16[64,1536]{1,0:T(8,128)(2,1)S(1)} %join.1.after.refs_0_), channel_id=1, source_target_pairs={{0,4},{4,0},{8,12},{12,8},{1,5},{5,1},{9,13},{13,9},{2,6},{6,2},{1... | collective-permute-start | bytes 589832 | tf_op jit(solution)/shard_map/ppermute | solution.py:33
  35.6 1.5 %collective-permute-start.8 = (bf16[64,1536]{1,0:T(8,128)(2,1)S(1)}, bf16[64,1536]{1,0:T(8,128)(2,1)S(1)}, u32[]{:S(2)}, u32[]{:S(2)}) collective-permute-start(bf16[64,1536]{1,0:T(8,128)(2,1)S(1)} %collective-permute-done.7.refs_2_), channel_id=1, source_target_pairs={{0,4},{4,0},{8,12},{12,8},{1,5},{5,1},{9,13},{13,9},{2,6},{6,2},{1... | collective-permute-start | bytes 589832 | tf_op jit(solution)/shard_map/ppermute | solution.py:33
  76.8 1.8 %collective-permute-start.9 = (bf16[32,6144]{1,0:T(8,128)(2,1)S(1)}, bf16[32,6144]{1,0:T(8,128)(2,1)S(1)}, u32[]{:S(2)}, u32[]{:S(2)}) collective-permute-start(bf16[32,6144]{1,0:T(8,128)(2,1)S(1)} %get-tuple-element.44), channel_id=1, source_target_pairs={{0,4},{4,0},{8,12},{12,8},{1,5},{5,1},{9,13},{13,9},{2,6},{6,2},{1... | collective-permute-start | bytes 1179656 | tf_op jit(solution)/shard_map/ppermute | solution.py:33
  78.7 5.7 %collective-permute-start.11 = (bf16[16,3072]{1,0:T(8,128)(2,1)S(1)}, bf16[16,3072]{1,0:T(8,128)(2,1)S(1)}, u32[]{:S(2)}, u32[]{:S(2)}) collective-permute-start(bf16[16,3072]{1,0:T(8,128)(2,1)S(1)} %get-tuple-element.48), channel_id=1, source_target_pairs={{0,8},{4,12},{8,0},{12,4},{1,9},{5,13},{9,1},{13,5},{2,10},{6,14},... | collective-permute-start | bytes 294920 | tf_op jit(solution)/shard_map/ppermute | solution.py:33
  79.8 6.0 %collective-permute-start.10 = (bf16[16,3072]{1,0:T(8,128)(2,1)S(1)}, bf16[16,3072]{1,0:T(8,128)(2,1)S(1)}, u32[]{:S(2)}, u32[]{:S(2)}) collective-permute-start(bf16[16,3072]{1,0:T(8,128)(2,1)S(1)} %get-tuple-element.46), channel_id=1, source_target_pairs={{0,8},{4,12},{8,0},{12,4},{1,9},{5,13},{9,1},{13,5},{2,10},{6,14},... | collective-permute-start | bytes 294920 | tf_op jit(solution)/shard_map/ppermute | solution.py:33
  84.4 4.7 %collective-permute-start.12 = (bf16[16,3072]{1,0:T(8,128)(2,1)S(1)}, bf16[16,3072]{1,0:T(8,128)(2,1)S(1)}, u32[]{:S(2)}, u32[]{:S(2)}) collective-permute-start(bf16[16,3072]{1,0:T(8,128)(2,1)S(1)} %total.1), channel_id=1, source_target_pairs={{0,1},{1,0},{2,3},{3,2},{4,5},{5,4},{6,7},{7,6},{8,9},{9,8},{10,11... | collective-permute-start | bytes 294920 | tf_op jit(solution)/shard_map/ppermute | solution.py:33
  89.1 5.1 %collective-permute-start.13 = (bf16[16,1536]{1,0:T(8,128)(2,1)S(1)}, bf16[16,1536]{1,0:T(8,128)(2,1)S(1)}, u32[]{:S(2)}, u32[]{:S(2)}) collective-permute-start(bf16[16,1536]{1,0:T(8,128)(2,1)S(1)} %get-tuple-element.50), channel_id=1, source_target_pairs={{0,2},{1,3},{2,0},{3,1},{4,6},{5,7},{6,4},{7,5},{8,10},{9,11},{10,... | collective-permute-start | bytes 147464 | tf_op jit(solution)/shard_map/ppermute | solution.py:33

commit v4 on v3

--- a/solution.py
+++ b/solution.py
@@ -294,12 +294,13 @@
     )(mine, arrived, *in_vmem(after))
 
 
-def prefetch_body(first, count, per_slot, block, w_gate, w_up, w_down, after, *refs):
+def prefetch_body(first, count, per_slot, block, number, w_gate, w_up, w_down, after, *refs):
     del after
     outs, sems = refs[:-1], refs[-1]
     copies = []
     if block:
         start = lax.axis_index("tensor") * (w_down.shape[2] // lax.axis_size("tensor"))
+        start = start + number * block
         for i in range(w_down.shape[0]):
             copies.append(
                 pltpu.make_async_copy(
@@ -322,13 +323,13 @@
         c.wait()
 
 
-def prefetch(first, count, weights, after, block=0):
+def prefetch(first, count, weights, after, block=0, number=0):
     w_gate, _, w_down = weights
     slots, depth, hidden = w_gate.shape
     shapes = [(2, depth, FBLOCK)] * count + [(*w_down.shape[:2], block)] * bool(block)
     return list(
         pl.pallas_call(
-            functools.partial(prefetch_body, first, count, hidden // FBLOCK, block),
+            functools.partial(prefetch_body, first, count, hidden // FBLOCK, block, number),
             in_specs=[HBM] * 3 + [VMEM],
             out_specs=[VMEM] * len(shapes),
             out_shape=[pltpu.VMEM(s, BF16) for s in shapes],
@@ -512,7 +513,8 @@
     )(*arguments, *in_hbm(w_gate, w_up), *in_vmem(*ready))
 
 
-def contract_body(tensors, ring, block, inner, first, w_down, keep, send, buffer, sems):
+def contract_body(tensors, ring, block, kept, inner, *refs):
+    ready, (w_down, keep, send, buffer, sems) = refs[:kept], refs[kept:]
     slots, hidden, features = w_down.shape
     tensor = lax.axis_index("tensor")
     part = features // tensors
@@ -522,10 +524,7 @@
     deep = ring // slots
 
     def copies(step):
-        number = step // per_part
-        bits = tensors.bit_length() - 1
-        chunk = sum((number >> b) % 2 * 2 ** (bits - 1 - b) for b in range(bits))
-        start = jnp.bitwise_xor(tensor, chunk) * part + step % per_part * block
+        start = jnp.bitwise_xor(tensor, step // per_part) * part + step % per_part * block
         return [
             pltpu.make_async_copy(
                 w_down.at[slot, :, columns(start, block)],
@@ -535,12 +534,14 @@
             for slot in range(slots)
         ]
 
-    for step in range(1, min(deep + 1, steps)):
+    for step in range(kept, min(deep + kept, steps)):
         for c in copies(step):
             c.start()
 
-    def run(step, more, weights):
+    def run(step, more, weights, arriving=()):
         total = None
+        for c in arriving:
+            c.wait()
         for slot in range(slots):
             value = jnp.dot(
                 inner[:, slot * hidden : (slot + 1) * hidden],
@@ -557,24 +558,23 @@
                 c.start()
 
     def from_ring(step, more):
-        for c in copies(step):
-            c.wait()
-        run(step, more, buffer.at[step % deep])
-
-    run(0, False, first)
-    edge = max(1, steps - deep)
-    pl.loop(1, edge)(lambda step: from_ring(step, True))
+        run(step, more, buffer.at[step % deep], copies(step))
+
+    for step, weights in enumerate(ready):
+        run(step, False, weights)
+    edge = max(kept, steps - deep)
+    pl.loop(kept, edge)(lambda step: from_ring(step, True))
     for step in range(edge, steps):
         from_ring(step, False)
 
 
-def contract(tensors, block, inner, first, w_down):
+def contract(tensors, block, inner, ready, w_down):
     count = inner.shape[0] // 2
     slots, hidden, features = w_down.shape
     ring = 3 * slots
     return pl.pallas_call(
-        functools.partial(contract_body, tensors, ring, block),
-        in_specs=[VMEM, VMEM, HBM],
+        functools.partial(contract_body, tensors, ring, block, len(ready)),
+        in_specs=[VMEM] * (1 + len(ready)) + [HBM],
         out_specs=[VMEM, VMEM],
         out_shape=[
             jax.ShapeDtypeStruct((count // 2, features), F32),
@@ -587,7 +587,7 @@
         compiler_params=pltpu.CompilerParams(vmem_limit_bytes=16 * 2**20),
         cost_estimate=cost(4 * count * w_down.size, 2 * w_down.size),
         name="contract",
-    )(inner, *in_vmem(first), *in_hbm(w_down))
+    )(inner, *in_vmem(*ready), *in_hbm(w_down))
 
 
 def halve_body(keep, arrived, low_here, low_there, high_here, high_there):
@@ -611,41 +611,23 @@
     )(keep, arrived)
 
 
-def total_body(low, arrived, out):
-    out[...] = (low[...] + arrived[...].astype(F32)).astype(BF16)
-
-
-def total_of(low, arrived):
-    return pl.pallas_call(
-        total_body,
+def deal_body(low, arrived, *outs):
+    width = outs[0].shape[1]
+    for i, out in enumerate(outs):
+        s = slice(i * width, (i + 1) * width)
+        out[...] = (low[:, s] + arrived[:, s].astype(F32)).astype(out.dtype)
+
+
+def deal(low, arrived, kinds):
+    rows, width = low.shape
+    return pl.pallas_call(
+        deal_body,
         in_specs=[VMEM] * 2,
-        out_specs=VMEM,
-        out_shape=jax.ShapeDtypeStruct(low.shape, BF16),
+        out_specs=[VMEM] * len(kinds),
+        out_shape=[jax.ShapeDtypeStruct((rows, width // len(kinds)), t) for t in kinds],
         compiler_params=pltpu.CompilerParams(vmem_limit_bytes=SCOPE),
-        name="total",
+        name="deal",
     )(low, arrived)
-
-
-def split_body(*refs):
-    parts, (keep, send) = refs[:-2], refs[-2:]
-    value = parts[0][...]
-    for part in parts[1:]:
-        value = value + part[...].astype(F32)
-    width = keep.shape[1]
-    keep[...] = value[:, :width]
-    send[...] = value[:, width:].astype(BF16)
-
-
-def split_columns(*parts):
-    rows, width = parts[0].shape
-    return pl.pallas_call(
-        split_body,
-        in_specs=[VMEM] * len(parts),
-        out_specs=[VMEM] * 2,
-        out_shape=[jax.ShapeDtypeStruct((rows, width // 2), t) for t in (F32, BF16)],
-        compiler_params=pltpu.CompilerParams(vmem_limit_bytes=SCOPE),
-        name="split",
-    )(*parts)
 
 
 def last_body(*refs):
@@ -690,6 +672,8 @@
     slots, _, hidden = w_gate.shape
     held = [1, 1, 1, 1, 1]
     weights = (w_gate, w_up, w_down)
+    part = features // tensors
+    block = 512 if part % 512 == 0 else LANES
     *blocks, w_here = attend(
         sides,
         extra,
@@ -703,7 +687,8 @@
         route_ids,
         w_out,
     )
-    ready = prefetch(0, held[0], weights, blocks[0])
+    *more, block_0 = prefetch(0, held[0], weights, blocks[0], block, 0)
+    ready = more
     blocks = [blocks[0]] + [swap(blocks[k], "side", sides, k) for k in range(1, sides)]
     mine, other = project(sides, blocks, w_here, ready[-1])
     ready += prefetch(len(ready), held[1], weights, other)
@@ -716,13 +701,11 @@
     stream = stream_of(sides, depth, mine, swap(other, "tensor", tensors, step), blocks, ready[-1])
     ready += prefetch(len(ready), held[3], weights, stream)
     own = join(stream, swap(stream, "tensor", tensors, 1), ready[-1])
-    part = features // tensors
-    block = 512 if part % 512 == 0 else LANES
-    *more, down = prefetch(len(ready), held[4], weights, own, block)
+    *more, block_1 = prefetch(len(ready), held[4], weights, own, block, 1)
     ready += more
     across = swap(own, "side", sides, 2)
     beside = swap(own, "side", sides, 1)
-    across, down = lax.optimization_barrier((across, down))
+    across, block_1 = lax.optimization_barrier((across, block_1))
     chunks = [own, beside, across, swap(across, "side", sides, 1)]
     inner, mine = expand(
         sides,
@@ -736,16 +719,17 @@
         ready,
         part,
     )
-    keep, send = contract(tensors, block, inner, down, w_down)
+    keep, send = contract(tensors, block, inner, [block_0, block_1], w_down)
     low_here, low_there, high_here, high_there = halve(keep, swap(send, "side", sides, 1))
-    there = total_of(low_there, swap(high_there, "side", sides, 2))
-    parts = [low_here, swap(high_here, "side", sides, 2), swap(there, "tensor", tensors, 1)]
-    mask = 2
-    while mask < tensors:
-        keep, send = split_columns(*parts)
-        parts = [keep, swap(send, "tensor", tensors, mask)]
-        mask *= 2
-    return last(mine, parts)
+    count = tensors // 2
+    arrived = swap(high_there, "side", sides, 2)
+    arrived, high_here = lax.optimization_barrier((arrived, high_here))
+    there = deal(low_there, arrived, [BF16] * count)
+    parts = [swap(v, "tensor", tensors, count + i) for i, v in enumerate(there)]
+    kinds = [F32] + [BF16] * (count - 1)
+    here = deal(low_here, swap(high_here, "side", sides, 2), kinds)
+    parts += [swap(v, "tensor", tensors, i) for i, v in enumerate(here) if i]
+    return last(mine, [here[0], *parts])
 
 
 def attend_local(query, new_key, new_value, key_cache, value_cache, cache_len):

time: 95 us -> 93.9 us (0.988)
  waiting for transfers between devices: 17.4 us -> 14.4 us
  starting transfers between devices: 15.8 us -> 17.1 us
    ppermute x14 -> x15, waiting for transfers between devices: 17.4 us -> 14.4 us  [swap(): return lax.ppermute(value, axis, [(i, i ^ mask) for i in range(count)])]
    ppermute x14 -> x15, starting transfers between devices: 15.8 us -> 17.1 us  [swap(): return lax.ppermute(value, axis, [(i, i ^ mask) for i in range(count)])]
    pallas_call x5, Pallas kernels: 16 us -> 17.2 us  [prefetch(): pl.pallas_call(functools.partial(prefetch_body, first, count, hidden // F...]
  transfers between devices with their start and end apart: 14 -> 15, of which waited for: 10 -> 8; matrix products, arithmetic and copies ran while one was open for 0% -> 0% of each run, Pallas kernels for 17% -> 18%
where the time goes in v4:
time: 93.9 us; the launch traced here: 93.8 us
  Pallas kernels  62 us (66%)
  starting transfers between devices  17.1 us (18%)
  waiting for transfers between devices  14.4 us (15%)
    pallas_call x1, Pallas kernels, expand(): pl.pallas_call(functools.partial(expand_body, sides, len(ready), split, r...  23.6 us
    pallas_call x5, Pallas kernels, prefetch(): pl.pallas_call(functools.partial(prefetch_body, first, count, hidden // F...  17.2 us
    ppermute x15, starting transfers between devices, swap(): return lax.ppermute(value, axis, [(i, i ^ mask) for i in range(count)])  17.1 us
    pallas_call x1, Pallas kernels, contract(): pl.pallas_call(functools.partial(contract_body, tensors, ring, block, len...  15.5 us
    ppermute x15, waiting for transfers between devices, swap(): return lax.ppermute(value, axis, [(i, i ^ mask) for i in range(count)])  14.4 us
    pallas_call x1, Pallas kernels, attend(): pl.pallas_call(functools.partial(attend_body, sides, block), in_specs=[HB...  3.88 us
  transfers between devices with their start and end apart: 15, of which 8 were waited for; matrix products, arithmetic and copies ran while one was open for 0% of the time, Pallas kernels for 18%

profile of v4, /device:TPU:0, one launch (start us, length us, event | category | flops | bytes accessed | tf_op | source)
XLA Modules:
  0.0 93.8 jit_solution(15222796506848404522)
XLA Ops:
  0.0 3.9 %attend.1 = (bf16[16,2432]{1,0:T(8,128)(2,1)S(1)}, bf16[16,2432]{1,0:T(8,128)(2,1)S(1)}, bf16[16,2432]{1,0:T(8,128)(2,1)S(1)}, bf16[16,2432]{1,0:T(8,128)(2,1)S(1)}, bf16[1536,1536]{1,0:T(8,128)(2,1)S(1)}) custom-call(s32[16]{0:T(128)} %length_at.1, bf16[16,1536]{1,0:T(8,128)(2,1)} %query_at.1, bf16[16,256]{1,0:T(8,128)(2,1)} %new_key_at.1, ...), custom_call_target="tpu_custom_call" | custom-call | flops 67108864 | bytes 4194304 | tf_op jit(solution)/shard_map/attend/pallas_call | solution.py:177
  3.9 0.5 collective-permute-start
  4.4 2.6 %collective-permute-start.1 = (bf16[16,2432]{1,0:T(8,128)(2,1)S(1)}, bf16[16,2432]{1,0:T(8,128)(2,1)S(1)}, u32[]{:S(2)}, u32[]{:S(2)}) collective-permute-start(bf16[16,2432]{1,0:T(8,128)(2,1)S(1)} %get-tuple-element.36), channel_id=1, source_target_pairs={{0,8},{4,12},{8,0},{12,4},{1,9},{5,13},{9,1},{13,5},{2,10},{6,14},... | collective-permute-start | bytes 233480 | tf_op jit(solution)/shard_map/ppermute | solution.py:33
  7.0 0.1 collective-permute-start.2
  7.0 4.2 %prefetch.5 = (bf16[2,6144,256]{2,1,0:T(8,128)(2,1)S(1)}, bf16[2,2048,512]{2,1,0:T(8,128)(2,1)S(1)}) custom-call(bf16[2,6144,2048]{2,1,0:T(8,128)(2,1)} %refs_10_.1, bf16[2,6144,2048]{2,1,0:T(8,128)(2,1)} %refs_11_.1, bf16[2,2048,6144]{2,1,0:T(8,128)(2,1)} %refs_2_.1, bf16[16,2432]{1,0:T(8,128)(2,1)S(1)} %get-tuple-element.34.after.refs_0_.refs_4_), custom_call_target="tpu_custom_call" | custom-call | bytes 10485760 | tf_op jit(solution)/shard_map/prefetch/pallas_call | solution.py:331
  11.2 0.0 copy-start
  11.2 0.0 collective-permute-done.refs_1_.refs_5_
  11.2 0.0 collective-permute-done.1.refs_2_.refs_6_
  11.2 0.0 collective-permute-done.2.refs_3_.refs_7_
  11.3 1.0 %project.1 = (f32[64,768]{1,0:T(8,128)S(1)}, bf16[64,768]{1,0:T(8,128)(2,1)S(1)}) custom-call(bf16[16,2432]{1,0:T(8,128)(2,1)S(1)} %get-tuple-element.34.after.refs_0_.refs_4_, bf16[16,2432]{1,0:T(8,128)(2,1)S(1)} %collective-permute-done.refs_1_.refs_5_, bf16[16,2432]{1,0:T(8,128)(2,1)S(1)} %collective-permute-done.1.refs_2_.refs_6_, ...), custom_call_target="tpu_custom_call" | custom-call | flops 301989888 | bytes 4718592 | tf_op jit(solution)/shard_map/project/pallas_call | solution.py:220
  12.3 2.0 %collective-permute-start.3 = (bf16[64,768]{1,0:T(8,128)(2,1)S(1)}, bf16[64,768]{1,0:T(8,128)(2,1)S(1)}, u32[]{:S(2)}, u32[]{:S(2)}) collective-permute-start(bf16[64,768]{1,0:T(8,128)(2,1)S(1)} %get-tuple-element.41.after), channel_id=1, source_target_pairs={{0,1},{1,0},{2,3},{3,2},{4,5},{5,4},{6,7},{7,6},{8,9},{9,8},{10,11... | collective-permute-start | bytes 294920 | tf_op jit(solution)/shard_map/ppermute | solution.py:33
  14.2 2.9 %prefetch.6.after.refs_13_ = bf16[2,6144,256]{2,1,0:T(8,128)(2,1)S(1)} custom-call(bf16[2,6144,2048]{2,1,0:T(8,128)(2,1)} %refs_10_.1, bf16[2,6144,2048]{2,1,0:T(8,128)(2,1)} %refs_11_.1, bf16[2,2048,6144]{2,1,0:T(8,128)(2,1)} %refs_2_.1, bf16[64,768]{1,0:T(8,128)(2,1)S(1)} %get-tuple-element.41.after), custom_call_target="tpu_custom_call" | custom-call | bytes 6291456 | tf_op jit(solution)/shard_map/prefetch/pallas_call | solution.py:331
  17.1 0.0 copy-done
  17.1 0.3 collective-permute-done.3.arrived
  17.5 2.7 %collective-permute-start.4 = (bf16[64,768]{1,0:T(8,128)(2,1)S(1)}, bf16[64,768]{1,0:T(8,128)(2,1)S(1)}, u32[]{:S(2)}, u32[]{:S(2)}) collective-permute-start(bf16[64,768]{1,0:T(8,128)(2,1)S(1)} %get-tuple-element.43.after), channel_id=1, source_target_pairs={{0,2},{1,3},{2,0},{3,1},{4,6},{5,7},{6,4},{7,5},{8,10},{9,11},{10,... | collective-permute-start | bytes 294920 | tf_op jit(solution)/shard_map/ppermute | solution.py:33
  20.2 2.9 %prefetch.7.refs_4_.refs_14_ = bf16[2,6144,256]{2,1,0:T(8,128)(2,1)S(1)} custom-call(bf16[2,6144,2048]{2,1,0:T(8,128)(2,1)} %refs_10_.1, bf16[2,6144,2048]{2,1,0:T(8,128)(2,1)} %refs_11_.1, bf16[2,2048,6144]{2,1,0:T(8,128)(2,1)} %refs_2_.1, bf16[64,768]{1,0:T(8,128)(2,1)S(1)} %get-tuple-element.43.after), custom_call_target="tpu_custom_call" | custom-call | bytes 6291456 | tf_op jit(solution)/shard_map/prefetch/pallas_call | solution.py:331
  23.1 1.8 %collective-permute-done.4.arrived = bf16[64,768]{1,0:T(8,128)(2,1)S(1)} collective-permute-done((bf16[64,768]{1,0:T(8,128)(2,1)S(1)}, bf16[64,768]{1,0:T(8,128)(2,1)S(1)}, u32[]{:S(2)}, u32[]{:S(2)}) %collective-permute-start.4) | collective-permute-done | bytes 98336 | tf_op jit(solution)/shard_map/ppermute | solution.py:33
  25.0 0.6 collective-permute-start.5
  25.6 2.9 %prefetch.8.after.refs_15_ = bf16[2,6144,256]{2,1,0:T(8,128)(2,1)S(1)} custom-call(bf16[2,6144,2048]{2,1,0:T(8,128)(2,1)} %refs_10_.1, bf16[2,6144,2048]{2,1,0:T(8,128)(2,1)} %refs_11_.1, bf16[2,2048,6144]{2,1,0:T(8,128)(2,1)} %refs_2_.1, bf16[64,768]{1,0:T(8,128)(2,1)S(1)} %stream.1.after.mine), custom_call_target="tpu_custom_call" | custom-call | bytes 6291456 | tf_op jit(solution)/shard_map/prefetch/pallas_call | solution.py:331
  28.5 1.2 %collective-permute-done.5.arrived = bf16[64,768]{1,0:T(8,128)(2,1)S(1)} collective-permute-done((bf16[64,768]{1,0:T(8,128)(2,1)S(1)}, bf16[64,768]{1,0:T(8,128)(2,1)S(1)}, u32[]{:S(2)}, u32[]{:S(2)}) %collective-permute-start.5) | collective-permute-done | bytes 98336 | tf_op jit(solution)/shard_map/ppermute | solution.py:33
  29.7 0.0 copy-start.2
  29.7 0.0 slice-start.1
  29.7 0.0 copy-start.1
  29.7 1.6 %collective-permute-start.7 = (bf16[64,1536]{1,0:T(8,128)(2,1)S(1)}, bf16[64,1536]{1,0:T(8,128)(2,1)S(1)}, u32[]{:S(2)}, u32[]{:S(2)}) collective-permute-start(bf16[64,1536]{1,0:T(8,128)(2,1)S(1)} %join.1.after.refs_0_), channel_id=1, source_target_pairs={{0,8},{4,12},{8,0},{12,4},{1,9},{5,13},{9,1},{13,5},{2,10},{6,14},... | collective-permute-start | bytes 589832 | tf_op jit(solution)/shard_map/ppermute | solution.py:33
  31.3 0.0 collective-permute-start.6
  31.3 4.4 %prefetch.9 = (bf16[2,6144,256]{2,1,0:T(8,128)(2,1)S(1)}, bf16[2,2048,512]{2,1,0:T(8,128)(2,1)S(1)}) custom-call(bf16[2,6144,2048]{2,1,0:T(8,128)(2,1)} %refs_10_.1, bf16[2,6144,2048]{2,1,0:T(8,128)(2,1)} %refs_11_.1, bf16[2,2048,6144]{2,1,0:T(8,128)(2,1)} %refs_2_.1, bf16[64,1536]{1,0:T(8,128)(2,1)S(1)} %join.1.after.refs_0_), custom_call_target="tpu_custom_call" | custom-call | bytes 10485760 | tf_op jit(solution)/shard_map/prefetch/pallas_call | solution.py:331
  35.7 0.0 collective-permute-done.7.refs_2_
  35.7 0.3 collective-permute-start.8
  36.0 0.0 copy-done.2
  36.0 0.0 collective-permute-done.6.refs_1_
  36.0 1.2 %collective-permute-done.8.refs_3_ = bf16[64,1536]{1,0:T(8,128)(2,1)S(1)} collective-permute-done((bf16[64,1536]{1,0:T(8,128)(2,1)S(1)}, bf16[64,1536]{1,0:T(8,128)(2,1)S(1)}, u32[]{:S(2)}, u32[]{:S(2)}) %collective-permute-start.8) | collective-permute-done | bytes 196640 | tf_op jit(solution)/shard_map/ppermute | solution.py:33
  37.3 0.0 slice-done
  37.3 23.6 %expand.1 = (bf16[128,4096]{1,0:T(8,128)(2,1)S(1)}, bf16[16,1536]{1,0:T(8,128)(2,1)S(1)}) custom-call(bf16[64,1536]{1,0:T(8,128)(2,1)S(1)} %join.1.after.refs_0_, bf16[64,1536]{1,0:T(8,128)(2,1)S(1)} %collective-permute-done.6.refs_1_, bf16[64,1536]{1,0:T(8,128)(2,1)S(1)} %collective-permute-done.7.refs_2_, ...), custom_call_target="tpu_custom_call" | custom-call | flops 12884901888 | bytes 100663296 | tf_op jit(solution)/shard_map/expand/pallas_call | solution.py:492
  60.9 15.5 %contract.1 = (f32[32,6144]{1,0:T(8,128)S(1)}, bf16[32,6144]{1,0:T(8,128)(2,1)S(1)}) custom-call(bf16[128,4096]{1,0:T(8,128)(2,1)S(1)} %get-tuple-element.48.inner, bf16[2,2048,512]{2,1,0:T(8,128)(2,1)S(1)} %get-tuple-element.49.refs_0_, bf16[2,2048,512]{2,1,0:T(8,128)(2,1)S(1)} %get-tuple-element.50.refs_1_, bf16[2,2048,6144]{2,1,0:T(8,128)(2,1)} %refs_2_.1), custom_call_target="tpu_custom_call" | custom-call | flops 6442450944 | bytes 50331648 | tf_op jit(solution)/shard_map/contract/pallas_call | solution.py:575
  76.4 0.3 collective-permute-start.9
  76.6 1.5 %collective-permute-done.9.arrived = bf16[32,6144]{1,0:T(8,128)(2,1)S(1)} collective-permute-done((bf16[32,6144]{1,0:T(8,128)(2,1)S(1)}, bf16[32,6144]{1,0:T(8,128)(2,1)S(1)}, u32[]{:S(2)}, u32[]{:S(2)}) %collective-permute-start.9) | collective-permute-done | bytes 393248 | tf_op jit(solution)/shard_map/ppermute | solution.py:33
  78.2 0.1 halve.1
  78.2 1.2 %collective-permute-start.10 = (bf16[16,3072]{1,0:T(8,128)(2,1)S(1)}, bf16[16,3072]{1,0:T(8,128)(2,1)S(1)}, u32[]{:S(2)}, u32[]{:S(2)}) collective-permute-start(bf16[16,3072]{1,0:T(8,128)(2,1)S(1)} %get-tuple-element.54), channel_id=1, source_target_pairs={{0,8},{4,12},{8,0},{12,4},{1,9},{5,13},{9,1},{13,5},{2,10},{6,14},... | collective-permute-start | bytes 294920 | tf_op jit(solution)/shard_map/ppermute | solution.py:33
  79.5 3.8 %collective-permute-done.10.arrived = bf16[16,3072]{1,0:T(8,128)(2,1)S(1)} collective-permute-done((bf16[16,3072]{1,0:T(8,128)(2,1)S(1)}, bf16[16,3072]{1,0:T(8,128)(2,1)S(1)}, u32[]{:S(2)}, u32[]{:S(2)}) %collective-permute-start.10) | collective-permute-done | bytes 98336 | tf_op jit(solution)/shard_map/ppermute | solution.py:33
  83.2 1.1 %collective-permute-start.11 = (bf16[16,3072]{1,0:T(8,128)(2,1)S(1)}, bf16[16,3072]{1,0:T(8,128)(2,1)S(1)}, u32[]{:S(2)}, u32[]{:S(2)}) collective-permute-start(bf16[16,3072]{1,0:T(8,128)(2,1)S(1)} %get-tuple-element.56), channel_id=1, source_target_pairs={{0,8},{4,12},{8,0},{12,4},{1,9},{5,13},{9,1},{13,5},{2,10},{6,14},... | collective-permute-start | bytes 294920 | tf_op jit(solution)/shard_map/ppermute | solution.py:33
  84.3 2.9 %collective-permute-start.12 = (bf16[16,1536]{1,0:T(8,128)(2,1)S(1)}, bf16[16,1536]{1,0:T(8,128)(2,1)S(1)}, u32[]{:S(2)}, u32[]{:S(2)}) collective-permute-start(bf16[16,1536]{1,0:T(8,128)(2,1)S(1)} %get-tuple-element.60), channel_id=1, source_target_pairs={{0,2},{1,3},{2,0},{3,1},{4,6},{5,7},{6,4},{7,5},{8,10},{9,11},{10,... | collective-permute-start | bytes 147464 | tf_op jit(solution)/shard_map/ppermute | solution.py:33
  87.2 0.7 collective-permute-start.13
  87.9 0.0 collective-permute-done.11.arrived
  87.9 0.6 collective-permute-start.14
  88.5 1.6 %collective-permute-done.12.refs_2_ = bf16[16,1536]{1,0:T(8,128)(2,1)S(1)} collective-permute-done((bf16[16,1536]{1,0:T(8,128)(2,1)S(1)}, bf16[16,1536]{1,0:T(8,128)(2,1)S(1)}, u32[]{:S(2)}, u32[]{:S(2)}) %collective-permute-start.12) | collective-permute-done | bytes 49184 | tf_op jit(solution)/shard_map/ppermute | solution.py:33
  90.1 3.0 %collective-permute-done.13.refs_3_ = bf16[16,1536]{1,0:T(8,128)(2,1)S(1)} collective-permute-done((bf16[16,1536]{1,0:T(8,128)(2,1)S(1)}, bf16[16,1536]{1,0:T(8,128)(2,1)S(1)}, u32[]{:S(2)}, u32[]{:S(2)}) %collective-permute-start.13) | collective-permute-done | bytes 49184 | tf_op jit(solution)/shard_map/ppermute | solution.py:33
  93.1 0.0 collective-permute-done.14.refs_4_
  93.1 0.7 last.1
  (10 shorter events, 0.1 us)
Async XLA Ops:
  3.9 7.3 %collective-permute-start = (bf16[16,2432]{1,0:T(8,128)(2,1)S(1)}, bf16[16,2432]{1,0:T(8,128)(2,1)S(1)}, u32[]{:S(2)}, u32[]{:S(2)}) collective-permute-start(bf16[16,2432]{1,0:T(8,128)(2,1)S(1)} %get-tuple-element.35), channel_id=1, source_target_pairs={{0,4},{4,0},{8,12},{12,8},{1,5},{5,1},{9,13},{13,9},{2,6},{6,2},{1... | collective-permute-start | bytes 233480 | tf_op jit(solution)/shard_map/ppermute | solution.py:33
  4.4 6.8 %collective-permute-start.1 = (bf16[16,2432]{1,0:T(8,128)(2,1)S(1)}, bf16[16,2432]{1,0:T(8,128)(2,1)S(1)}, u32[]{:S(2)}, u32[]{:S(2)}) collective-permute-start(bf16[16,2432]{1,0:T(8,128)(2,1)S(1)} %get-tuple-element.36), channel_id=1, source_target_pairs={{0,8},{4,12},{8,0},{12,4},{1,9},{5,13},{9,1},{13,5},{2,10},{6,14},... | collective-permute-start | bytes 233480 | tf_op jit(solution)/shard_map/ppermute | solution.py:33
  7.0 4.3 %collective-permute-start.2 = (bf16[16,2432]{1,0:T(8,128)(2,1)S(1)}, bf16[16,2432]{1,0:T(8,128)(2,1)S(1)}, u32[]{:S(2)}, u32[]{:S(2)}) collective-permute-start(bf16[16,2432]{1,0:T(8,128)(2,1)S(1)} %get-tuple-element.37), channel_id=1, source_target_pairs={{0,12},{4,8},{8,4},{12,0},{1,13},{5,9},{9,5},{13,1},{2,14},{6,10},... | collective-permute-start | bytes 233480 | tf_op jit(solution)/shard_map/ppermute | solution.py:33
  11.2 5.9 %copy-start = (bf16[2,6144,256]{2,1,0:T(8,128)(2,1)}, bf16[2,6144,256]{2,1,0:T(8,128)(2,1)S(1)}, u32[]{:S(2)}) copy-start(bf16[2,6144,256]{2,1,0:T(8,128)(2,1)S(1)} %get-tuple-element.39.refs_5_.refs_12_) | copy-start | bytes 18874372
  12.3 5.2 %collective-permute-start.3 = (bf16[64,768]{1,0:T(8,128)(2,1)S(1)}, bf16[64,768]{1,0:T(8,128)(2,1)S(1)}, u32[]{:S(2)}, u32[]{:S(2)}) collective-permute-start(bf16[64,768]{1,0:T(8,128)(2,1)S(1)} %get-tuple-element.41.after), channel_id=1, source_target_pairs={{0,1},{1,0},{2,3},{3,2},{4,5},{5,4},{6,7},{7,6},{8,9},{9,8},{10,11... | collective-permute-start | bytes 294920 | tf_op jit(solution)/shard_map/ppermute | solution.py:33
  17.5 7.4 %collective-permute-start.4 = (bf16[64,768]{1,0:T(8,128)(2,1)S(1)}, bf16[64,768]{1,0:T(8,128)(2,1)S(1)}, u32[]{:S(2)}, u32[]{:S(2)}) collective-permute-start(bf16[64,768]{1,0:T(8,128)(2,1)S(1)} %get-tuple-element.43.after), channel_id=1, source_target_pairs={{0,2},{1,3},{2,0},{3,1},{4,6},{5,7},{6,4},{7,5},{8,10},{9,11},{10,... | collective-permute-start | bytes 294920 | tf_op jit(solution)/shard_map/ppermute | solution.py:33
  25.0 4.7 %collective-permute-start.5 = (bf16[64,768]{1,0:T(8,128)(2,1)S(1)}, bf16[64,768]{1,0:T(8,128)(2,1)S(1)}, u32[]{:S(2)}, u32[]{:S(2)}) collective-permute-start(bf16[64,768]{1,0:T(8,128)(2,1)S(1)} %stream.1.after.mine), channel_id=1, source_target_pairs={{0,1},{1,0},{2,3},{3,2},{4,5},{5,4},{6,7},{7,6},{8,9},{9,8},{10,11... | collective-permute-start | bytes 294920 | tf_op jit(solution)/shard_map/ppermute | solution.py:33
  29.7 7.6 %slice-start = ((s8[6291456]{0:T(1024)(128)(4,1)}), s8[4194304]{0:T(1024)(128)(4,1)S(1)}, s32[]{:S(2)}) async-start(s8[6291456]{0:T(1024)(128)(4,1)} %bitcast.2), calls=%async_computation | async-start | bytes 8388608
  29.7 6.3 %copy-start.2 = (bf16[6144]{0:T(1024)(128)(2,1)S(1)}, bf16[6144]{0:T(1024)(128)(2,1)}, u32[]{:S(2)}) copy-start(bf16[6144]{0:T(1024)(128)(2,1)} %param.22) | copy-start | bytes 36868
  29.7 7.6 %slice-start.1 = ((s8[6291456]{0:T(1024)(128)(4,1)}), s8[2097152]{0:T(1024)(128)(4,1)S(1)}, s32[]{:S(2)}) async-start(s8[6291456]{0:T(1024)(128)(4,1)} %bitcast.2), calls=%async_computation.1 | async-start | bytes 4194304
  29.7 7.5 %copy-start.1 = (f32[6144,8]{0,1:T(8,128)S(1)}, f32[6144,8]{0,1:T(8,128)}, u32[]{:S(2)}) copy-start(f32[6144,8]{0,1:T(8,128)} %param.23) | copy-start | bytes 589828
  29.7 6.0 %collective-permute-start.7 = (bf16[64,1536]{1,0:T(8,128)(2,1)S(1)}, bf16[64,1536]{1,0:T(8,128)(2,1)S(1)}, u32[]{:S(2)}, u32[]{:S(2)}) collective-permute-start(bf16[64,1536]{1,0:T(8,128)(2,1)S(1)} %join.1.after.refs_0_), channel_id=1, source_target_pairs={{0,8},{4,12},{8,0},{12,4},{1,9},{5,13},{9,1},{13,5},{2,10},{6,14},... | collective-permute-start | bytes 589832 | tf_op jit(solution)/shard_map/ppermute | solution.py:33
  31.3 4.8 %collective-permute-start.6 = (bf16[64,1536]{1,0:T(8,128)(2,1)S(1)}, bf16[64,1536]{1,0:T(8,128)(2,1)S(1)}, u32[]{:S(2)}, u32[]{:S(2)}) collective-permute-start(bf16[64,1536]{1,0:T(8,128)(2,1)S(1)} %join.1.after.refs_0_), channel_id=1, source_target_pairs={{0,4},{4,0},{8,12},{12,8},{1,5},{5,1},{9,13},{13,9},{2,6},{6,2},{1... | collective-permute-start | bytes 589832 | tf_op jit(solution)/shard_map/ppermute | solution.py:33
  35.7 1.5 %collective-permute-start.8 = (bf16[64,1536]{1,0:T(8,128)(2,1)S(1)}, bf16[64,1536]{1,0:T(8,128)(2,1)S(1)}, u32[]{:S(2)}, u32[]{:S(2)}) collective-permute-start(bf16[64,1536]{1,0:T(8,128)(2,1)S(1)} %collective-permute-done.7.refs_2_), channel_id=1, source_target_pairs={{0,4},{4,0},{8,12},{12,8},{1,5},{5,1},{9,13},{13,9},{2,6},{6,2},{1... | collective-permute-start | bytes 589832 | tf_op jit(solution)/shard_map/ppermute | solution.py:33
  76.4 1.8 %collective-permute-start.9 = (bf16[32,6144]{1,0:T(8,128)(2,1)S(1)}, bf16[32,6144]{1,0:T(8,128)(2,1)S(1)}, u32[]{:S(2)}, u32[]{:S(2)}) collective-permute-start(bf16[32,6144]{1,0:T(8,128)(2,1)S(1)} %get-tuple-element.52), channel_id=1, source_target_pairs={{0,4},{4,0},{8,12},{12,8},{1,5},{5,1},{9,13},{13,9},{2,6},{6,2},{1... | collective-permute-start | bytes 1179656 | tf_op jit(solution)/shard_map/ppermute | solution.py:33
  78.2 5.0 %collective-permute-start.10 = (bf16[16,3072]{1,0:T(8,128)(2,1)S(1)}, bf16[16,3072]{1,0:T(8,128)(2,1)S(1)}, u32[]{:S(2)}, u32[]{:S(2)}) collective-permute-start(bf16[16,3072]{1,0:T(8,128)(2,1)S(1)} %get-tuple-element.54), channel_id=1, source_target_pairs={{0,8},{4,12},{8,0},{12,4},{1,9},{5,13},{9,1},{13,5},{2,10},{6,14},... | collective-permute-start | bytes 294920 | tf_op jit(solution)/shard_map/ppermute | solution.py:33
  83.2 4.7 %collective-permute-start.11 = (bf16[16,3072]{1,0:T(8,128)(2,1)S(1)}, bf16[16,3072]{1,0:T(8,128)(2,1)S(1)}, u32[]{:S(2)}, u32[]{:S(2)}) collective-permute-start(bf16[16,3072]{1,0:T(8,128)(2,1)S(1)} %get-tuple-element.56), channel_id=1, source_target_pairs={{0,8},{4,12},{8,0},{12,4},{1,9},{5,13},{9,1},{13,5},{2,10},{6,14},... | collective-permute-start | bytes 294920 | tf_op jit(solution)/shard_map/ppermute | solution.py:33
  84.3 5.8 %collective-permute-start.12 = (bf16[16,1536]{1,0:T(8,128)(2,1)S(1)}, bf16[16,1536]{1,0:T(8,128)(2,1)S(1)}, u32[]{:S(2)}, u32[]{:S(2)}) collective-permute-start(bf16[16,1536]{1,0:T(8,128)(2,1)S(1)} %get-tuple-element.60), channel_id=1, source_target_pairs={{0,2},{1,3},{2,0},{3,1},{4,6},{5,7},{6,4},{7,5},{8,10},{9,11},{10,... | collective-permute-start | bytes 147464 | tf_op jit(solution)/shard_map/ppermute | solution.py:33
  87.2 5.9 %collective-permute-start.13 = (bf16[16,1536]{1,0:T(8,128)(2,1)S(1)}, bf16[16,1536]{1,0:T(8,128)(2,1)S(1)}, u32[]{:S(2)}, u32[]{:S(2)}) collective-permute-start(bf16[16,1536]{1,0:T(8,128)(2,1)S(1)} %get-tuple-element.61), channel_id=1, source_target_pairs={{0,3},{1,2},{2,1},{3,0},{4,7},{5,6},{6,5},{7,4},{8,11},{9,10},{10,... | collective-permute-start | bytes 147464 | tf_op jit(solution)/shard_map/ppermute | solution.py:33
  87.9 5.2 %collective-permute-start.14 = (bf16[16,1536]{1,0:T(8,128)(2,1)S(1)}, bf16[16,1536]{1,0:T(8,128)(2,1)S(1)}, u32[]{:S(2)}, u32[]{:S(2)}) collective-permute-start(bf16[16,1536]{1,0:T(8,128)(2,1)S(1)} %get-tuple-element.62), channel_id=1, source_target_pairs={{0,1},{1,0},{2,3},{3,2},{4,5},{5,4},{6,7},{7,6},{8,9},{9,8},{10,11... | collective-permute-start | bytes 147464 | tf_op jit(solution)/shard_map/ppermute | solution.py:33

commit v5 on v4

--- a/solution.py
+++ b/solution.py
@@ -304,7 +304,9 @@
         for i in range(w_down.shape[0]):
             copies.append(
                 pltpu.make_async_copy(
-                    w_down.at[i, :, columns(start, block)], outs[count].at[i], sems.at[count, i]
+                    w_down.at[i, :, columns(start, block)],
+                    outs[count].at[pl.ds(i * w_down.shape[1], w_down.shape[1])],
+                    sems.at[count, i],
                 )
             )
     for i, out in enumerate(outs[:count]):
@@ -326,7 +328,7 @@
 def prefetch(first, count, weights, after, block=0, number=0):
     w_gate, _, w_down = weights
     slots, depth, hidden = w_gate.shape
-    shapes = [(2, depth, FBLOCK)] * count + [(*w_down.shape[:2], block)] * bool(block)
+    shapes = [(2, depth, FBLOCK)] * count + [(slots * hidden, block)] * bool(block)
     return list(
         pl.pallas_call(
             functools.partial(prefetch_body, first, count, hidden // FBLOCK, block, number),
@@ -528,7 +530,7 @@
         return [
             pltpu.make_async_copy(
                 w_down.at[slot, :, columns(start, block)],
-                buffer.at[step % deep, slot],
+                buffer.at[step % deep, pl.ds(slot * hidden, hidden)],
                 sems.at[step % deep, slot],
             )
             for slot in range(slots)
@@ -539,17 +541,9 @@
             c.start()
 
     def run(step, more, weights, arriving=()):
-        total = None
         for c in arriving:
             c.wait()
-        for slot in range(slots):
-            value = jnp.dot(
-                inner[:, slot * hidden : (slot + 1) * hidden],
-                weights[slot],
-                preferred_element_type=F32,
-            )
-            total = value if total is None else total + value
-        total = fold(total)
+        total = fold(jnp.dot(inner[...], weights[...], preferred_element_type=F32))
         where = columns(step * block, block)
         keep[:, where] = total[:half]
         send[:, where] = total[half:].astype(BF16)
@@ -581,7 +575,7 @@
             jax.ShapeDtypeStruct((count // 2, features), BF16),
         ],
         scratch_shapes=[
-            pltpu.VMEM((ring // slots, slots, hidden, block), BF16),
+            pltpu.VMEM((ring // slots, slots * hidden, block), BF16),
             pltpu.SemaphoreType.DMA((ring // slots, slots)),
         ],
         compiler_params=pltpu.CompilerParams(vmem_limit_bytes=16 * 2**20),

time: 93.9 us -> 93.9 us (level)
  no operation moved by 1% of the time
where the time goes in v5:
time: 93.9 us; the launch traced here: 93.8 us
  Pallas kernels  62 us (66%)
  starting transfers between devices  17.1 us (18%)
  waiting for transfers between devices  14.4 us (15%)
    pallas_call x1, Pallas kernels, expand(): pl.pallas_call(functools.partial(expand_body, sides, len(ready), split, r...  23.6 us
    pallas_call x5, Pallas kernels, prefetch(): pl.pallas_call(functools.partial(prefetch_body, first, count, hidden // F...  17.2 us
    ppermute x15, starting transfers between devices, swap(): return lax.ppermute(value, axis, [(i, i ^ mask) for i in range(count)])  17.1 us
    pallas_call x1, Pallas kernels, contract(): pl.pallas_call(functools.partial(contract_body, tensors, ring, block, len...  15.5 us
    ppermute x15, waiting for transfers between devices, swap(): return lax.ppermute(value, axis, [(i, i ^ mask) for i in range(count)])  14.4 us
    pallas_call x1, Pallas kernels, attend(): pl.pallas_call(functools.partial(attend_body, sides, block), in_specs=[HB...  3.88 us
  transfers between devices with their start and end apart: 15, of which 8 were waited for; matrix products, arithmetic and copies ran while one was open for 0% of the time, Pallas kernels for 18%

profile of v5, /device:TPU:0, one launch (start us, length us, event | category | flops | bytes accessed | tf_op | source)
XLA Modules:
  0.0 93.8 jit_solution(9650830223397377759)
XLA Ops:
  0.0 3.9 %attend.1 = (bf16[16,2432]{1,0:T(8,128)(2,1)S(1)}, bf16[16,2432]{1,0:T(8,128)(2,1)S(1)}, bf16[16,2432]{1,0:T(8,128)(2,1)S(1)}, bf16[16,2432]{1,0:T(8,128)(2,1)S(1)}, bf16[1536,1536]{1,0:T(8,128)(2,1)S(1)}) custom-call(s32[16]{0:T(128)} %length_at.1, bf16[16,1536]{1,0:T(8,128)(2,1)} %query_at.1, bf16[16,256]{1,0:T(8,128)(2,1)} %new_key_at.1, ...), custom_call_target="tpu_custom_call" | custom-call | flops 67108864 | bytes 4194304 | tf_op jit(solution)/shard_map/attend/pallas_call | solution.py:177
  3.9 0.5 collective-permute-start
  4.4 2.6 %collective-permute-start.1 = (bf16[16,2432]{1,0:T(8,128)(2,1)S(1)}, bf16[16,2432]{1,0:T(8,128)(2,1)S(1)}, u32[]{:S(2)}, u32[]{:S(2)}) collective-permute-start(bf16[16,2432]{1,0:T(8,128)(2,1)S(1)} %get-tuple-element.36), channel_id=1, source_target_pairs={{0,8},{4,12},{8,0},{12,4},{1,9},{5,13},{9,1},{13,5},{2,10},{6,14},... | collective-permute-start | bytes 233480 | tf_op jit(solution)/shard_map/ppermute | solution.py:33
  7.0 0.1 collective-permute-start.2
  7.0 4.2 %prefetch.5 = (bf16[2,6144,256]{2,1,0:T(8,128)(2,1)S(1)}, bf16[4096,512]{1,0:T(8,128)(2,1)S(1)}) custom-call(bf16[2,6144,2048]{2,1,0:T(8,128)(2,1)} %refs_10_.1, bf16[2,6144,2048]{2,1,0:T(8,128)(2,1)} %refs_11_.1, bf16[2,2048,6144]{2,1,0:T(8,128)(2,1)} %refs_2_.1, bf16[16,2432]{1,0:T(8,128)(2,1)S(1)} %get-tuple-element.34.after.refs_0_.refs_4_), custom_call_target="tpu_custom_call" | custom-call | bytes 10485760 | tf_op jit(solution)/shard_map/prefetch/pallas_call | solution.py:333
  11.2 0.0 copy-start
  11.2 0.0 collective-permute-done.refs_1_.refs_5_
  11.2 0.0 collective-permute-done.1.refs_2_.refs_6_
  11.2 0.0 collective-permute-done.2.refs_3_.refs_7_
  11.3 1.0 %project.1 = (f32[64,768]{1,0:T(8,128)S(1)}, bf16[64,768]{1,0:T(8,128)(2,1)S(1)}) custom-call(bf16[16,2432]{1,0:T(8,128)(2,1)S(1)} %get-tuple-element.34.after.refs_0_.refs_4_, bf16[16,2432]{1,0:T(8,128)(2,1)S(1)} %collective-permute-done.refs_1_.refs_5_, bf16[16,2432]{1,0:T(8,128)(2,1)S(1)} %collective-permute-done.1.refs_2_.refs_6_, ...), custom_call_target="tpu_custom_call" | custom-call | flops 301989888 | bytes 4718592 | tf_op jit(solution)/shard_map/project/pallas_call | solution.py:220
  12.3 2.0 %collective-permute-start.3 = (bf16[64,768]{1,0:T(8,128)(2,1)S(1)}, bf16[64,768]{1,0:T(8,128)(2,1)S(1)}, u32[]{:S(2)}, u32[]{:S(2)}) collective-permute-start(bf16[64,768]{1,0:T(8,128)(2,1)S(1)} %get-tuple-element.41.after), channel_id=1, source_target_pairs={{0,1},{1,0},{2,3},{3,2},{4,5},{5,4},{6,7},{7,6},{8,9},{9,8},{10,11... | collective-permute-start | bytes 294920 | tf_op jit(solution)/shard_map/ppermute | solution.py:33
  14.2 2.9 %prefetch.6.after.refs_13_ = bf16[2,6144,256]{2,1,0:T(8,128)(2,1)S(1)} custom-call(bf16[2,6144,2048]{2,1,0:T(8,128)(2,1)} %refs_10_.1, bf16[2,6144,2048]{2,1,0:T(8,128)(2,1)} %refs_11_.1, bf16[2,2048,6144]{2,1,0:T(8,128)(2,1)} %refs_2_.1, bf16[64,768]{1,0:T(8,128)(2,1)S(1)} %get-tuple-element.41.after), custom_call_target="tpu_custom_call" | custom-call | bytes 6291456 | tf_op jit(solution)/shard_map/prefetch/pallas_call | solution.py:333
  17.1 0.0 copy-done
  17.1 0.3 collective-permute-done.3.arrived
  17.5 2.7 %collective-permute-start.4 = (bf16[64,768]{1,0:T(8,128)(2,1)S(1)}, bf16[64,768]{1,0:T(8,128)(2,1)S(1)}, u32[]{:S(2)}, u32[]{:S(2)}) collective-permute-start(bf16[64,768]{1,0:T(8,128)(2,1)S(1)} %get-tuple-element.43.after), channel_id=1, source_target_pairs={{0,2},{1,3},{2,0},{3,1},{4,6},{5,7},{6,4},{7,5},{8,10},{9,11},{10,... | collective-permute-start | bytes 294920 | tf_op jit(solution)/shard_map/ppermute | solution.py:33
  20.2 2.9 %prefetch.7.refs_4_.refs_14_ = bf16[2,6144,256]{2,1,0:T(8,128)(2,1)S(1)} custom-call(bf16[2,6144,2048]{2,1,0:T(8,128)(2,1)} %refs_10_.1, bf16[2,6144,2048]{2,1,0:T(8,128)(2,1)} %refs_11_.1, bf16[2,2048,6144]{2,1,0:T(8,128)(2,1)} %refs_2_.1, bf16[64,768]{1,0:T(8,128)(2,1)S(1)} %get-tuple-element.43.after), custom_call_target="tpu_custom_call" | custom-call | bytes 6291456 | tf_op jit(solution)/shard_map/prefetch/pallas_call | solution.py:333
  23.1 1.8 %collective-permute-done.4.arrived = bf16[64,768]{1,0:T(8,128)(2,1)S(1)} collective-permute-done((bf16[64,768]{1,0:T(8,128)(2,1)S(1)}, bf16[64,768]{1,0:T(8,128)(2,1)S(1)}, u32[]{:S(2)}, u32[]{:S(2)}) %collective-permute-start.4) | collective-permute-done | bytes 98336 | tf_op jit(solution)/shard_map/ppermute | solution.py:33
  25.0 0.6 collective-permute-start.5
  25.6 2.9 %prefetch.8.after.refs_15_ = bf16[2,6144,256]{2,1,0:T(8,128)(2,1)S(1)} custom-call(bf16[2,6144,2048]{2,1,0:T(8,128)(2,1)} %refs_10_.1, bf16[2,6144,2048]{2,1,0:T(8,128)(2,1)} %refs_11_.1, bf16[2,2048,6144]{2,1,0:T(8,128)(2,1)} %refs_2_.1, bf16[64,768]{1,0:T(8,128)(2,1)S(1)} %stream.1.after.mine), custom_call_target="tpu_custom_call" | custom-call | bytes 6291456 | tf_op jit(solution)/shard_map/prefetch/pallas_call | solution.py:333
  28.5 1.2 %collective-permute-done.5.arrived = bf16[64,768]{1,0:T(8,128)(2,1)S(1)} collective-permute-done((bf16[64,768]{1,0:T(8,128)(2,1)S(1)}, bf16[64,768]{1,0:T(8,128)(2,1)S(1)}, u32[]{:S(2)}, u32[]{:S(2)}) %collective-permute-start.5) | collective-permute-done | bytes 98336 | tf_op jit(solution)/shard_map/ppermute | solution.py:33
  29.7 0.0 copy-start.2
  29.7 0.0 slice-start.1
  29.7 0.0 copy-start.1
  29.7 1.6 %collective-permute-start.7 = (bf16[64,1536]{1,0:T(8,128)(2,1)S(1)}, bf16[64,1536]{1,0:T(8,128)(2,1)S(1)}, u32[]{:S(2)}, u32[]{:S(2)}) collective-permute-start(bf16[64,1536]{1,0:T(8,128)(2,1)S(1)} %join.1.after.refs_0_), channel_id=1, source_target_pairs={{0,8},{4,12},{8,0},{12,4},{1,9},{5,13},{9,1},{13,5},{2,10},{6,14},... | collective-permute-start | bytes 589832 | tf_op jit(solution)/shard_map/ppermute | solution.py:33
  31.3 0.0 collective-permute-start.6
  31.3 4.4 %prefetch.9 = (bf16[2,6144,256]{2,1,0:T(8,128)(2,1)S(1)}, bf16[4096,512]{1,0:T(8,128)(2,1)S(1)}) custom-call(bf16[2,6144,2048]{2,1,0:T(8,128)(2,1)} %refs_10_.1, bf16[2,6144,2048]{2,1,0:T(8,128)(2,1)} %refs_11_.1, bf16[2,2048,6144]{2,1,0:T(8,128)(2,1)} %refs_2_.1, bf16[64,1536]{1,0:T(8,128)(2,1)S(1)} %join.1.after.refs_0_), custom_call_target="tpu_custom_call" | custom-call | bytes 10485760 | tf_op jit(solution)/shard_map/prefetch/pallas_call | solution.py:333
  35.7 0.0 collective-permute-done.7.refs_2_
  35.7 0.3 collective-permute-start.8
  36.0 0.0 copy-done.2
  36.0 0.0 collective-permute-done.6.refs_1_
  36.0 1.2 %collective-permute-done.8.refs_3_ = bf16[64,1536]{1,0:T(8,128)(2,1)S(1)} collective-permute-done((bf16[64,1536]{1,0:T(8,128)(2,1)S(1)}, bf16[64,1536]{1,0:T(8,128)(2,1)S(1)}, u32[]{:S(2)}, u32[]{:S(2)}) %collective-permute-start.8) | collective-permute-done | bytes 196640 | tf_op jit(solution)/shard_map/ppermute | solution.py:33
  37.3 0.0 slice-done
  37.3 23.6 %expand.1 = (bf16[128,4096]{1,0:T(8,128)(2,1)S(1)}, bf16[16,1536]{1,0:T(8,128)(2,1)S(1)}) custom-call(bf16[64,1536]{1,0:T(8,128)(2,1)S(1)} %join.1.after.refs_0_, bf16[64,1536]{1,0:T(8,128)(2,1)S(1)} %collective-permute-done.6.refs_1_, bf16[64,1536]{1,0:T(8,128)(2,1)S(1)} %collective-permute-done.7.refs_2_, ...), custom_call_target="tpu_custom_call" | custom-call | flops 12884901888 | bytes 100663296 | tf_op jit(solution)/shard_map/expand/pallas_call | solution.py:494
  60.9 15.5 %contract.1 = (f32[32,6144]{1,0:T(8,128)S(1)}, bf16[32,6144]{1,0:T(8,128)(2,1)S(1)}) custom-call(bf16[128,4096]{1,0:T(8,128)(2,1)S(1)} %get-tuple-element.48.inner, bf16[4096,512]{1,0:T(8,128)(2,1)S(1)} %get-tuple-element.49.refs_0_, bf16[4096,512]{1,0:T(8,128)(2,1)S(1)} %get-tuple-element.50.refs_1_, bf16[2,2048,6144]{2,1,0:T(8,128)(2,1)} %refs_2_.1), custom_call_target="tpu_custom_call" | custom-call | flops 6442450944 | bytes 50331648 | tf_op jit(solution)/shard_map/contract/pallas_call | solution.py:569
  76.4 0.3 collective-permute-start.9
  76.6 1.5 %collective-permute-done.9.arrived = bf16[32,6144]{1,0:T(8,128)(2,1)S(1)} collective-permute-done((bf16[32,6144]{1,0:T(8,128)(2,1)S(1)}, bf16[32,6144]{1,0:T(8,128)(2,1)S(1)}, u32[]{:S(2)}, u32[]{:S(2)}) %collective-permute-start.9) | collective-permute-done | bytes 393248 | tf_op jit(solution)/shard_map/ppermute | solution.py:33
  78.2 0.1 halve.1
  78.2 1.2 %collective-permute-start.10 = (bf16[16,3072]{1,0:T(8,128)(2,1)S(1)}, bf16[16,3072]{1,0:T(8,128)(2,1)S(1)}, u32[]{:S(2)}, u32[]{:S(2)}) collective-permute-start(bf16[16,3072]{1,0:T(8,128)(2,1)S(1)} %get-tuple-element.54), channel_id=1, source_target_pairs={{0,8},{4,12},{8,0},{12,4},{1,9},{5,13},{9,1},{13,5},{2,10},{6,14},... | collective-permute-start | bytes 294920 | tf_op jit(solution)/shard_map/ppermute | solution.py:33
  79.5 3.8 %collective-permute-done.10.arrived = bf16[16,3072]{1,0:T(8,128)(2,1)S(1)} collective-permute-done((bf16[16,3072]{1,0:T(8,128)(2,1)S(1)}, bf16[16,3072]{1,0:T(8,128)(2,1)S(1)}, u32[]{:S(2)}, u32[]{:S(2)}) %collective-permute-start.10) | collective-permute-done | bytes 98336 | tf_op jit(solution)/shard_map/ppermute | solution.py:33
  83.2 1.1 %collective-permute-start.11 = (bf16[16,3072]{1,0:T(8,128)(2,1)S(1)}, bf16[16,3072]{1,0:T(8,128)(2,1)S(1)}, u32[]{:S(2)}, u32[]{:S(2)}) collective-permute-start(bf16[16,3072]{1,0:T(8,128)(2,1)S(1)} %get-tuple-element.56), channel_id=1, source_target_pairs={{0,8},{4,12},{8,0},{12,4},{1,9},{5,13},{9,1},{13,5},{2,10},{6,14},... | collective-permute-start | bytes 294920 | tf_op jit(solution)/shard_map/ppermute | solution.py:33
  84.3 2.9 %collective-permute-start.12 = (bf16[16,1536]{1,0:T(8,128)(2,1)S(1)}, bf16[16,1536]{1,0:T(8,128)(2,1)S(1)}, u32[]{:S(2)}, u32[]{:S(2)}) collective-permute-start(bf16[16,1536]{1,0:T(8,128)(2,1)S(1)} %get-tuple-element.60), channel_id=1, source_target_pairs={{0,2},{1,3},{2,0},{3,1},{4,6},{5,7},{6,4},{7,5},{8,10},{9,11},{10,... | collective-permute-start | bytes 147464 | tf_op jit(solution)/shard_map/ppermute | solution.py:33
  87.2 0.7 collective-permute-start.13
  87.9 0.0 collective-permute-done.11.arrived
  87.9 0.6 collective-permute-start.14
  88.5 1.6 %collective-permute-done.12.refs_2_ = bf16[16,1536]{1,0:T(8,128)(2,1)S(1)} collective-permute-done((bf16[16,1536]{1,0:T(8,128)(2,1)S(1)}, bf16[16,1536]{1,0:T(8,128)(2,1)S(1)}, u32[]{:S(2)}, u32[]{:S(2)}) %collective-permute-start.12) | collective-permute-done | bytes 49184 | tf_op jit(solution)/shard_map/ppermute | solution.py:33
  90.1 3.0 %collective-permute-done.13.refs_3_ = bf16[16,1536]{1,0:T(8,128)(2,1)S(1)} collective-permute-done((bf16[16,1536]{1,0:T(8,128)(2,1)S(1)}, bf16[16,1536]{1,0:T(8,128)(2,1)S(1)}, u32[]{:S(2)}, u32[]{:S(2)}) %collective-permute-start.13) | collective-permute-done | bytes 49184 | tf_op jit(solution)/shard_map/ppermute | solution.py:33
  93.1 0.0 collective-permute-done.14.refs_4_
  93.1 0.7 last.1
  (10 shorter events, 0.1 us)
Async XLA Ops:
  3.9 7.3 %collective-permute-start = (bf16[16,2432]{1,0:T(8,128)(2,1)S(1)}, bf16[16,2432]{1,0:T(8,128)(2,1)S(1)}, u32[]{:S(2)}, u32[]{:S(2)}) collective-permute-start(bf16[16,2432]{1,0:T(8,128)(2,1)S(1)} %get-tuple-element.35), channel_id=1, source_target_pairs={{0,4},{4,0},{8,12},{12,8},{1,5},{5,1},{9,13},{13,9},{2,6},{6,2},{1... | collective-permute-start | bytes 233480 | tf_op jit(solution)/shard_map/ppermute | solution.py:33
  4.4 6.8 %collective-permute-start.1 = (bf16[16,2432]{1,0:T(8,128)(2,1)S(1)}, bf16[16,2432]{1,0:T(8,128)(2,1)S(1)}, u32[]{:S(2)}, u32[]{:S(2)}) collective-permute-start(bf16[16,2432]{1,0:T(8,128)(2,1)S(1)} %get-tuple-element.36), channel_id=1, source_target_pairs={{0,8},{4,12},{8,0},{12,4},{1,9},{5,13},{9,1},{13,5},{2,10},{6,14},... | collective-permute-start | bytes 233480 | tf_op jit(solution)/shard_map/ppermute | solution.py:33
  7.0 4.3 %collective-permute-start.2 = (bf16[16,2432]{1,0:T(8,128)(2,1)S(1)}, bf16[16,2432]{1,0:T(8,128)(2,1)S(1)}, u32[]{:S(2)}, u32[]{:S(2)}) collective-permute-start(bf16[16,2432]{1,0:T(8,128)(2,1)S(1)} %get-tuple-element.37), channel_id=1, source_target_pairs={{0,12},{4,8},{8,4},{12,0},{1,13},{5,9},{9,5},{13,1},{2,14},{6,10},... | collective-permute-start | bytes 233480 | tf_op jit(solution)/shard_map/ppermute | solution.py:33
  11.2 5.9 %copy-start = (bf16[2,6144,256]{2,1,0:T(8,128)(2,1)}, bf16[2,6144,256]{2,1,0:T(8,128)(2,1)S(1)}, u32[]{:S(2)}) copy-start(bf16[2,6144,256]{2,1,0:T(8,128)(2,1)S(1)} %get-tuple-element.39.refs_5_.refs_12_) | copy-start | bytes 18874372
  12.3 5.2 %collective-permute-start.3 = (bf16[64,768]{1,0:T(8,128)(2,1)S(1)}, bf16[64,768]{1,0:T(8,128)(2,1)S(1)}, u32[]{:S(2)}, u32[]{:S(2)}) collective-permute-start(bf16[64,768]{1,0:T(8,128)(2,1)S(1)} %get-tuple-element.41.after), channel_id=1, source_target_pairs={{0,1},{1,0},{2,3},{3,2},{4,5},{5,4},{6,7},{7,6},{8,9},{9,8},{10,11... | collective-permute-start | bytes 294920 | tf_op jit(solution)/shard_map/ppermute | solution.py:33
  17.5 7.4 %collective-permute-start.4 = (bf16[64,768]{1,0:T(8,128)(2,1)S(1)}, bf16[64,768]{1,0:T(8,128)(2,1)S(1)}, u32[]{:S(2)}, u32[]{:S(2)}) collective-permute-start(bf16[64,768]{1,0:T(8,128)(2,1)S(1)} %get-tuple-element.43.after), channel_id=1, source_target_pairs={{0,2},{1,3},{2,0},{3,1},{4,6},{5,7},{6,4},{7,5},{8,10},{9,11},{10,... | collective-permute-start | bytes 294920 | tf_op jit(solution)/shard_map/ppermute | solution.py:33
  25.0 4.7 %collective-permute-start.5 = (bf16[64,768]{1,0:T(8,128)(2,1)S(1)}, bf16[64,768]{1,0:T(8,128)(2,1)S(1)}, u32[]{:S(2)}, u32[]{:S(2)}) collective-permute-start(bf16[64,768]{1,0:T(8,128)(2,1)S(1)} %stream.1.after.mine), channel_id=1, source_target_pairs={{0,1},{1,0},{2,3},{3,2},{4,5},{5,4},{6,7},{7,6},{8,9},{9,8},{10,11... | collective-permute-start | bytes 294920 | tf_op jit(solution)/shard_map/ppermute | solution.py:33
  29.7 7.6 %slice-start = ((s8[6291456]{0:T(1024)(128)(4,1)}), s8[4194304]{0:T(1024)(128)(4,1)S(1)}, s32[]{:S(2)}) async-start(s8[6291456]{0:T(1024)(128)(4,1)} %bitcast.2), calls=%async_computation | async-start | bytes 8388608
  29.7 6.3 %copy-start.2 = (bf16[6144]{0:T(1024)(128)(2,1)S(1)}, bf16[6144]{0:T(1024)(128)(2,1)}, u32[]{:S(2)}) copy-start(bf16[6144]{0:T(1024)(128)(2,1)} %param.22) | copy-start | bytes 36868
  29.7 7.6 %slice-start.1 = ((s8[6291456]{0:T(1024)(128)(4,1)}), s8[2097152]{0:T(1024)(128)(4,1)S(1)}, s32[]{:S(2)}) async-start(s8[6291456]{0:T(1024)(128)(4,1)} %bitcast.2), calls=%async_computation.1 | async-start | bytes 4194304
  29.7 7.5 %copy-start.1 = (f32[6144,8]{0,1:T(8,128)S(1)}, f32[6144,8]{0,1:T(8,128)}, u32[]{:S(2)}) copy-start(f32[6144,8]{0,1:T(8,128)} %param.23) | copy-start | bytes 589828
  29.7 6.0 %collective-permute-start.7 = (bf16[64,1536]{1,0:T(8,128)(2,1)S(1)}, bf16[64,1536]{1,0:T(8,128)(2,1)S(1)}, u32[]{:S(2)}, u32[]{:S(2)}) collective-permute-start(bf16[64,1536]{1,0:T(8,128)(2,1)S(1)} %join.1.after.refs_0_), channel_id=1, source_target_pairs={{0,8},{4,12},{8,0},{12,4},{1,9},{5,13},{9,1},{13,5},{2,10},{6,14},... | collective-permute-start | bytes 589832 | tf_op jit(solution)/shard_map/ppermute | solution.py:33
  31.3 4.8 %collective-permute-start.6 = (bf16[64,1536]{1,0:T(8,128)(2,1)S(1)}, bf16[64,1536]{1,0:T(8,128)(2,1)S(1)}, u32[]{:S(2)}, u32[]{:S(2)}) collective-permute-start(bf16[64,1536]{1,0:T(8,128)(2,1)S(1)} %join.1.after.refs_0_), channel_id=1, source_target_pairs={{0,4},{4,0},{8,12},{12,8},{1,5},{5,1},{9,13},{13,9},{2,6},{6,2},{1... | collective-permute-start | bytes 589832 | tf_op jit(solution)/shard_map/ppermute | solution.py:33
  35.7 1.5 %collective-permute-start.8 = (bf16[64,1536]{1,0:T(8,128)(2,1)S(1)}, bf16[64,1536]{1,0:T(8,128)(2,1)S(1)}, u32[]{:S(2)}, u32[]{:S(2)}) collective-permute-start(bf16[64,1536]{1,0:T(8,128)(2,1)S(1)} %collective-permute-done.7.refs_2_), channel_id=1, source_target_pairs={{0,4},{4,0},{8,12},{12,8},{1,5},{5,1},{9,13},{13,9},{2,6},{6,2},{1... | collective-permute-start | bytes 589832 | tf_op jit(solution)/shard_map/ppermute | solution.py:33
  76.4 1.8 %collective-permute-start.9 = (bf16[32,6144]{1,0:T(8,128)(2,1)S(1)}, bf16[32,6144]{1,0:T(8,128)(2,1)S(1)}, u32[]{:S(2)}, u32[]{:S(2)}) collective-permute-start(bf16[32,6144]{1,0:T(8,128)(2,1)S(1)} %get-tuple-element.52), channel_id=1, source_target_pairs={{0,4},{4,0},{8,12},{12,8},{1,5},{5,1},{9,13},{13,9},{2,6},{6,2},{1... | collective-permute-start | bytes 1179656 | tf_op jit(solution)/shard_map/ppermute | solution.py:33
  78.2 5.0 %collective-permute-start.10 = (bf16[16,3072]{1,0:T(8,128)(2,1)S(1)}, bf16[16,3072]{1,0:T(8,128)(2,1)S(1)}, u32[]{:S(2)}, u32[]{:S(2)}) collective-permute-start(bf16[16,3072]{1,0:T(8,128)(2,1)S(1)} %get-tuple-element.54), channel_id=1, source_target_pairs={{0,8},{4,12},{8,0},{12,4},{1,9},{5,13},{9,1},{13,5},{2,10},{6,14},... | collective-permute-start | bytes 294920 | tf_op jit(solution)/shard_map/ppermute | solution.py:33
  83.2 4.7 %collective-permute-start.11 = (bf16[16,3072]{1,0:T(8,128)(2,1)S(1)}, bf16[16,3072]{1,0:T(8,128)(2,1)S(1)}, u32[]{:S(2)}, u32[]{:S(2)}) collective-permute-start(bf16[16,3072]{1,0:T(8,128)(2,1)S(1)} %get-tuple-element.56), channel_id=1, source_target_pairs={{0,8},{4,12},{8,0},{12,4},{1,9},{5,13},{9,1},{13,5},{2,10},{6,14},... | collective-permute-start | bytes 294920 | tf_op jit(solution)/shard_map/ppermute | solution.py:33
  84.3 5.8 %collective-permute-start.12 = (bf16[16,1536]{1,0:T(8,128)(2,1)S(1)}, bf16[16,1536]{1,0:T(8,128)(2,1)S(1)}, u32[]{:S(2)}, u32[]{:S(2)}) collective-permute-start(bf16[16,1536]{1,0:T(8,128)(2,1)S(1)} %get-tuple-element.60), channel_id=1, source_target_pairs={{0,2},{1,3},{2,0},{3,1},{4,6},{5,7},{6,4},{7,5},{8,10},{9,11},{10,... | collective-permute-start | bytes 147464 | tf_op jit(solution)/shard_map/ppermute | solution.py:33
  87.2 5.9 %collective-permute-start.13 = (bf16[16,1536]{1,0:T(8,128)(2,1)S(1)}, bf16[16,1536]{1,0:T(8,128)(2,1)S(1)}, u32[]{:S(2)}, u32[]{:S(2)}) collective-permute-start(bf16[16,1536]{1,0:T(8,128)(2,1)S(1)} %get-tuple-element.61), channel_id=1, source_target_pairs={{0,3},{1,2},{2,1},{3,0},{4,7},{5,6},{6,5},{7,4},{8,11},{9,10},{10,... | collective-permute-start | bytes 147464 | tf_op jit(solution)/shard_map/ppermute | solution.py:33
  87.9 5.2 %collective-permute-start.14 = (bf16[16,1536]{1,0:T(8,128)(2,1)S(1)}, bf16[16,1536]{1,0:T(8,128)(2,1)S(1)}, u32[]{:S(2)}, u32[]{:S(2)}) collective-permute-start(bf16[16,1536]{1,0:T(8,128)(2,1)S(1)} %get-tuple-element.62), channel_id=1, source_target_pairs={{0,1},{1,0},{2,3},{3,2},{4,5},{5,4},{6,7},{7,6},{8,9},{9,8},{10,11... | collective-permute-start | bytes 147464 | tf_op jit(solution)/shard_map/ppermute | solution.py:33
